TPU v7x, 32 devices: a whole 2x2x4 slice. The times are simulated.
32 devices in a mesh: groups: 2 (over y), dp: 4 (over z), tensor: 2 (over x), seq: 2 (over core).
Axes of the slice: x: 2, y: 2, z: 4, core: 2. Of those that a mesh axis runs over, the one named last changes fastest.
Arguments:
- saved_layer_input: bfloat16 [2048, 5120], P(('groups', 'dp', 'seq'), 'tensor'), parts along dimension 0, may hold values from -6 to 6
- output_gradient: bfloat16 [2048, 2560], P(('groups', 'dp', 'seq'), 'tensor'), parts along dimension 0, may hold values from -6 to 6
- adapter_of_row: int32 [2048], P(('groups', 'dp')), parts along dimension 0, may hold values from 0 to 3, as said below
- adapter_owner_slot: int32 [8], P('groups'), parts along dimension 0, may hold values from 0 to 7, as said below
- frozen_query_weight: bfloat16 [5120, 2560], P(('dp', 'seq'), 'tensor'), may hold values from -0.078125 to 0.078125
- adapter_down_factors: bfloat16 [10240, 4, 16], P(('groups', 'tensor')), parts along dimension 0, may hold values from -0.078125 to 0.078125
- adapter_up_factors: bfloat16 [8, 16, 2560], P('groups', None, 'tensor'), parts along dimension 0, may hold values from -0.125 to 0.125
Outputs:
- input_gradient: bfloat16 [2048, 5120], P(('groups', 'dp', 'seq'), 'tensor'), parts along dimension 0
- down_grad: float32 [10240, 8, 16], P(('groups', 'tensor', 'seq'), 'dp'), parts along dimension 0
- up_grad: float32 [16, 16, 2560], P(('groups', 'dp'), None, ('tensor', 'seq')), parts along dimension 0
There are 2 independent parts, one for each index of `groups`. A program takes and returns all parts, laid end to end along the dimension named above; an argument that names none is the same for every part. Nothing has to cross between parts.
Inputs may be any that keep to these rules, and one draw needn't show every extreme that they name: `adapter_of_row`: within each aligned block of 128 rows the ids do not fall; every adapter is named by at least one row. `adapter_owner_slot`: distinct slots; the owner of slot s is index s // 2 of dp; some owner has all 2 of its slots taken.
All inputs are finite; a program needn't handle non-finite values.
Results may differ from a plain program's by a relative error of at most 0.017.
Values may be sent and summed in bfloat16 or wider, within the bound.
No kernel may reach another device: no remote copies, remote signals or barrier semaphores. Data moves between devices by JAX's collectives and lax.ppermute only.
A program may use at most 64 MiB of HBM per device.

v0:
```python
import jax
import jax.numpy as jnp
from jax import lax
from jax.sharding import PartitionSpec as P

OWN_MAX = 2


adapter_scale = 2.0


def contract_final_axis(left_side, right_side):
    return lax.dot_general(
        left_side, right_side, (((1,), (1,)), ((), ())), preferred_element_type=jnp.float32
    )


def contract_rows(left_side, right_side):
    return lax.dot_general(
        left_side, right_side, (((0,), (0,)), ((), ())), preferred_element_type=jnp.float32
    )


def local(
    saved_layer_input,
    output_gradient,
    adapter_of_row,
    adapter_owner_slot,
    frozen_query_weight,
    adapter_down_factors,
    adapter_up_factors,
):
    own_rows = saved_layer_input.shape[0]
    chip_rows = adapter_of_row.shape[0]
    adapter_total = adapter_owner_slot.shape[0]
    rank_length = adapter_up_factors.shape[1]
    owners = lax.axis_size("dp")
    core_count = lax.axis_size("seq")
    worker_index = lax.axis_index("seq")
    slot_total = owners * OWN_MAX
    labels = jnp.arange(adapter_total, dtype=jnp.int32)
    matches = (adapter_of_row[:, None] == labels[None, :]).astype(jnp.int32)
    local_hist = jnp.sum(matches, axis=0)
    every_hist = lax.all_gather(local_hist, "dp", axis=0, tiled=True)
    counts = jnp.sum(every_hist.reshape(owners, adapter_total), axis=0).astype(jnp.float32)
    total_rows = own_rows * core_count * owners
    per_adapter = jnp.float32(total_rows) / (jnp.float32(adapter_total) * counts)
    match_float = matches.astype(jnp.float32)
    device_weight = jnp.sum(match_float * per_adapter[None, :], axis=1)
    row_start = worker_index * own_rows
    owned_weight = lax.dynamic_slice_in_dim(device_weight, row_start, own_rows, 0)
    own_match = lax.dynamic_slice_in_dim(matches, row_start, own_rows, 0)
    partial_value = contract_final_axis(
        output_gradient, lax.all_gather(frozen_query_weight, ("dp", "seq"), axis=0, tiled=True)
    )
    frozen_sum = lax.psum_scatter(
        partial_value.astype(jnp.bfloat16), "tensor", scatter_dimension=1, tiled=True
    ).astype(jnp.float32)
    input_half, grad_half = (
        lax.all_to_all(saved_layer_input, "seq", split_axis=1, concat_axis=0, tiled=True),
        lax.all_to_all(output_gradient, "seq", split_axis=1, concat_axis=0, tiled=True),
    )
    input_width = input_half.shape[1]
    output_width = grad_half.shape[1]
    down_factor_half = lax.dynamic_slice_in_dim(
        adapter_down_factors, worker_index * input_width, input_width, 0
    ).reshape(input_width, adapter_total * rank_length)
    up_factor_half = lax.dynamic_slice_in_dim(
        adapter_up_factors, worker_index * output_width, output_width, 2
    ).reshape(adapter_total * rank_length, output_width)
    into_everyone = jnp.dot(
        input_half, down_factor_half, preferred_element_type=jnp.float32
    ).reshape(chip_rows, adapter_total, rank_length)
    output_everyone = contract_final_axis(grad_half, up_factor_half).reshape(
        chip_rows, adapter_total, rank_length
    )
    in_part = jnp.sum(into_everyone * match_float[:, :, None], axis=1)
    out_part = jnp.sum(output_everyone * match_float[:, :, None], axis=1)
    in_sum, output_sum_total = (
        lax.psum(in_part.astype(jnp.bfloat16), ("tensor", "seq")).astype(jnp.float32),
        lax.psum(out_part.astype(jnp.bfloat16), ("tensor", "seq")).astype(jnp.float32),
    )
    reduced_input = in_sum.astype(jnp.bfloat16)
    reduced_output = (adapter_scale * device_weight[:, None] * output_sum_total).astype(
        jnp.bfloat16
    )
    raised_rows = (
        adapter_scale * device_weight[:, None] * reduced_input.astype(jnp.float32)
    ).astype(jnp.bfloat16)
    own_low = lax.dynamic_slice_in_dim(reduced_output, row_start, own_rows, 0)
    distribute_rows = (own_match.astype(jnp.bfloat16)[:, :, None] * own_low[:, None, :]).reshape(
        own_rows, adapter_total * rank_length
    )
    adapter_term = contract_final_axis(
        distribute_rows,
        adapter_down_factors.reshape(adapter_down_factors.shape[0], adapter_total * rank_length),
    )
    input_gradient = (owned_weight[:, None] * frozen_sum + adapter_term).astype(jnp.bfloat16)
    slot_of_row = jnp.sum(matches * adapter_owner_slot[None, :], axis=1)
    slot_match = (slot_of_row[:, None] == jnp.arange(slot_total, dtype=jnp.int32)[None, :]).astype(
        jnp.bfloat16
    )
    spread_out = (slot_match[:, :, None] * reduced_output[:, None, :]).reshape(
        chip_rows, slot_total * rank_length
    )
    spread_in = (slot_match[:, :, None] * raised_rows[:, None, :]).reshape(
        chip_rows, slot_total * rank_length
    )
    down_part = contract_rows(input_half, spread_out).reshape(input_width, slot_total, rank_length)
    up_part = contract_rows(spread_in, grad_half).reshape(slot_total, rank_length, output_width)
    down_grad, up_grad = (
        lax.psum_scatter(
            down_part.astype(jnp.bfloat16), "dp", scatter_dimension=1, tiled=True
        ).astype(jnp.float32),
        lax.psum_scatter(
            up_part.astype(jnp.bfloat16), "dp", scatter_dimension=0, tiled=True
        ).astype(jnp.float32),
    )
    return (input_gradient, down_grad, up_grad)


def solution(mesh):
    in_specs = (
        P(("groups", "dp", "seq"), "tensor"),
        P(("groups", "dp", "seq"), "tensor"),
        P(("groups", "dp")),
        P("groups"),
        P(("dp", "seq"), "tensor"),
        P(("groups", "tensor"), None, None),
        P("groups", None, "tensor"),
    )
    out_specs = (
        P(("groups", "dp", "seq"), "tensor"),
        P(("groups", "tensor", "seq"), "dp", None),
        P(("groups", "dp"), None, ("tensor", "seq")),
    )
    return jax.shard_map(local, mesh=mesh, in_specs=in_specs, out_specs=out_specs, check_vma=False)
```

profile of v0, /device:TPU:0, one launch (start us, length us, event | category | flops | bytes accessed | tf_op | source)
XLA Modules:
  0.0 191.1 jit_solution(11992169826238449842)
XLA Ops:
  8.0 0.0 copy-start
  8.0 0.0 copy-start.2
  8.0 0.0 all-gather.2.cloned.1.call-start
  8.1 0.7 all-gather.2.cloned.1.call-update
  8.8 0.4 copy-done.2
  9.1 0.0 copy-start.6
  9.2 0.0 copy-start.4
  9.2 0.0 copy-start.5
  9.2 0.0 copy-start.1
  9.2 1.1 copy.13
  10.2 3.5 %all-to-all-start.1 = ((bf16[128,2,1280]{0,2,1:T(8,128)(2,1)}), bf16[128,2,1280]{0,2,1:T(8,128)(2,1)S(1)}, u32[]{:S(2)}, u32[]{:S(2)}) async-start(bf16[128,2,1280]{0,2,1:T(8,128)(2,1)} %bitcast.8), calls=%async_computation.2 | async-start | bytes 1310720 | tf_op jit(solution)/shard_map/all_to_all | solution.py:60
  13.8 0.0 copy-done.6
  13.8 0.6 dynamic-slice
  15.0 0.0 copy-done.4
  15.0 0.0 copy-done.5
  15.0 0.1 select_reduce_fusion
  15.2 0.2 dynamic-update-slice
  15.4 10.0 %all-reduce = s32[16]{0:T(128)S(1)} all-reduce(s32[16]{0:T(128)S(1)} %dynamic-update-slice), channel_id=1, replica_groups=mesh['groups'=2,'dp'=4,'tensor'=2,'seq'=2] {'dp'}, use_global_device_ids=true, to_apply=%add | all-reduce | flops 16 | bytes 128
  25.4 0.1 reshape.109
  25.5 0.0 copy-done.1
  25.5 0.0 copy-start.3
  25.5 0.8 copy.17
  26.3 0.0 all-to-all-done.1
  26.3 3.5 %all-to-all-start = ((bf16[128,2,640]{2,0,1:T(8,128)(2,1)}), bf16[128,2,640]{2,0,1:T(8,128)(2,1)S(1)}, u32[]{:S(2)}, u32[]{:S(2)}) async-start(bf16[128,2,640]{2,0,1:T(8,128)(2,1)} %bitcast.47), calls=%async_computation.1 | async-start | bytes 655360 | tf_op jit(solution)/shard_map/all_to_all | solution.py:61
  29.8 0.0 reduce-scatter.8.cloned.1.call-start
  29.8 0.3 copy.14
  30.1 0.0 copy-done.3
  30.1 0.0 copy-done
  30.2 1.2 all-to-all-done
  31.4 0.2 fusion.13
  31.6 0.3 fusion.14
  31.9 0.1 multiply_reduce_fusion
  32.0 12.0 %all-reduce.1 = (bf16[256,16]{0,1:T(8,128)(2,1)S(1)}, bf16[256,16]{0,1:T(8,128)(2,1)S(1)}) all-reduce(bf16[256,16]{0,1:T(8,128)(2,1)S(1)} %get-tuple-element.4, bf16[256,16]{0,1:T(8,128)(2,1)S(1)} %get-tuple-element.3), channel_id=1, replica_groups=mesh['groups'=2,'dp'=4,'tensor'=2,'seq'=2] {'tensor','seq'}, use_global_device_ids=true, to_apply=%region_5.0 | all-reduce | flops 8192 | bytes 32768 | tf_op jit(solution)/shard_map/psum | solution.py:81
  44.0 0.1 multiply_reduce_fusion.2
  44.1 0.9 convolution_convert_fusion.2
  45.0 0.0 reduce-scatter.8.cloned.1.call-update
  45.0 0.0 reduce-scatter.6.cloned.1.call-start
  45.1 1.0 convolution_convert_fusion.1
  46.1 0.0 reduce-scatter.6.cloned.1.call-update
  46.1 0.0 reduce-scatter.4.cloned.1.call-start
  46.2 90.0 %all-gather.2.cloned.1.call-done = bf16[5120,1280]{1,0:T(8,128)(2,1)} async-done(((bf16[640,1280]{1,0:T(8,128)(2,1)}), bf16[5120,1280]{1,0:T(8,128)(2,1)}) %all-gather.2.cloned.1.call-update) | async-done | bytes 13107216 | tf_op jit(solution)/shard_map/all_gather | solution.py:54
  136.2 10.1 %convolution_convert_fusion = bf16[128,5120]{1,0:T(8,128)(2,1)} fusion(bf16[128,1280]{1,0:T(8,128)(2,1)S(1)} %copy-done.1, bf16[5120,1280]{1,0:T(8,128)(2,1)} %all-gather.2.cloned.1.call-done), kind=kOutput, calls=%fused_computation | convolution fusion | flops 1678376960 | bytes 14745600 | tf_op jit(solution)/shard_map/dot_general | solution.py:13
  146.3 0.0 reduce-scatter.4.cloned.1.call-update
  146.4 0.1 dynamic_slice.15
  146.4 0.0 reduce-scatter.8.cloned.1.call-done
  146.4 1.4 convert_element_type.97
  147.9 9.6 %reduce-scatter.6.cloned.1.call-done = bf16[1280,2,16]{0,2,1:T(8,128)(2,1)} async-done(((bf16[1280,8,16]{0,2,1:T(8,128)(2,1)}), bf16[1280,2,16]{0,2,1:T(8,128)(2,1)}) %reduce-scatter.6.cloned.1.call-update) | async-done | bytes 81936 | tf_op jit(solution)/shard_map/reduce_scatter | solution.py:112
  157.5 1.6 convert_element_type.92
  159.1 22.1 %reduce-scatter.4.cloned.1.call-done = bf16[128,2560]{1,0:T(8,128)(2,1)} async-done(((bf16[128,5120]{1,0:T(8,128)(2,1)}), bf16[128,2560]{1,0:T(8,128)(2,1)}) %reduce-scatter.4.cloned.1.call-update) | async-done | bytes 655376 | tf_op jit(solution)/shard_map/reduce_scatter | solution.py:56
  181.2 2.3 %fusion.1 = bf16[128,2560]{1,0:T(8,128)(2,1)} fusion(bf16[2560,4,16]{0,2,1:T(8,128)(2,1)S(1)} %copy-done, bf16[128,2560]{1,0:T(8,128)(2,1)} %reduce-scatter.4.cloned.1.call-done, f32[128]{0:T(128)S(1)} %dynamic_slice.15, bf16[128,16]{0,1:T(8,128)(2,1)S(1)} %constant_dynamic-slice_fusion.1, bf16[128,4]{0,1:T(4,128)(2,1)S(1)} %dynamic-slice_convert_fusion), kind=kOutput, calls=%fused_computation.3 | convolution fusion | flops 43261952 | bytes 1644032 | tf_op jit(solution)/shard_map/dot_general | solution.py:13
  (12 shorter events, 0.1 us)
Async XLA Ops:
  8.0 22.1 %copy-start = (bf16[2560,4,16]{0,2,1:T(8,128)(2,1)S(1)}, bf16[2560,4,16]{0,2,1:T(8,128)(2,1)}, u32[]{:S(2)}) copy-start(bf16[2560,4,16]{0,2,1:T(8,128)(2,1)} %param.12) | copy-start | bytes 983044
  8.0 1.1 copy-start.2
  8.0 128.2 %all-gather.2.cloned.1.call-start = ((), (), s32[]{:S(2)}) async-start(), calls=%async_computation.5 | async-start | bytes 14745600 | tf_op jit(solution)/shard_map/all_gather | solution.py:54
  9.1 4.6 %copy-start.6 = (u32[32]{0:T(128)S(1)}, u32[32]{0:T(128)}, u32[]{:S(2)}) copy-start(u32[32]{0:T(128)} %constant.27) | copy-start | bytes 388
  9.2 5.9 %copy-start.4 = (s32[256]{0:T(256)S(1)}, s32[256]{0:T(256)}, u32[]{:S(2)}) copy-start(s32[256]{0:T(256)} %param.9) | copy-start | bytes 3076
  9.2 5.9 %copy-start.5 = (s32[4]{0:T(128)S(1)}, s32[4]{0:T(128)}, u32[]{:S(2)}) copy-start(s32[4]{0:T(128)} %param.10) | copy-start | bytes 52
  9.2 16.4 %copy-start.1 = (bf16[128,1280]{1,0:T(8,128)(2,1)S(1)}, bf16[128,1280]{1,0:T(8,128)(2,1)}, u32[]{:S(2)}) copy-start(bf16[128,1280]{1,0:T(8,128)(2,1)} %param.8) | copy-start | bytes 983044
  10.2 16.1 %all-to-all-start.1 = ((bf16[128,2,1280]{0,2,1:T(8,128)(2,1)}), bf16[128,2,1280]{0,2,1:T(8,128)(2,1)S(1)}, u32[]{:S(2)}, u32[]{:S(2)}) async-start(bf16[128,2,1280]{0,2,1:T(8,128)(2,1)} %bitcast.8), calls=%async_computation.2 | async-start | bytes 1310720 | tf_op jit(solution)/shard_map/all_to_all | solution.py:60
  25.5 4.6 %copy-start.3 = (bf16[4,16,1280]{2,1,0:T(8,128)(2,1)S(1)}, bf16[4,16,1280]{2,1,0:T(8,128)(2,1)}, u32[]{:S(2)}) copy-start(bf16[4,16,1280]{2,1,0:T(8,128)(2,1)} %param.13) | copy-start | bytes 491524
  26.3 5.0 %all-to-all-start = ((bf16[128,2,640]{2,0,1:T(8,128)(2,1)}), bf16[128,2,640]{2,0,1:T(8,128)(2,1)S(1)}, u32[]{:S(2)}, u32[]{:S(2)}) async-start(bf16[128,2,640]{2,0,1:T(8,128)(2,1)} %bitcast.47), calls=%async_computation.1 | async-start | bytes 655360 | tf_op jit(solution)/shard_map/all_to_all | solution.py:61
  29.8 116.7 %reduce-scatter.8.cloned.1.call-start = ((), (), s32[]{:S(2)}) async-start(), calls=%async_computation.8 | async-start | bytes 204800 | tf_op jit(solution)/shard_map/reduce_scatter | solution.py:115
  45.0 112.5 %reduce-scatter.6.cloned.1.call-start = ((), (), s32[]{:S(2)}) async-start(), calls=%async_computation.7 | async-start | bytes 409600 | tf_op jit(solution)/shard_map/reduce_scatter | solution.py:112
  46.1 135.1 %reduce-scatter.4.cloned.1.call-start = ((), (), s32[]{:S(2)}) async-start(), calls=%async_computation.6 | async-start | bytes 1966080 | tf_op jit(solution)/shard_map/reduce_scatter | solution.py:56
Sparse Core Ops, SparseCore 0:
  10.6 125.5 all-gather.1
Sparse Core Ops, SparseCore 1:
  45.1 91.1 reduce-scatter.7
  139.1 18.4 reduce-scatter.5
  159.7 21.4 reduce-scatter.3
where the time goes:
time: 192 us; the launch traced here: 191 us
  waiting for transfers between devices  124 us (65%)
  blocking collectives  22 us (11%)
  between operations  16.5 us (9%)
  matrix products  14.8 us (8%)
  starting transfers between devices  7.14 us (4%)
  local copies, waits for them, and re-layouts  3.56 us (2%)
  other arithmetic  3.34 us (2%)
    all_gather x1, waiting for transfers between devices, local(): lax.all_gather(frozen_query_weight, ('dp', 'seq'), axis=0, tiled=True)  90 us
    reduce_scatter x1, waiting for transfers between devices, local(): lax.psum_scatter(partial_value.astype(jnp.bfloat16), 'tensor', scatter_di...  22.1 us
    dot_general x3, matrix products, contract_final_axis(): lax.dot_general(left_side, right_side, (((1,), (1,)), ((), ())), preferre...  12.6 us
    psum x1, blocking collectives, local(): lax.psum(out_part.astype(jnp.bfloat16), ('tensor', 'seq'))  12 us
    unnamed x1, blocking collectives  9.99 us
    reduce_scatter x1, waiting for transfers between devices, local(): lax.psum_scatter(down_part.astype(jnp.bfloat16), 'dp', scatter_dimension=...  9.64 us
  transfers between devices with their start and end apart: 6, of which 4 were waited for; matrix products, arithmetic and copies ran while one was open for 10% of the time, Pallas kernels for 0%

commit v1 on v0

v1 whole, which is shorter than its diff:
```python
import jax
import jax.numpy as jnp
from jax import lax
from jax.sharding import PartitionSpec as P

OWN_MAX = 2
ADAPTER_SCALE = 2.0
F32 = jnp.float32
BF16 = jnp.bfloat16


def dot_last(left, right):
    return lax.dot_general(left, right, (((1,), (1,)), ((), ())), preferred_element_type=F32)


def dot_plain(left, right):
    return lax.dot_general(left, right, (((1,), (0,)), ((), ())), preferred_element_type=F32)


def shift(value, axis, step):
    size = lax.axis_size(axis)
    return lax.ppermute(value, axis, [(i, (i + step) % size) for i in range(size)])


def pick(value, index):
    return lax.dynamic_index_in_dim(value, index, 0, keepdims=False)


def local(x, g, ids, owner_slot, w, down, up):
    rows = x.shape[0]
    adapters = owner_slot.shape[0]
    rank = up.shape[1]
    n, tensors, cores = lax.axis_size("dp"), lax.axis_size("tensor"), lax.axis_size("seq")
    z, t, c = lax.axis_index("dp"), lax.axis_index("tensor"), lax.axis_index("seq")
    slots = n * OWN_MAX
    labels = jnp.arange(adapters, dtype=jnp.int32)

    blocks = [g] + [shift(g, "dp", s) for s in range(1, n)]
    w_other = lax.ppermute(w, "seq", [(0, 1), (1, 0)])
    w_chip = jnp.concatenate(
        [jnp.where(c == 0, w, w_other), jnp.where(c == 0, w_other, w)], axis=0
    )
    width = w_chip.shape[0]

    down_t = down.transpose(1, 2, 0).reshape(adapters * rank, -1)
    up_t = up.reshape(adapters * rank, -1)
    own_ids = lax.dynamic_slice_in_dim(ids, c * rows, rows, 0)
    own_match = (own_ids[None, :] == labels[:, None]).astype(F32)
    low_in = dot_last(down_t, x).reshape(adapters, rank, rows)
    low_out = dot_last(up_t, g).reshape(adapters, rank, rows)
    low = jnp.concatenate(
        [
            jnp.sum(low_in * own_match[:, None, :], axis=0),
            jnp.sum(low_out * own_match[:, None, :], axis=0),
        ],
        axis=0,
    )
    low_sum = low
    for s in range(1, tensors):
        low_sum = low_sum + shift(low, "tensor", s)
    low_bf = low_sum.astype(BF16)
    low_in, low_out = low_bf[:rank], low_bf[rank:]

    id_rows = ids.reshape(cores, rows).astype(BF16)
    card = jnp.concatenate(
        [low_in, id_rows, jnp.zeros((16 - cores, rows), BF16)], axis=0
    )
    cards = jnp.stack([card] + [shift(card, "dp", s) for s in range(1, n)])
    all_ids = cards[:, rank : rank + cores].astype(jnp.int32)
    counts = jnp.sum(
        (all_ids.reshape(1, -1) == labels[:, None]).astype(F32), axis=1
    )
    weight = F32(n * cores * rows) / (F32(adapters) * counts)

    own_slot = jnp.sum((own_match * owner_slot.astype(F32)[:, None]), axis=0).astype(jnp.int32)
    slot_labels = jnp.arange(slots, dtype=jnp.int32)
    spread = (
        (own_slot[None, :] == slot_labels[:, None]).astype(BF16)[:, None, :] * low_out[None]
    ).reshape(slots * rank, rows)
    down_part = dot_plain(spread, x).astype(BF16)
    half = down_part.shape[1] // cores
    away = lax.dynamic_slice_in_dim(down_part, (1 - c) * half, half, 1)
    mine = lax.dynamic_slice_in_dim(down_part, c * half, half, 1)
    got = lax.ppermute(away, "seq", [(0, 1), (1, 0)])
    chip_part = (mine.astype(F32) + got.astype(F32)).astype(BF16)
    chip_part = chip_part.reshape(n, OWN_MAX * rank, half)
    down_sum = pick(chip_part, z).astype(F32)
    for s in range(1, n):
        down_sum = down_sum + shift(pick(chip_part, (z + s) % n), "dp", s).astype(F32)
    my_slots = z * OWN_MAX + jnp.arange(OWN_MAX, dtype=jnp.int32)
    slot_weight = ADAPTER_SCALE * jnp.sum(
        jnp.where(owner_slot[None, :] == my_slots[:, None], weight[None, :], 0.0), axis=1
    )
    down_grad = down_sum.reshape(OWN_MAX, rank, half) * slot_weight[:, None, None]
    down_grad = down_grad.transpose(2, 0, 1)

    chunk = width // tensors
    back = []
    for s in range(n):
        part = dot_last(blocks[s], w_chip).astype(BF16)
        part = part.reshape(rows, tensors, chunk).transpose(1, 0, 2)
        total = pick(part, t).astype(F32)
        for k in range(1, tensors):
            total = total + shift(pick(part, (t + k) % tensors), "tensor", k).astype(F32)
        total = total.astype(BF16)
        back.append(shift(total, "dp", -s) if s else total)
    span = n // tensors
    groups = []
    for r in range(span):
        stack = jnp.stack([back[r + k * span] for k in range(tensors)])
        first = ((z + r) % n) // span
        order = lambda p: (p - first) % tensors
        pieces = [pick(stack, order(t))]
        for k in range(1, tensors):
            pieces.append(shift(pick(stack, order((t + k) % tensors)), "tensor", k))
        pieces = jnp.stack(pieces)
        groups.append(jnp.stack([pick(pieces, (t - p) % tensors) for p in range(tensors)]))
    groups = jnp.stack(groups)
    base = jnp.stack([pick(groups, (q - z) % span) for q in range(span)])
    base = base.transpose(2, 0, 1, 3).reshape(rows, span * width)

    own_weight = jnp.sum(own_match * weight[:, None], axis=0)
    scattered = (own_match.astype(BF16)[:, None, :] * low_out[None]).reshape(adapters * rank, rows)
    adapter_term = lax.dot_general(
        scattered, down_t, (((0,), (0,)), ((), ())), preferred_element_type=F32
    )
    input_gradient = (
        own_weight[:, None] * (base.astype(F32) + ADAPTER_SCALE * adapter_term)
    ).astype(BF16)

    slot_of = jnp.sum(
        jnp.where(
            lax.dynamic_index_in_dim(all_ids, c, 1, keepdims=False)[:, None, :] == labels[None, :, None],
            owner_slot[None, :, None],
            0,
        ),
        axis=1,
    )
    up_part = jnp.zeros((OWN_MAX * rank, g.shape[1]), F32)
    for s in range(n):
        lift = (
            (slot_of[s][None, :] == my_slots[:, None]).astype(BF16)[:, None, :]
            * cards[s, :rank][None]
        ).reshape(OWN_MAX * rank, rows)
        up_part = up_part + dot_plain(lift, blocks[s])
    up_half = up_part.shape[1] // cores
    up_mine = lax.dynamic_slice_in_dim(up_part, c * up_half, up_half, 1)
    up_away = lax.dynamic_slice_in_dim(up_part, (1 - c) * up_half, up_half, 1)
    up_sum = up_mine + lax.ppermute(up_away, "seq", [(0, 1), (1, 0)])
    up_grad = up_sum.reshape(OWN_MAX, rank, up_half) * slot_weight[:, None, None]
    return input_gradient, down_grad, up_grad


def solution(mesh):
    in_specs = (
        P(("groups", "dp", "seq"), "tensor"),
        P(("groups", "dp", "seq"), "tensor"),
        P(("groups", "dp")),
        P("groups"),
        P(("dp", "seq"), "tensor"),
        P(("groups", "tensor"), None, None),
        P("groups", None, "tensor"),
    )
    out_specs = (
        P(("groups", "dp", "seq"), "tensor"),
        P(("groups", "tensor", "seq"), "dp", None),
        P(("groups", "dp"), None, ("tensor", "seq")),
    )
    return jax.shard_map(local, mesh=mesh, in_specs=in_specs, out_specs=out_specs, check_vma=False)
```

time: 192 us -> 94.5 us (0.49)
  waiting for transfers between devices: 124 us -> 39 us
  starting transfers between devices: 7.14 us -> 36.6 us
  blocking collectives: 22 us -> 0 us
  between operations: 16.5 us -> 1.07 us
  matrix products: 14.8 us -> 11.8 us
  local copies, waits for them, and re-layouts: 3.56 us -> 1.45 us
    all_gather x1 -> x0, waiting for transfers between devices: 90 us -> none  [local(): lax.all_gather(frozen_query_weight, ('dp', 'seq'), axis=0, tiled=True)]
    ppermute x0 -> x22, waiting for transfers between devices: none -> 39 us  [the longest x19 38.9 us: shift(): lax.ppermute(value, axis, [(i, (i + step) % size) for i in range(size)])]
    ppermute x0 -> x22, starting transfers between devices: none -> 36.6 us  [the longest x19 36 us: shift(): lax.ppermute(value, axis, [(i, (i + step) % size) for i in range(size)])]
    reduce_scatter x3 -> x0, waiting for transfers between devices: 31.8 us -> none  [the longest x1 22.1 us: local(): lax.psum_scatter(partial_value.astype(jnp.bfloat16), 'tensor', scatter_di...]
    psum x1 -> x0, blocking collectives: 12 us -> none  [local(): lax.psum(out_part.astype(jnp.bfloat16), ('tensor', 'seq'))]
    unnamed x1 -> x0, blocking collectives: 9.99 us -> none
    all_to_all x2 -> x0, starting transfers between devices: 6.97 us -> none  [the longest x1 3.51 us: local(): lax.all_to_all(saved_layer_input, 'seq', split_axis=1, concat_axis=0, til...]
    dot_general x6 -> x12, matrix products: 14.8 us -> 11.8 us  [the longest x6 7.6 us: dot_last(): lax.dot_general(left, right, (((1,), (1,)), ((), ())), preferred_element_...]
  transfers between devices with their start and end apart: 6 -> 22, of which waited for: 4 -> 11; matrix products, arithmetic and copies ran while one was open for 10% -> 12% of each run, Pallas kernels for 0% -> 0%
where the time goes in v1:
time: 94.5 us; the launch traced here: 94.2 us
  waiting for transfers between devices  39 us (41%)
  starting transfers between devices  36.6 us (39%)
  matrix products  11.8 us (12%)
  other arithmetic  4.31 us (5%)
  local copies, waits for them, and re-layouts  1.45 us (2%)
  between operations  1.07 us (1%)
    ppermute x19, waiting for transfers between devices, shift(): lax.ppermute(value, axis, [(i, (i + step) % size) for i in range(size)])  38.9 us
    ppermute x19, starting transfers between devices, shift(): lax.ppermute(value, axis, [(i, (i + step) % size) for i in range(size)])  36 us
    dot_general x6, matrix products, dot_last(): lax.dot_general(left, right, (((1,), (1,)), ((), ())), preferred_element_...  7.6 us
    dot_general x1, matrix products, local(): lax.dot_general(scattered, down_t, (((0,), (0,)), ((), ())), preferred_el...  2.17 us
    dot_general x5, matrix products, dot_plain(): lax.dot_general(left, right, (((1,), (0,)), ((), ())), preferred_element_...  2 us
  transfers between devices with their start and end apart: 22, of which 11 were waited for; matrix products, arithmetic and copies ran while one was open for 12% of the time, Pallas kernels for 0%

profile of v1, /device:TPU:0, one launch (start us, length us, event | category | flops | bytes accessed | tf_op | source)
XLA Modules:
  0.0 94.2 jit_solution(16347801926724253414)
XLA Ops:
  0.7 3.1 %collective-permute-start.10 = (bf16[128,1280]{1,0:T(8,128)(2,1)}, bf16[128,1280]{1,0:T(8,128)(2,1)}, u32[]{:S(2)}, u32[]{:S(2)}) collective-permute-start(bf16[128,1280]{1,0:T(8,128)(2,1)} %param.8), channel_id=1, source_target_pairs={{0,4},{4,8},{8,12},{12,0},{1,5},{5,9},{9,13},{13,1},{2,6},{6,10},{... | collective-permute-start | bytes 983048 | tf_op jit(solution)/shard_map/ppermute | solution.py:22
  3.7 2.1 %collective-permute-start.13 = (bf16[128,1280]{1,0:T(8,128)(2,1)}, bf16[128,1280]{1,0:T(8,128)(2,1)S(1)}, u32[]{:S(2)}, u32[]{:S(2)}) collective-permute-start(bf16[128,1280]{1,0:T(8,128)(2,1)} %param.8), channel_id=1, source_target_pairs={{0,12},{4,0},{8,4},{12,8},{1,13},{5,1},{9,5},{13,9},{2,14},{6,2},{... | collective-permute-start | bytes 983048 | tf_op jit(solution)/shard_map/ppermute | solution.py:22
  5.8 0.9 %collective-permute-start.6 = (bf16[128,1280]{1,0:T(8,128)(2,1)}, bf16[128,1280]{1,0:T(8,128)(2,1)S(1)}, u32[]{:S(2)}, u32[]{:S(2)}) collective-permute-start(bf16[128,1280]{1,0:T(8,128)(2,1)} %param.8), channel_id=1, source_target_pairs={{0,8},{4,12},{8,0},{12,4},{1,9},{5,13},{9,1},{13,5},{2,10},{6,14},... | collective-permute-start | bytes 983048 | tf_op jit(solution)/shard_map/ppermute | solution.py:22
  6.8 0.8 dynamic_slice.72
  7.5 1.3 %fusion.6 = f32[16,128]{1,0:T(8,128)S(1)} fusion(bf16[4,16,1280]{2,1,0:T(8,128)(2,1)} %param.13, bf16[128,1280]{1,0:T(8,128)(2,1)} %param.8, f32[4,128]{1,0:T(4,128)S(1)} %get-tuple-element.33), kind=kOutput, calls=%fused_computation.19 | convolution fusion | flops 20985856 | bytes 501760 | tf_op jit(solution)/shard_map/dot_general | solution.py:13
  8.8 0.0 copy-done
  8.8 1.3 %fusion.5 = f32[16,128]{1,0:T(8,128)S(1)} fusion(bf16[128,2560]{1,0:T(8,128)(2,1)S(1)} %copy-done, bf16[2560,4,16]{0,2,1:T(8,128)(2,1)} %param.12, f32[4,128]{1,0:T(4,128)S(1)} %get-tuple-element.33), kind=kOutput, calls=%fused_computation.18 | convolution fusion | flops 41957376 | bytes 993280 | tf_op jit(solution)/shard_map/dot_general | solution.py:13
  10.2 1.6 %collective-permute-start = (f32[32,128]{1,0:T(8,128)S(1)}, f32[32,128]{1,0:T(8,128)S(1)}, u32[]{:S(2)}, u32[]{:S(2)}) collective-permute-start(f32[32,128]{1,0:T(8,128)S(1)} %pad_maximum_fusion.1), channel_id=1, source_target_pairs={{0,2},{2,0},{1,3},{3,1},{4,6},{6,4},{5,7},{7,5},{8,10},{10,8},{9,1... | collective-permute-start | bytes 49160 | tf_op jit(solution)/shard_map/ppermute | solution.py:22
  11.7 0.7 convert_bitcast_fusion
  12.5 0.1 pad.24.clone
  12.6 1.4 %collective-permute-done = f32[32,128]{1,0:T(8,128)S(1)} collective-permute-done((f32[32,128]{1,0:T(8,128)S(1)}, f32[32,128]{1,0:T(8,128)S(1)}, u32[]{:S(2)}, u32[]{:S(2)}) %collective-permute-start) | collective-permute-done | bytes 16416 | tf_op jit(solution)/shard_map/ppermute | solution.py:22
  14.0 0.1 fusion.38
  14.1 1.3 %collective-permute-start.3 = (bf16[32,128]{1,0:T(8,128)(2,1)S(1)}, bf16[32,128]{1,0:T(8,128)(2,1)S(1)}, u32[]{:S(2)}, u32[]{:S(2)}) collective-permute-start(bf16[32,128]{1,0:T(8,128)(2,1)S(1)} %get-tuple-element.23), channel_id=1, source_target_pairs={{0,12},{4,0},{8,4},{12,8},{1,13},{5,1},{9,5},{13,9},{2,14},{6,2},{... | collective-permute-start | bytes 24584 | tf_op jit(solution)/shard_map/ppermute | solution.py:22
  15.4 9.8 %collective-permute-done.3 = bf16[32,128]{1,0:T(8,128)(2,1)S(1)} collective-permute-done((bf16[32,128]{1,0:T(8,128)(2,1)S(1)}, bf16[32,128]{1,0:T(8,128)(2,1)S(1)}, u32[]{:S(2)}, u32[]{:S(2)}) %collective-permute-start.3) | collective-permute-done | bytes 8224 | tf_op jit(solution)/shard_map/ppermute | solution.py:22
  25.2 10.5 %collective-permute-start.1 = (bf16[32,128]{1,0:T(8,128)(2,1)S(1)}, bf16[32,128]{1,0:T(8,128)(2,1)S(1)}, u32[]{:S(2)}, u32[]{:S(2)}) collective-permute-start(bf16[32,128]{1,0:T(8,128)(2,1)S(1)} %get-tuple-element.23), channel_id=1, source_target_pairs={{0,4},{4,8},{8,12},{12,0},{1,5},{5,9},{9,13},{13,1},{2,6},{6,10},{... | collective-permute-start | bytes 24584 | tf_op jit(solution)/shard_map/ppermute | solution.py:22
  35.7 1.4 %collective-permute-done.1 = bf16[32,128]{1,0:T(8,128)(2,1)S(1)} collective-permute-done((bf16[32,128]{1,0:T(8,128)(2,1)S(1)}, bf16[32,128]{1,0:T(8,128)(2,1)S(1)}, u32[]{:S(2)}, u32[]{:S(2)}) %collective-permute-start.1) | collective-permute-done | bytes 8224 | tf_op jit(solution)/shard_map/ppermute | solution.py:22
  37.0 1.7 %collective-permute-start.2 = (bf16[32,128]{1,0:T(8,128)(2,1)S(1)}, bf16[32,128]{1,0:T(8,128)(2,1)S(1)}, u32[]{:S(2)}, u32[]{:S(2)}) collective-permute-start(bf16[32,128]{1,0:T(8,128)(2,1)S(1)} %get-tuple-element.23), channel_id=1, source_target_pairs={{0,8},{4,12},{8,0},{12,4},{1,9},{5,13},{9,1},{13,5},{2,10},{6,14},... | collective-permute-start | bytes 24584 | tf_op jit(solution)/shard_map/ppermute | solution.py:22
  38.8 2.8 %collective-permute-done.2 = bf16[32,128]{1,0:T(8,128)(2,1)S(1)} collective-permute-done((bf16[32,128]{1,0:T(8,128)(2,1)S(1)}, bf16[32,128]{1,0:T(8,128)(2,1)S(1)}, u32[]{:S(2)}, u32[]{:S(2)}) %collective-permute-start.2) | collective-permute-done | bytes 8224 | tf_op jit(solution)/shard_map/ppermute | solution.py:22
  41.6 0.1 convert_reduce_fusion
  41.7 0.1 select_reduce_fusion.1
  41.9 0.3 convolution_convert_fusion
  42.2 0.1 collective-permute-start.17
  42.3 0.1 select_reduce_fusion
  42.4 0.1 compare_convert_fusion.1
  42.5 0.2 fusion.40
  42.7 0.2 fusion.36
  42.9 0.2 fusion.41
  43.1 1.2 %convolution_add_fusion.1 = f32[32,1280]{1,0:T(8,128)S(1)} fusion(f32[32,1280]{1,0:T(8,128)S(1)} %fusion.40, bf16[32,128]{1,0:T(8,128)(2,1)S(1)} %bitcast.152, bf16[128,1280]{1,0:T(8,128)(2,1)} %collective-permute-done.10), kind=kOutput, calls=%fused_computation.13 | convolution fusion | flops 10526720 | bytes 663552 | tf_op jit(solution)/shard_map/dot_general | solution.py:17
  44.3 0.2 fusion.4
  44.5 0.6 collective-permute-start.21
  45.0 0.1 add_convert_fusion
  45.1 1.8 %collective-permute-start.20 = (bf16[32,1280]{1,0:T(8,128)(2,1)S(1)}, bf16[32,1280]{1,0:T(8,128)(2,1)S(1)}, u32[]{:S(2)}, u32[]{:S(2)}) collective-permute-start(bf16[32,1280]{1,0:T(8,128)(2,1)S(1)} %get-tuple-element.10), channel_id=1, source_target_pairs={{0,12},{4,0},{8,4},{12,8},{1,13},{5,1},{9,5},{13,9},{2,14},{6,2},{... | collective-permute-start | bytes 245768 | tf_op jit(solution)/shard_map/ppermute | solution.py:22
  46.9 2.0 %collective-permute-start.19 = (bf16[32,1280]{1,0:T(8,128)(2,1)S(1)}, bf16[32,1280]{1,0:T(8,128)(2,1)S(1)}, u32[]{:S(2)}, u32[]{:S(2)}) collective-permute-start(bf16[32,1280]{1,0:T(8,128)(2,1)S(1)} %get-tuple-element.11), channel_id=1, source_target_pairs={{0,8},{4,12},{8,0},{12,4},{1,9},{5,13},{9,1},{13,5},{2,10},{6,14},... | collective-permute-start | bytes 245768 | tf_op jit(solution)/shard_map/ppermute | solution.py:22
  48.9 0.0 collective-permute-start.18
  49.0 0.7 broadcast_multiply_fusion
  49.7 0.4 collective-permute-done.20
  50.1 6.4 %collective-permute-done.19 = bf16[32,1280]{1,0:T(8,128)(2,1)S(1)} collective-permute-done((bf16[32,1280]{1,0:T(8,128)(2,1)S(1)}, bf16[32,1280]{1,0:T(8,128)(2,1)S(1)}, u32[]{:S(2)}, u32[]{:S(2)}) %collective-permute-start.19) | collective-permute-done | bytes 81952 | tf_op jit(solution)/shard_map/ppermute | solution.py:22
  56.6 0.2 broadcast_select_fusion.1
  56.8 1.0 %convolution_convert_fusion.4 = bf16[1280,128]{1,0:T(8,128)(2,1)S(1)} fusion(bf16[128,1280]{1,0:T(8,128)(2,1)S(1)} %copy-done.2, bf16[640,1280]{1,0:T(8,128)(2,1)S(1)} %get-tuple-element.6, bf16[640,1280]{1,0:T(8,128)(2,1)S(1)} %get-tuple-element.5), kind=kOutput, calls=%fused_computation.10 | convolution fusion | flops 426147840 | bytes 3932160 | tf_op jit(solution)/shard_map/dot_general | solution.py:13
  57.9 2.0 %convolution_convert_fusion.2 = bf16[1280,128]{1,0:T(8,128)(2,1)S(1)} fusion(bf16[128,1280]{1,0:T(8,128)(2,1)} %collective-permute-done.10, bf16[640,1280]{1,0:T(8,128)(2,1)S(1)} %get-tuple-element.6, bf16[640,1280]{1,0:T(8,128)(2,1)S(1)} %get-tuple-element.5), kind=kOutput, calls=%fused_computation.8 | convolution fusion | flops 426147840 | bytes 3932160 | tf_op jit(solution)/shard_map/dot_general | solution.py:13
  59.9 1.6 %collective-permute-start.11 = (bf16[128,640]{0,1:T(8,128)(2,1)S(1)}, bf16[128,640]{0,1:T(8,128)(2,1)S(1)}, u32[]{:S(2)}, u32[]{:S(2)}) collective-permute-start(bf16[128,640]{0,1:T(8,128)(2,1)S(1)} %dynamic-slice_bitcast_fusion.1), channel_id=1, source_target_pairs={{0,2},{2,0},{1,3},{3,1},{4,6},{6,4},{5,7},{7,5},{8,10},{10,8},{9,1... | collective-permute-start | bytes 491528 | tf_op jit(solution)/shard_map/ppermute | solution.py:22
  61.4 1.0 %convolution_convert_fusion.1 = bf16[1280,128]{1,0:T(8,128)(2,1)S(1)} fusion(bf16[128,1280]{1,0:T(8,128)(2,1)S(1)} %collective-permute-done.13, bf16[640,1280]{1,0:T(8,128)(2,1)S(1)} %get-tuple-element.6, bf16[640,1280]{1,0:T(8,128)(2,1)S(1)} %get-tuple-element.5), kind=kOutput, calls=%fused_computation.7 | convolution fusion | flops 426147840 | bytes 3932160 | tf_op jit(solution)/shard_map/dot_general | solution.py:13
  62.5 0.6 collective-permute-start.14
  63.1 1.6 %collective-permute-start.5 = (bf16[128,640]{0,1:T(8,128)(2,1)S(1)}, bf16[128,640]{0,1:T(8,128)(2,1)S(1)}, u32[]{:S(2)}, u32[]{:S(2)}) collective-permute-start(bf16[128,640]{0,1:T(8,128)(2,1)S(1)} %dynamic-slice_bitcast_fusion.3), channel_id=1, source_target_pairs={{0,2},{2,0},{1,3},{3,1},{4,6},{6,4},{5,7},{7,5},{8,10},{10,8},{9,1... | collective-permute-start | bytes 491528 | tf_op jit(solution)/shard_map/ppermute | solution.py:22
  64.6 1.0 %convolution_convert_fusion.3 = bf16[1280,128]{1,0:T(8,128)(2,1)S(1)} fusion(bf16[128,1280]{1,0:T(8,128)(2,1)S(1)} %collective-permute-done.6, bf16[640,1280]{1,0:T(8,128)(2,1)S(1)} %get-tuple-element.6, bf16[640,1280]{1,0:T(8,128)(2,1)S(1)} %get-tuple-element.5), kind=kOutput, calls=%fused_computation.9 | convolution fusion | flops 426147840 | bytes 3932160 | tf_op jit(solution)/shard_map/dot_general | solution.py:13
  65.7 0.6 collective-permute-start.7
  66.3 0.5 collective-permute-done.11
  66.8 0.4 collective-permute-start.12
  67.3 3.0 %collective-permute-done.14 = bf16[128,640]{0,1:T(8,128)(2,1)S(1)} collective-permute-done((bf16[128,640]{0,1:T(8,128)(2,1)S(1)}, bf16[128,640]{0,1:T(8,128)(2,1)S(1)}, u32[]{:S(2)}, u32[]{:S(2)}) %collective-permute-start.14) | collective-permute-done | bytes 163872 | tf_op jit(solution)/shard_map/ppermute | solution.py:22
  70.3 0.1 collective-permute-start.15
  70.4 5.4 %collective-permute-done.7 = bf16[128,640]{0,1:T(8,128)(2,1)S(1)} collective-permute-done((bf16[128,640]{0,1:T(8,128)(2,1)S(1)}, bf16[128,640]{0,1:T(8,128)(2,1)S(1)}, u32[]{:S(2)}, u32[]{:S(2)}) %collective-permute-start.7) | collective-permute-done | bytes 163872 | tf_op jit(solution)/shard_map/ppermute | solution.py:22
  75.8 1.8 %collective-permute-start.8 = (bf16[128,640]{0,1:T(8,128)(2,1)S(1)}, bf16[128,640]{0,1:T(8,128)(2,1)S(1)}, u32[]{:S(2)}, u32[]{:S(2)}) collective-permute-start(bf16[128,640]{0,1:T(8,128)(2,1)S(1)} %fusion.12), channel_id=1, source_target_pairs={{0,8},{4,12},{8,0},{12,4},{1,9},{5,13},{9,1},{13,5},{2,10},{6,14},... | collective-permute-start | bytes 491528 | tf_op jit(solution)/shard_map/ppermute | solution.py:22
  77.7 0.1 fusion.21
  77.8 2.5 %collective-permute-start.16 = (bf16[128,640]{0,1:T(8,128)(2,1)S(1)}, bf16[128,640]{0,1:T(8,128)(2,1)S(1)}, u32[]{:S(2)}, u32[]{:S(2)}) collective-permute-start(bf16[128,640]{0,1:T(8,128)(2,1)S(1)} %get-tuple-element.14), channel_id=1, source_target_pairs={{0,2},{2,0},{1,3},{3,1},{4,6},{6,4},{5,7},{7,5},{8,10},{10,8},{9,1... | collective-permute-start | bytes 491528 | tf_op jit(solution)/shard_map/ppermute | solution.py:22
  80.4 4.2 %collective-permute-done.8 = bf16[128,640]{0,1:T(8,128)(2,1)S(1)} collective-permute-done((bf16[128,640]{0,1:T(8,128)(2,1)S(1)}, bf16[128,640]{0,1:T(8,128)(2,1)S(1)}, u32[]{:S(2)}, u32[]{:S(2)}) %collective-permute-start.8) | collective-permute-done | bytes 163872 | tf_op jit(solution)/shard_map/ppermute | solution.py:22
  84.5 0.1 fusion.26
  84.7 1.9 %collective-permute-start.9 = (bf16[128,640]{0,1:T(8,128)(2,1)S(1)}, bf16[128,640]{0,1:T(8,128)(2,1)S(1)}, u32[]{:S(2)}, u32[]{:S(2)}) collective-permute-start(bf16[128,640]{0,1:T(8,128)(2,1)S(1)} %get-tuple-element.18), channel_id=1, source_target_pairs={{0,2},{2,0},{1,3},{3,1},{4,6},{6,4},{5,7},{7,5},{8,10},{10,8},{9,1... | collective-permute-start | bytes 491528 | tf_op jit(solution)/shard_map/ppermute | solution.py:22
  86.5 0.7 multiply_bitcast_fusion
  87.3 3.6 %collective-permute-done.9 = bf16[128,640]{0,1:T(8,128)(2,1)S(1)} collective-permute-done((bf16[128,640]{0,1:T(8,128)(2,1)S(1)}, bf16[128,640]{0,1:T(8,128)(2,1)S(1)}, u32[]{:S(2)}, u32[]{:S(2)}) %collective-permute-start.9) | collective-permute-done | bytes 163872 | tf_op jit(solution)/shard_map/ppermute | solution.py:22
  90.9 0.2 fusion.19
  91.2 0.3 fusion.9
  91.5 0.1 maximum_convert_fusion
  91.6 0.4 copy.12
  92.0 2.2 %fusion.3 = bf16[128,2560]{1,0:T(8,128)(2,1)} fusion(f32[128,2560]{1,0:T(8,128)S(1)} %copy.12, f32[128]{0:T(128)S(1)} %get-tuple-element.4, bf16[2560,4,16]{0,2,1:T(8,128)(2,1)} %param.12, bf16[16,128]{1,0:T(8,128)(2,1)S(1)} %get-tuple-element.20, bf16[4,128]{1,0:T(4,128)(2,1)S(1)} %get-tuple-element.32), kind=kOutput, calls=%fused_computation.4 | convolution fusion | flops 43261952 | bytes 2299392 | tf_op jit(solution)/shard_map/dot_general | solution.py:124
  (57 shorter events, 0.6 us)
Async XLA Ops:
  0.6 8.2 %copy-start = (bf16[128,2560]{1,0:T(8,128)(2,1)S(1)}, bf16[128,2560]{1,0:T(8,128)(2,1)}, u32[]{:S(2)}) copy-start(bf16[128,2560]{1,0:T(8,128)(2,1)} %param.7) | copy-start | bytes 1966084
  0.6 11.8 %copy-start.3 = (s32[4]{0:T(128)S(1)}, s32[4]{0:T(128)}, u32[]{:S(2)}) copy-start(s32[4]{0:T(128)} %param.10) | copy-start | bytes 52
  0.7 42.4 %collective-permute-start.10 = (bf16[128,1280]{1,0:T(8,128)(2,1)}, bf16[128,1280]{1,0:T(8,128)(2,1)}, u32[]{:S(2)}, u32[]{:S(2)}) collective-permute-start(bf16[128,1280]{1,0:T(8,128)(2,1)} %param.8), channel_id=1, source_target_pairs={{0,4},{4,8},{8,12},{12,0},{1,5},{5,9},{9,13},{13,1},{2,6},{6,10},{... | collective-permute-start | bytes 983048 | tf_op jit(solution)/shard_map/ppermute | solution.py:22
  3.7 39.2 %collective-permute-start.13 = (bf16[128,1280]{1,0:T(8,128)(2,1)}, bf16[128,1280]{1,0:T(8,128)(2,1)S(1)}, u32[]{:S(2)}, u32[]{:S(2)}) collective-permute-start(bf16[128,1280]{1,0:T(8,128)(2,1)} %param.8), channel_id=1, source_target_pairs={{0,12},{4,0},{8,4},{12,8},{1,13},{5,1},{9,5},{13,9},{2,14},{6,2},{... | collective-permute-start | bytes 983048 | tf_op jit(solution)/shard_map/ppermute | solution.py:22
  5.8 38.4 %collective-permute-start.6 = (bf16[128,1280]{1,0:T(8,128)(2,1)}, bf16[128,1280]{1,0:T(8,128)(2,1)S(1)}, u32[]{:S(2)}, u32[]{:S(2)}) collective-permute-start(bf16[128,1280]{1,0:T(8,128)(2,1)} %param.8), channel_id=1, source_target_pairs={{0,8},{4,12},{8,0},{12,4},{1,9},{5,13},{9,1},{13,5},{2,10},{6,14},... | collective-permute-start | bytes 983048 | tf_op jit(solution)/shard_map/ppermute | solution.py:22
  6.8 49.8 %collective-permute-start.4 = (bf16[640,1280]{1,0:T(8,128)(2,1)}, bf16[640,1280]{1,0:T(8,128)(2,1)S(1)}, u32[]{:S(2)}, u32[]{:S(2)}) collective-permute-start(bf16[640,1280]{1,0:T(8,128)(2,1)} %param.11), channel_id=1, source_target_pairs={{0,1},{1,0},{2,3},{3,2},{4,5},{5,4},{6,7},{7,6},{8,9},{9,8},{10,11... | collective-permute-start | bytes 4915208 | tf_op jit(solution)/shard_map/ppermute | solution.py:39
  10.2 32.3 %copy-start.2 = (bf16[128,1280]{1,0:T(8,128)(2,1)S(1)}, bf16[128,1280]{1,0:T(8,128)(2,1)}, u32[]{:S(2)}) copy-start(bf16[128,1280]{1,0:T(8,128)(2,1)} %param.8) | copy-start | bytes 983044
  10.2 3.8 %collective-permute-start = (f32[32,128]{1,0:T(8,128)S(1)}, f32[32,128]{1,0:T(8,128)S(1)}, u32[]{:S(2)}, u32[]{:S(2)}) collective-permute-start(f32[32,128]{1,0:T(8,128)S(1)} %pad_maximum_fusion.1), channel_id=1, source_target_pairs={{0,2},{2,0},{1,3},{3,1},{4,6},{6,4},{5,7},{7,5},{8,10},{10,8},{9,1... | collective-permute-start | bytes 49160 | tf_op jit(solution)/shard_map/ppermute | solution.py:22
  14.1 11.1 %collective-permute-start.3 = (bf16[32,128]{1,0:T(8,128)(2,1)S(1)}, bf16[32,128]{1,0:T(8,128)(2,1)S(1)}, u32[]{:S(2)}, u32[]{:S(2)}) collective-permute-start(bf16[32,128]{1,0:T(8,128)(2,1)S(1)} %get-tuple-element.23), channel_id=1, source_target_pairs={{0,12},{4,0},{8,4},{12,8},{1,13},{5,1},{9,5},{13,9},{2,14},{6,2},{... | collective-permute-start | bytes 24584 | tf_op jit(solution)/shard_map/ppermute | solution.py:22
  25.2 11.8 %collective-permute-start.1 = (bf16[32,128]{1,0:T(8,128)(2,1)S(1)}, bf16[32,128]{1,0:T(8,128)(2,1)S(1)}, u32[]{:S(2)}, u32[]{:S(2)}) collective-permute-start(bf16[32,128]{1,0:T(8,128)(2,1)S(1)} %get-tuple-element.23), channel_id=1, source_target_pairs={{0,4},{4,8},{8,12},{12,0},{1,5},{5,9},{9,13},{13,1},{2,6},{6,10},{... | collective-permute-start | bytes 24584 | tf_op jit(solution)/shard_map/ppermute | solution.py:22
  37.0 4.5 %collective-permute-start.2 = (bf16[32,128]{1,0:T(8,128)(2,1)S(1)}, bf16[32,128]{1,0:T(8,128)(2,1)S(1)}, u32[]{:S(2)}, u32[]{:S(2)}) collective-permute-start(bf16[32,128]{1,0:T(8,128)(2,1)S(1)} %get-tuple-element.23), channel_id=1, source_target_pairs={{0,8},{4,12},{8,0},{12,4},{1,9},{5,13},{9,1},{13,5},{2,10},{6,14},... | collective-permute-start | bytes 24584 | tf_op jit(solution)/shard_map/ppermute | solution.py:22
  42.2 2.8 %collective-permute-start.17 = (bf16[128,1280]{1,0:T(8,128)(2,1)S(1)}, bf16[128,1280]{1,0:T(8,128)(2,1)S(1)}, u32[]{:S(2)}, u32[]{:S(2)}) collective-permute-start(bf16[128,1280]{1,0:T(8,128)(2,1)S(1)} %constant_dynamic-slice_fusion.2), channel_id=1, source_target_pairs={{0,1},{1,0},{2,3},{3,2},{4,5},{5,4},{6,7},{7,6},{8,9},{9,8},{10,11... | collective-permute-start | bytes 983048 | tf_op jit(solution)/shard_map/ppermute | solution.py:84
  44.2 12.4 %copy-start.1 = (bf16[640,1280]{1,0:T(8,128)(2,1)S(1)}, bf16[640,1280]{1,0:T(8,128)(2,1)}, u32[]{:S(2)}) copy-start(bf16[640,1280]{1,0:T(8,128)(2,1)} %param.11) | copy-start | bytes 4915204
  44.5 4.5 %collective-permute-start.21 = (f32[32,640]{1,0:T(8,128)S(1)}, f32[32,640]{1,0:T(8,128)S(1)}, u32[]{:S(2)}, u32[]{:S(2)}) collective-permute-start(f32[32,640]{1,0:T(8,128)S(1)} %constant_dynamic-slice_fusion), channel_id=1, source_target_pairs={{0,1},{1,0},{2,3},{3,2},{4,5},{5,4},{6,7},{7,6},{8,9},{9,8},{10,11... | collective-permute-start | bytes 245768 | tf_op jit(solution)/shard_map/ppermute | solution.py:149
  45.1 5.0 %collective-permute-start.20 = (bf16[32,1280]{1,0:T(8,128)(2,1)S(1)}, bf16[32,1280]{1,0:T(8,128)(2,1)S(1)}, u32[]{:S(2)}, u32[]{:S(2)}) collective-permute-start(bf16[32,1280]{1,0:T(8,128)(2,1)S(1)} %get-tuple-element.10), channel_id=1, source_target_pairs={{0,12},{4,0},{8,4},{12,8},{1,13},{5,1},{9,5},{13,9},{2,14},{6,2},{... | collective-permute-start | bytes 245768 | tf_op jit(solution)/shard_map/ppermute | solution.py:22
  46.9 9.6 %collective-permute-start.19 = (bf16[32,1280]{1,0:T(8,128)(2,1)S(1)}, bf16[32,1280]{1,0:T(8,128)(2,1)S(1)}, u32[]{:S(2)}, u32[]{:S(2)}) collective-permute-start(bf16[32,1280]{1,0:T(8,128)(2,1)S(1)} %get-tuple-element.11), channel_id=1, source_target_pairs={{0,8},{4,12},{8,0},{12,4},{1,9},{5,13},{9,1},{13,5},{2,10},{6,14},... | collective-permute-start | bytes 245768 | tf_op jit(solution)/shard_map/ppermute | solution.py:22
  48.9 7.6 %collective-permute-start.18 = (bf16[32,1280]{1,0:T(8,128)(2,1)S(1)}, bf16[32,1280]{1,0:T(8,128)(2,1)S(1)}, u32[]{:S(2)}, u32[]{:S(2)}) collective-permute-start(bf16[32,1280]{1,0:T(8,128)(2,1)S(1)} %get-tuple-element.9), channel_id=1, source_target_pairs={{0,4},{4,8},{8,12},{12,0},{1,5},{5,9},{9,13},{13,1},{2,6},{6,10},{... | collective-permute-start | bytes 245768 | tf_op jit(solution)/shard_map/ppermute | solution.py:22
  59.9 6.9 %collective-permute-start.11 = (bf16[128,640]{0,1:T(8,128)(2,1)S(1)}, bf16[128,640]{0,1:T(8,128)(2,1)S(1)}, u32[]{:S(2)}, u32[]{:S(2)}) collective-permute-start(bf16[128,640]{0,1:T(8,128)(2,1)S(1)} %dynamic-slice_bitcast_fusion.1), channel_id=1, source_target_pairs={{0,2},{2,0},{1,3},{3,1},{4,6},{6,4},{5,7},{7,5},{8,10},{10,8},{9,1... | collective-permute-start | bytes 491528 | tf_op jit(solution)/shard_map/ppermute | solution.py:22
  62.5 7.8 %collective-permute-start.14 = (bf16[128,640]{0,1:T(8,128)(2,1)S(1)}, bf16[128,640]{0,1:T(8,128)(2,1)S(1)}, u32[]{:S(2)}, u32[]{:S(2)}) collective-permute-start(bf16[128,640]{0,1:T(8,128)(2,1)S(1)} %dynamic-slice_bitcast_fusion), channel_id=1, source_target_pairs={{0,2},{2,0},{1,3},{3,1},{4,6},{6,4},{5,7},{7,5},{8,10},{10,8},{9,1... | collective-permute-start | bytes 491528 | tf_op jit(solution)/shard_map/ppermute | solution.py:22
  63.1 14.5 %collective-permute-start.5 = (bf16[128,640]{0,1:T(8,128)(2,1)S(1)}, bf16[128,640]{0,1:T(8,128)(2,1)S(1)}, u32[]{:S(2)}, u32[]{:S(2)}) collective-permute-start(bf16[128,640]{0,1:T(8,128)(2,1)S(1)} %dynamic-slice_bitcast_fusion.3), channel_id=1, source_target_pairs={{0,2},{2,0},{1,3},{3,1},{4,6},{6,4},{5,7},{7,5},{8,10},{10,8},{9,1... | collective-permute-start | bytes 491528 | tf_op jit(solution)/shard_map/ppermute | solution.py:22
  65.7 10.1 %collective-permute-start.7 = (bf16[128,640]{0,1:T(8,128)(2,1)S(1)}, bf16[128,640]{0,1:T(8,128)(2,1)S(1)}, u32[]{:S(2)}, u32[]{:S(2)}) collective-permute-start(bf16[128,640]{0,1:T(8,128)(2,1)S(1)} %dynamic-slice_bitcast_fusion.2), channel_id=1, source_target_pairs={{0,2},{2,0},{1,3},{3,1},{4,6},{6,4},{5,7},{7,5},{8,10},{10,8},{9,1... | collective-permute-start | bytes 491528 | tf_op jit(solution)/shard_map/ppermute | solution.py:22
  66.8 10.8 %collective-permute-start.12 = (bf16[128,640]{0,1:T(8,128)(2,1)S(1)}, bf16[128,640]{0,1:T(8,128)(2,1)S(1)}, u32[]{:S(2)}, u32[]{:S(2)}) collective-permute-start(bf16[128,640]{0,1:T(8,128)(2,1)S(1)} %fusion.11), channel_id=1, source_target_pairs={{0,12},{4,0},{8,4},{12,8},{1,13},{5,1},{9,5},{13,9},{2,14},{6,2},{... | collective-permute-start | bytes 491528 | tf_op jit(solution)/shard_map/ppermute | solution.py:22
  70.3 7.3 %collective-permute-start.15 = (bf16[128,640]{0,1:T(8,128)(2,1)S(1)}, bf16[128,640]{0,1:T(8,128)(2,1)S(1)}, u32[]{:S(2)}, u32[]{:S(2)}) collective-permute-start(bf16[128,640]{0,1:T(8,128)(2,1)S(1)} %fusion.10), channel_id=1, source_target_pairs={{0,4},{4,8},{8,12},{12,0},{1,5},{5,9},{9,13},{13,1},{2,6},{6,10},{... | collective-permute-start | bytes 491528 | tf_op jit(solution)/shard_map/ppermute | solution.py:22
  75.8 8.7 %collective-permute-start.8 = (bf16[128,640]{0,1:T(8,128)(2,1)S(1)}, bf16[128,640]{0,1:T(8,128)(2,1)S(1)}, u32[]{:S(2)}, u32[]{:S(2)}) collective-permute-start(bf16[128,640]{0,1:T(8,128)(2,1)S(1)} %fusion.12), channel_id=1, source_target_pairs={{0,8},{4,12},{8,0},{12,4},{1,9},{5,13},{9,1},{13,5},{2,10},{6,14},... | collective-permute-start | bytes 491528 | tf_op jit(solution)/shard_map/ppermute | solution.py:22
  77.8 9.4 %collective-permute-start.16 = (bf16[128,640]{0,1:T(8,128)(2,1)S(1)}, bf16[128,640]{0,1:T(8,128)(2,1)S(1)}, u32[]{:S(2)}, u32[]{:S(2)}) collective-permute-start(bf16[128,640]{0,1:T(8,128)(2,1)S(1)} %get-tuple-element.14), channel_id=1, source_target_pairs={{0,2},{2,0},{1,3},{3,1},{4,6},{6,4},{5,7},{7,5},{8,10},{10,8},{9,1... | collective-permute-start | bytes 491528 | tf_op jit(solution)/shard_map/ppermute | solution.py:22
  84.7 6.2 %collective-permute-start.9 = (bf16[128,640]{0,1:T(8,128)(2,1)S(1)}, bf16[128,640]{0,1:T(8,128)(2,1)S(1)}, u32[]{:S(2)}, u32[]{:S(2)}) collective-permute-start(bf16[128,640]{0,1:T(8,128)(2,1)S(1)} %get-tuple-element.18), channel_id=1, source_target_pairs={{0,2},{2,0},{1,3},{3,1},{4,6},{6,4},{5,7},{7,5},{8,10},{10,8},{9,1... | collective-permute-start | bytes 491528 | tf_op jit(solution)/shard_map/ppermute | solution.py:22

commit v2 on v1

v2 whole, which is shorter than its diff:
```python
import jax
import jax.numpy as jnp
from jax import lax
from jax.experimental import pallas as pl
from jax.experimental.pallas import tpu as pltpu
from jax.sharding import PartitionSpec as P

OWN_MAX = 2
ADAPTER_SCALE = 2.0
F32 = jnp.float32
BF16 = jnp.bfloat16
VMEM = pl.BlockSpec(memory_space=pltpu.VMEM)
SMEM = pl.BlockSpec(memory_space=pltpu.SMEM)
ANY = pl.BlockSpec(memory_space=pl.ANY)


def dot_last(left, right):
    return lax.dot_general(left, right, (((1,), (1,)), ((), ())), preferred_element_type=F32)


def dot_plain(left, right):
    return lax.dot_general(left, right, (((1,), (0,)), ((), ())), preferred_element_type=F32)


def dot_first(left, right):
    return lax.dot_general(left, right, (((0,), (0,)), ((), ())), preferred_element_type=F32)


def call(body, out_shape, args, specs, out_specs=None, scratch=(), aliases=None):
    in_specs = [specs.get(i, VMEM) for i in range(len(args))]
    if out_specs is None:
        out_specs = jax.tree.map(lambda _: VMEM, out_shape)
    return pl.pallas_call(
        body,
        out_shape=out_shape,
        in_specs=in_specs,
        out_specs=out_specs,
        scratch_shapes=scratch,
        input_output_aliases=aliases or {},
        compiler_params=pltpu.CompilerParams(vmem_limit_bytes=12 << 20),
        cost_estimate=pl.CostEstimate(flops=1<<33, bytes_accessed=1<<25, transcendentals=0),
    )(*args)


def array(shape, dtype):
    return jax.ShapeDtypeStruct(shape, dtype)


def one(scalar):
    return scalar.reshape(1)


def multiply(piece, w_parts, first=None):
    parts = len(w_parts)

    def body(*refs):
        if first is None:
            refs = (None, *refs)
        piece_ref, ws, outs = refs[1], refs[2 : 2 + parts], refs[2 + parts :]

        def work(order):
            for k in range(parts):
                outs[k][...] = dot_last(piece_ref[...], ws[order[k]][...]).astype(BF16)

        if first is None:
            work(range(parts))
        else:
            pl.when(refs[0][0] == 0)(lambda: work((0, 1)))
            pl.when(refs[0][0] == 1)(lambda: work((1, 0)))

    shapes = [array((piece.shape[0], w.shape[0]), BF16) for w in w_parts]
    head = [] if first is None else [first]
    return list(call(body, shapes, [*head, piece, *w_parts], {i: SMEM for i in range(len(head))}))


def project(core, ids, x, g, down_t, up_t, rank):
    adapters = down_t.shape[0] // rank

    def body(core_ref, ids_ref, x_ref, g_ref, down_ref, up_ref, out_ref):
        own_ids = ids_ref[pl.ds(core_ref[0], 1), :]
        for i, (rows, factors) in enumerate(((x_ref, down_ref), (g_ref, up_ref))):
            every = dot_last(factors[...], rows[...])
            own = jnp.zeros((rank, every.shape[1]), F32)
            for a in range(adapters):
                own += jnp.where(own_ids == a, every[a * rank : (a + 1) * rank], 0.0)
            out_ref[i * rank : (i + 1) * rank] = own

    shape = array((2 * rank, x.shape[0]), F32)
    return call(body, shape, [core, ids, x, g, down_t, up_t], {0: SMEM})


def slot_row(ids, slot_ref, adapters):
    slot = jnp.zeros(ids.shape, jnp.int32)
    for a in range(adapters):
        slot = jnp.where(ids == a, slot_ref[a], slot)
    return slot


def lift_down(owner_slot, core, ids, x, lows, slots):
    adapters, cores = owner_slot.shape[0], ids.shape[0]
    rank = lows[0].shape[0] // 2
    rows, width = x.shape
    half = width // 2

    def body(slot_ref, core_ref, ids_ref, x_ref, *rest):
        low_refs = rest[: len(lows)]
        card_ref, low_ref, mine_ref, away_ref, spread_ref = rest[len(lows) :]
        low = low_refs[0][...]
        for ref in low_refs[1:]:
            low = low + ref[...]
        card_ref[...] = jnp.concatenate(
            [
                low[:rank],
                ids_ref[...].astype(F32),
                jnp.zeros((OWN_MAX * rank - rank - cores, rows), F32),
            ],
            axis=0,
        ).astype(BF16)
        low_out = low[rank:].astype(BF16)
        low_ref[...] = low_out
        core = core_ref[0]
        slot = slot_row(ids_ref[pl.ds(core, 1), :], slot_ref, adapters)
        for s in range(slots):
            part = jnp.where(slot == s, low_out.astype(F32), 0.0)
            spread_ref[s * rank : (s + 1) * rank] = part.astype(BF16)
        for ref, part in ((mine_ref, core), (away_ref, 1 - core)):
            at = pl.ds(pl.multiple_of(part * half, 128), half)
            ref[...] = dot_plain(spread_ref[...], x_ref[:, at]).astype(BF16)

    wide = array((slots * rank, half), BF16)
    shapes = [array((OWN_MAX * rank, rows), BF16), array((rank, rows), BF16), wide, wide]
    scratch = [pltpu.VMEM((slots * rank, rows), BF16)]
    args = [owner_slot, core, ids, x, *lows]
    return call(body, shapes, args, {0: SMEM, 1: SMEM}, scratch=scratch)


def letters(place, card, mine, got, n):
    deep, half, rows = mine.shape[0] // n, mine.shape[1], card.shape[1]

    def body(place_ref, card_ref, mine_ref, got_ref, *outs):
        for s, out in enumerate(outs):
            at = pl.ds(pl.multiple_of((place_ref[0] ^ s) * deep, 16), deep)
            total = mine_ref[at].astype(F32) + got_ref[at].astype(F32)
            out[:, :half] = total.astype(BF16)
            out[:, half:] = card_ref[...]

    shapes = [array((deep, half + rows), BF16)] * n
    return call(body, shapes, [place, card, mine, got], {0: SMEM})


def lift_up(owner_slot, core, place, cards, blocks, rank):
    n, adapters = len(blocks), owner_slot.shape[0]
    width = blocks[0].shape[1]
    half = width // 2

    def body(slot_ref, core_ref, place_ref, *refs):
        card_refs, block_refs, outs = refs[:n], refs[n : 2 * n], refs[2 * n :]
        core, first = core_ref[0], place_ref[0] * OWN_MAX
        lifts = []
        for ref in card_refs:
            card = ref[...].astype(F32)
            ids = jnp.where(core == 0, card[rank : rank + 1], card[rank + 1 : rank + 2])
            slot = slot_row(ids.astype(jnp.int32), slot_ref, adapters)
            lift = [jnp.where(slot == first + o, card[:rank], 0.0) for o in range(OWN_MAX)]
            lifts.append(jnp.concatenate(lift, axis=0).astype(BF16))
        if half % 128:
            outs[0][...] = sum(dot_plain(a, b[...]) for a, b in zip(lifts, block_refs))
            return
        for ref, part in zip(outs, (core, 1 - core)):
            at = pl.ds(pl.multiple_of(part * half, 128), half)
            ref[...] = sum(dot_plain(a, b[:, at]) for a, b in zip(lifts, block_refs))

    deep = OWN_MAX * rank
    shapes = [array((deep, width), F32)] if half % 128 else [array((deep, half), F32)] * 2
    args = [owner_slot, core, place, *cards, *blocks]
    out = call(body, shapes, args, {0: SMEM, 1: SMEM, 2: SMEM})
    if half % 128:
        at = core[0] * half
        return [lax.dynamic_slice_in_dim(out[0], p, half, 1) for p in (at, half - at)]
    return out


def finish(weight, core, offsets, ids, low_out, down_t, pieces, into=None):
    rows, width = ids.shape[1], down_t.shape[1]
    rank = low_out.shape[0]
    adapters, chunk, count = weight.shape[0], pieces[0].shape[1], len(pieces)

    def body(weight_ref, core_ref, *refs):
        offset_refs, (ids_ref, low_ref, down_ref) = refs[:count], refs[count : count + 3]
        piece_refs, (out_ref, held, sems) = refs[count + 3 : 2 * count + 3], refs[-3:]
        own_ids = ids_ref[pl.ds(core_ref[0], 1), :]
        scale = jnp.zeros(own_ids.shape, F32)
        spread = []
        for a in range(adapters):
            scale = jnp.where(own_ids == a, weight_ref[a], scale)
            spread.append(jnp.where(own_ids == a, low_ref[...].astype(F32), 0.0))
        spread = jnp.concatenate(spread, axis=0).astype(BF16)
        scale = jnp.broadcast_to(scale, (rows, rows)).T[:, :1]
        copies = []
        for i in range(count):
            at = pl.ds(pl.multiple_of(offset_refs[i][0], 128), chunk)
            term = dot_first(spread, down_ref[:, at])
            total = piece_refs[i][...].astype(F32) + ADAPTER_SCALE * term
            held[i] = (scale * total).astype(BF16)
            copies.append(pltpu.make_async_copy(held.at[i], out_ref.at[:, at], sems.at[i]))
            copies[-1].start()
        for copy in copies:
            copy.wait()

    args = [weight, core, *offsets, ids, low_out, down_t, *pieces]
    specs = {i: SMEM for i in range(2 + count)}
    aliases = None
    if into is not None:
        specs[len(args)] = ANY
        aliases = {len(args): 0}
        args.append(into)
    scratch = [pltpu.VMEM((count, rows, chunk), BF16), pltpu.SemaphoreType.DMA((count,))]
    shape = array((rows, width), BF16)
    return call(body, shape, args, specs, out_specs=ANY, scratch=scratch, aliases=aliases)


def swap(value, axis, step):
    size = lax.axis_size(axis)
    return lax.ppermute(value, axis, [(i, i ^ step) for i in range(size)])


def pick(value, index):
    return lax.dynamic_index_in_dim(value, index, 0, keepdims=False)


def choose(values, index):
    out = values[0]
    for i in range(1, len(values)):
        out = jnp.where(index == i, values[i], out)
    return out


def after(value, *others):
    return lax.optimization_barrier((value, *others))[0]


def local(x, g, ids, owner_slot, w, down, up):
    rows = x.shape[0]
    adapters = owner_slot.shape[0]
    rank = up.shape[1]
    n, tensors, cores = lax.axis_size("dp"), lax.axis_size("tensor"), lax.axis_size("seq")
    z, t, c = lax.axis_index("dp"), lax.axis_index("tensor"), lax.axis_index("seq")
    core, place = one(c), one(z)
    slots = n * OWN_MAX
    labels = jnp.arange(adapters, dtype=jnp.int32)
    ids = ids.reshape(cores, rows)

    top = n // 2
    blocks = {0: g, top: swap(g, "dp", top)}

    def hand_on(froms, *ready):
        bit = top // 2
        while bit:
            for s in [s for s in blocks if s in froms]:
                blocks[s ^ bit] = swap(after(blocks[s], *ready), "dp", bit)
            bit //= 2

    hand_on(range(top))

    w_other = swap(w, "seq", 1)
    width = cores * w.shape[0]
    chunk = width // tensors
    first = None
    if tensors == cores:
        w_parts, first = [w, w_other], one(t ^ c)
    else:
        w_chip = jnp.where(c == 0, jnp.stack([w, w_other]), jnp.stack([w_other, w]))
        w_chip = w_chip.reshape(tensors, chunk, -1)
        w_parts = [pick(w_chip, t ^ k) for k in range(tensors)]

    parts, totals = [], []

    def product(s, *ready):
        made = multiply(after(blocks[s], *ready), w_parts, first)
        kept = made[0].astype(F32)
        for k in range(1, tensors):
            kept = kept + swap(made[k], "tensor", k).astype(F32)
        parts.append(made)
        totals.append(kept.astype(BF16))

    product(0)

    down_t = down.transpose(1, 2, 0).reshape(adapters * rank, -1)
    up_t = up.reshape(adapters * rank, -1)
    low = project(core, after(ids, *parts[0]), x, g, down_t, up_t, rank)
    lows = [low] + [swap(low, "tensor", s) for s in range(1, tensors)]

    product(1, low)
    card, low_out, mine, away = lift_down(
        owner_slot, core, after(ids, *parts[1]), x, lows, slots
    )
    got = swap(away, "seq", 1)

    hand_on(range(top, n), mine)
    for s in range(2, n - 1):
        product(s, *parts[s - 1], mine, away)

    sent = letters(place, card, mine, after(got, *parts[n - 2]), n)

    product(n - 1, *parts[n - 2])

    received = [sent[0]] + [swap(sent[s], "dp", s) for s in range(1, n)]
    half = mine.shape[1]
    cards = [v[:, half:] for v in received]
    down_sum = sum(v[:, :half].astype(F32) for v in received)
    all_ids = jnp.stack([v[rank : rank + cores] for v in cards]).astype(jnp.int32)
    counts = jnp.sum((all_ids.reshape(1, -1) == labels[:, None]).astype(F32), axis=1)
    weight = F32(n * cores * rows) / (F32(adapters) * counts)
    my_slots = z * OWN_MAX + jnp.arange(OWN_MAX, dtype=jnp.int32)
    slot_weight = ADAPTER_SCALE * jnp.sum(
        jnp.where(owner_slot[None, :] == my_slots[:, None], weight[None, :], 0.0), axis=1
    )
    down_grad = down_sum.reshape(OWN_MAX, rank, half) * slot_weight[:, None, None]
    down_grad = down_grad.transpose(2, 0, 1)

    back = [swap(v, "dp", s) if s else v for s, v in enumerate(totals)]
    span = n // tensors
    low_bits, high_bits = z % span, z // span
    pieces, offsets = [], []
    for r in range(span):
        choices = [back[r + k * span] for k in range(tensors)]
        choices[0] = after(choices[0], *parts[n - 1])
        for k in range(tensors):
            piece = choose(choices, t ^ k ^ high_bits)
            pieces.append(swap(piece, "tensor", k) if k else piece)
            offsets.append((r ^ low_bits) * width + (t ^ k) * chunk)
    if chunk % 128 == 0:
        offsets = [one(v) for v in offsets]
        args = (ids, low_out, down_t)
        early = finish(weight, core, offsets[:-1], *args, pieces[:-1])
        input_gradient = finish(weight, core, offsets[-1:], *args, pieces[-1:], into=early)
    else:
        base = jnp.zeros((rows, span * width), BF16)
        for piece, offset in zip(pieces, offsets):
            base = lax.dynamic_update_slice_in_dim(base, piece, offset, 1)
        own_match = (pick(ids, c)[:, None] == labels[None, :]).astype(F32)
        own_weight = jnp.sum(own_match * weight[None, :], axis=1)
        spread = (own_match.T.astype(BF16)[:, None, :] * low_out[None]).reshape(-1, rows)
        total = base.astype(F32) + ADAPTER_SCALE * dot_first(spread, down_t)
        input_gradient = (own_weight[:, None] * total).astype(BF16)

    up_mine, up_away = lift_up(
        owner_slot, core, place, cards, [blocks[s] for s in range(n)], rank
    )
    up_sum = up_mine + swap(up_away, "seq", 1)
    up_grad = up_sum.reshape(OWN_MAX, rank, -1) * slot_weight[:, None, None]
    return input_gradient, down_grad, up_grad


def solution(mesh):
    in_specs = (
        P(("groups", "dp", "seq"), "tensor"),
        P(("groups", "dp", "seq"), "tensor"),
        P(("groups", "dp")),
        P("groups"),
        P(("dp", "seq"), "tensor"),
        P(("groups", "tensor"), None, None),
        P("groups", None, "tensor"),
    )
    out_specs = (
        P(("groups", "dp", "seq"), "tensor"),
        P(("groups", "tensor", "seq"), "dp", None),
        P(("groups", "dp"), None, ("tensor", "seq")),
    )
    return jax.shard_map(local, mesh=mesh, in_specs=in_specs, out_specs=out_specs, check_vma=False)
```

time: 94.5 us -> 68.4 us (0.72)
  starting transfers between devices: 36.6 us -> 22.5 us
  matrix products: 11.8 us -> 0 us
  Pallas kernels: 0 us -> 9.72 us
  waiting for transfers between devices: 39 us -> 30.4 us
  other arithmetic: 4.31 us -> 2.12 us
  local copies, waits for them, and re-layouts: 1.45 us -> 2.45 us
    ppermute x22 -> x19, starting transfers between devices: 36.6 us -> 22.5 us  [swap(): return lax.ppermute(value, axis, [(i, i ^ step) for i in range(size)])]
    dot_general x12 -> x0, matrix products: 11.8 us -> none  [the longest x6 7.6 us: dot_last(): lax.dot_general(left, right, (((1,), (1,)), ((), ())), preferred_element_...]
    pallas_call x0 -> x10, Pallas kernels: none -> 9.72 us  [call(): pl.pallas_call(body, out_shape=out_shape, in_specs=in_specs, out_specs=ou...]
    ppermute x22 -> x19, waiting for transfers between devices: 39 us -> 30.4 us  [swap(): return lax.ppermute(value, axis, [(i, i ^ step) for i in range(size)])]
    unnamed x8 -> x18, local copies, waits for them, and re-layouts: 0.04 us -> 2.43 us
  transfers between devices with their start and end apart: 22 -> 19, of which waited for: 11 -> 7; matrix products, arithmetic and copies ran while one was open for 12% -> 3% of each run, Pallas kernels for 0% -> 12%
where the time goes in v2:
time: 68.4 us; the launch traced here: 68.1 us
  waiting for transfers between devices  30.4 us (44%)
  starting transfers between devices  22.5 us (33%)
  Pallas kernels  9.72 us (14%)
  local copies, waits for them, and re-layouts  2.45 us (4%)
  other arithmetic  2.12 us (3%)
  between operations  0.86 us (1%)
    ppermute x19, waiting for transfers between devices, swap(): return lax.ppermute(value, axis, [(i, i ^ step) for i in range(size)])  30.4 us
    ppermute x19, starting transfers between devices, swap(): return lax.ppermute(value, axis, [(i, i ^ step) for i in range(size)])  22.5 us
    pallas_call x10, Pallas kernels, call(): pl.pallas_call(body, out_shape=out_shape, in_specs=in_specs, out_specs=ou...  9.72 us
    unnamed x18, local copies, waits for them, and re-layouts  2.43 us
  transfers between devices with their start and end apart: 19, of which 7 were waited for; matrix products, arithmetic and copies ran while one was open for 3% of the time, Pallas kernels for 12%

profile of v2, /device:TPU:0, one launch (start us, length us, event | category | flops | bytes accessed | tf_op | source)
XLA Modules:
  0.0 68.1 jit_solution(16093660814336849137)
XLA Ops:
  0.6 0.5 collective-permute-start.1
  1.1 3.7 %collective-permute-start.4 = (bf16[128,1280]{1,0:T(8,128)(2,1)}, bf16[128,1280]{1,0:T(8,128)(2,1)S(1)}, u32[]{:S(2)}, u32[]{:S(2)}) collective-permute-start(bf16[128,1280]{1,0:T(8,128)(2,1)} %refs_4_.1), channel_id=1, source_target_pairs={{0,8},{4,12},{8,0},{12,4},{1,9},{5,13},{9,1},{13,5},{2,10},{6,14},... | collective-permute-start | bytes 983048 | tf_op jit(solution)/shard_map/ppermute | solution.py:224
  4.8 1.6 %collective-permute-start = (bf16[128,1280]{1,0:T(8,128)(2,1)}, bf16[128,1280]{1,0:T(8,128)(2,1)S(1)}, u32[]{:S(2)}, u32[]{:S(2)}) collective-permute-start(bf16[128,1280]{1,0:T(8,128)(2,1)} %refs_4_.1), channel_id=1, source_target_pairs={{0,4},{4,0},{8,12},{12,8},{1,5},{5,1},{9,13},{13,9},{2,6},{6,2},{1... | collective-permute-start | bytes 983048 | tf_op jit(solution)/shard_map/ppermute | solution.py:224
  6.4 0.0 collective-permute-done.1.refs_3_
  6.4 1.4 %copy-done.1 = bf16[640,1280]{1,0:T(8,128)(2,1)S(1)} copy-done((bf16[640,1280]{1,0:T(8,128)(2,1)S(1)}, bf16[640,1280]{1,0:T(8,128)(2,1)}, u32[]{:S(2)}) %copy-start.1) | copy-done | bytes 1638424
  7.8 1.0 %copy-done.4 = bf16[128,1280]{1,0:T(8,128)(2,1)S(1)} copy-done((bf16[128,1280]{1,0:T(8,128)(2,1)S(1)}, bf16[128,1280]{1,0:T(8,128)(2,1)}, u32[]{:S(2)}) %copy-start.4) | copy-done | bytes 327704
  8.8 0.0 copy-start.8
  8.8 1.1 %shard_map.94 = (bf16[128,640]{1,0:T(8,128)(2,1)S(1)}, bf16[128,640]{1,0:T(8,128)(2,1)S(1)}) custom-call(s32[1]{0:T(128)} %bitcast.3.refs_0_, bf16[128,1280]{1,0:T(8,128)(2,1)S(1)} %copy-done.4, bf16[640,1280]{1,0:T(8,128)(2,1)S(1)} %copy-done.1, bf16[640,1280]{1,0:T(8,128)(2,1)S(1)} %collective-permute-done.1.refs_3_), custom_call_target="tpu_custom_call" | custom-call | flops 8589934592 | bytes 33554432 | tf_op jit(solution)/shard_map/pallas_call | solution.py:33
  9.9 1.6 %collective-permute-start.16 = (bf16[128,640]{1,0:T(8,128)(2,1)S(1)}, bf16[128,640]{1,0:T(8,128)(2,1)S(1)}, u32[]{:S(2)}, u32[]{:S(2)}) collective-permute-start(bf16[128,640]{1,0:T(8,128)(2,1)S(1)} %get-tuple-element.31), channel_id=1, source_target_pairs={{0,2},{2,0},{1,3},{3,1},{4,6},{6,4},{5,7},{7,5},{8,10},{10,8},{9,1... | collective-permute-start | bytes 491528 | tf_op jit(solution)/shard_map/ppermute | solution.py:224
  11.5 0.0 copy-done.3
  11.5 0.0 copy-done.5
  11.5 0.0 copy-done.6
  11.5 0.0 copy-done.7
  11.5 0.0 copy-done.8
  11.5 0.0 copy-start.2
  11.5 0.5 shard_map.95.rest_0_
  12.0 0.0 copy-start
  12.0 0.6 collective-permute-start.2
  12.6 8.0 %collective-permute-done.refs_1_.refs_5_ = bf16[128,1280]{1,0:T(8,128)(2,1)S(1)} collective-permute-done((bf16[128,1280]{1,0:T(8,128)(2,1)}, bf16[128,1280]{1,0:T(8,128)(2,1)S(1)}, u32[]{:S(2)}, u32[]{:S(2)}) %collective-permute-start) | collective-permute-done | bytes 327712 | tf_op jit(solution)/shard_map/ppermute | solution.py:224
  20.6 0.0 copy-done.2
  20.6 1.1 %shard_map.96 = (bf16[128,640]{1,0:T(8,128)(2,1)S(1)}, bf16[128,640]{1,0:T(8,128)(2,1)S(1)}) custom-call(s32[1]{0:T(128)} %bitcast.3.refs_0_, bf16[128,1280]{1,0:T(8,128)(2,1)S(1)} %collective-permute-done.refs_1_.refs_5_, bf16[640,1280]{1,0:T(8,128)(2,1)S(1)} %copy-done.2, bf16[640,1280]{1,0:T(8,128)(2,1)S(1)} %collective-permute-done.1.refs_3_), custom_call_target="tpu_custom_call" | custom-call | flops 8589934592 | bytes 33554432 | tf_op jit(solution)/shard_map/pallas_call | solution.py:33
  21.7 1.6 %collective-permute-start.11 = (bf16[128,640]{1,0:T(8,128)(2,1)S(1)}, bf16[128,640]{1,0:T(8,128)(2,1)S(1)}, u32[]{:S(2)}, u32[]{:S(2)}) collective-permute-start(bf16[128,640]{1,0:T(8,128)(2,1)S(1)} %get-tuple-element.35), channel_id=1, source_target_pairs={{0,2},{2,0},{1,3},{3,1},{4,6},{6,4},{5,7},{7,5},{8,10},{10,8},{9,1... | collective-permute-start | bytes 491528 | tf_op jit(solution)/shard_map/ppermute | solution.py:224
  23.4 0.0 collective-permute-done.2.rest_1_
  23.4 0.0 copy-done
  23.4 0.9 %shard_map.97 = (bf16[32,128]{1,0:T(8,128)(2,1)S(1)}, bf16[16,128]{1,0:T(8,128)(2,1)S(1)}, bf16[128,1280]{1,0:T(8,128)(2,1)S(1)}, bf16[128,1280]{1,0:T(8,128)(2,1)S(1)}) custom-call(s32[4]{0:T(128)S(1)} %copy-done, s32[1]{0:T(128)} %bitcast.1.core_ref, s32[2,128]{1,0:T(2,128)S(1)} %bitcast.31, bf16[128,2560]{1,0:T(8,128)(2,1)S(1)} %copy-done.3, ...), custom_call_target="tpu_custom_call" | custom-call | flops 8589934592 | bytes 33554432 | tf_op jit(solution)/shard_map/pallas_call | solution.py:33
  24.2 0.1 collective-permute-start.3
  24.3 0.0 collective-permute-done.4.refs_1_.refs_6_
  24.3 1.5 %collective-permute-start.8 = (bf16[128,1280]{1,0:T(8,128)(2,1)S(1)}, bf16[128,1280]{1,0:T(8,128)(2,1)S(1)}, u32[]{:S(2)}, u32[]{:S(2)}) collective-permute-start(bf16[128,1280]{1,0:T(8,128)(2,1)S(1)} %collective-permute-done.4.refs_1_.refs_6_), channel_id=1, source_target_pairs={{0,4},{4,0},{8,12},{12,8},{1,5},{5,1},{9,13},{13,9},{2,6},{6,2},{1... | collective-permute-start | bytes 983048 | tf_op jit(solution)/shard_map/ppermute | solution.py:224
  25.8 1.1 %shard_map.98 = (bf16[128,640]{1,0:T(8,128)(2,1)S(1)}, bf16[128,640]{1,0:T(8,128)(2,1)S(1)}) custom-call(s32[1]{0:T(128)} %bitcast.3.refs_0_, bf16[128,1280]{1,0:T(8,128)(2,1)S(1)} %collective-permute-done.4.refs_1_.refs_6_, bf16[640,1280]{1,0:T(8,128)(2,1)S(1)} %copy-done.2, bf16[640,1280]{1,0:T(8,128)(2,1)S(1)} %collective-permute-done.1.refs_3_), custom_call_target="tpu_custom_call" | custom-call | flops 8589934592 | bytes 33554432 | tf_op jit(solution)/shard_map/pallas_call | solution.py:33
  26.9 0.6 collective-permute-start.14
  27.5 0.0 collective-permute-done.11
  27.6 1.6 %collective-permute-start.12 = (bf16[128,640]{1,0:T(8,128)(2,1)S(1)}, bf16[128,640]{1,0:T(8,128)(2,1)S(1)}, u32[]{:S(2)}, u32[]{:S(2)}) collective-permute-start(bf16[128,640]{1,0:T(8,128)(2,1)S(1)} %add_convert_fusion.2), channel_id=1, source_target_pairs={{0,4},{4,0},{8,12},{12,8},{1,5},{5,1},{9,13},{13,9},{2,6},{6,2},{1... | collective-permute-start | bytes 491528 | tf_op jit(solution)/shard_map/ppermute | solution.py:224
  29.2 0.0 collective-permute-done.16
  29.2 4.0 %collective-permute-done.14 = bf16[128,640]{1,0:T(8,128)(2,1)S(1)} collective-permute-done((bf16[128,640]{1,0:T(8,128)(2,1)S(1)}, bf16[128,640]{1,0:T(8,128)(2,1)S(1)}, u32[]{:S(2)}, u32[]{:S(2)}) %collective-permute-start.14) | collective-permute-done | bytes 163872 | tf_op jit(solution)/shard_map/ppermute | solution.py:224
  33.3 0.2 collective-permute-start.15
  33.5 0.0 collective-permute-done.3.got_ref
  33.5 0.1 shard_map.99
  33.6 1.8 %collective-permute-start.5 = (bf16[32,1408]{1,0:T(8,128)(2,1)S(1)}, bf16[32,1408]{1,0:T(8,128)(2,1)S(1)}, u32[]{:S(2)}, u32[]{:S(2)}) collective-permute-start(bf16[32,1408]{1,0:T(8,128)(2,1)S(1)} %get-tuple-element.45), channel_id=1, source_target_pairs={{0,4},{4,0},{8,12},{12,8},{1,5},{5,1},{9,13},{13,9},{2,6},{6,2},{1... | collective-permute-start | bytes 270344 | tf_op jit(solution)/shard_map/ppermute | solution.py:224
  35.4 1.6 %collective-permute-start.6 = (bf16[32,1408]{1,0:T(8,128)(2,1)S(1)}, bf16[32,1408]{1,0:T(8,128)(2,1)S(1)}, u32[]{:S(2)}, u32[]{:S(2)}) collective-permute-start(bf16[32,1408]{1,0:T(8,128)(2,1)S(1)} %get-tuple-element.46), channel_id=1, source_target_pairs={{0,8},{4,12},{8,0},{12,4},{1,9},{5,13},{9,1},{13,5},{2,10},{6,14},... | collective-permute-start | bytes 270344 | tf_op jit(solution)/shard_map/ppermute | solution.py:224
  37.0 0.0 collective-permute-done.8.refs_1_.refs_7_
  37.0 1.1 %shard_map.100 = (bf16[128,640]{1,0:T(8,128)(2,1)S(1)}, bf16[128,640]{1,0:T(8,128)(2,1)S(1)}) custom-call(s32[1]{0:T(128)} %bitcast.3.refs_0_, bf16[128,1280]{1,0:T(8,128)(2,1)S(1)} %collective-permute-done.8.refs_1_.refs_7_, bf16[640,1280]{1,0:T(8,128)(2,1)S(1)} %copy-done.2, bf16[640,1280]{1,0:T(8,128)(2,1)S(1)} %collective-permute-done.1.refs_3_), custom_call_target="tpu_custom_call" | custom-call | flops 8589934592 | bytes 33554432 | tf_op jit(solution)/shard_map/pallas_call | solution.py:33
  38.2 0.5 collective-permute-start.9
  38.7 2.3 %collective-permute-done.12 = bf16[128,640]{1,0:T(8,128)(2,1)S(1)} collective-permute-done((bf16[128,640]{1,0:T(8,128)(2,1)S(1)}, bf16[128,640]{1,0:T(8,128)(2,1)S(1)}, u32[]{:S(2)}, u32[]{:S(2)}) %collective-permute-start.12) | collective-permute-done | bytes 163872 | tf_op jit(solution)/shard_map/ppermute | solution.py:224
  41.0 2.0 %collective-permute-start.7 = (bf16[32,1408]{1,0:T(8,128)(2,1)S(1)}, bf16[32,1408]{1,0:T(8,128)(2,1)S(1)}, u32[]{:S(2)}, u32[]{:S(2)}) collective-permute-start(bf16[32,1408]{1,0:T(8,128)(2,1)S(1)} %get-tuple-element.47), channel_id=1, source_target_pairs={{0,12},{4,8},{8,4},{12,0},{1,13},{5,9},{9,5},{13,1},{2,14},{6,10},... | collective-permute-start | bytes 270344 | tf_op jit(solution)/shard_map/ppermute | solution.py:224
  43.0 5.8 %collective-permute-done.15 = bf16[128,640]{1,0:T(8,128)(2,1)S(1)} collective-permute-done((bf16[128,640]{1,0:T(8,128)(2,1)S(1)}, bf16[128,640]{1,0:T(8,128)(2,1)S(1)}, u32[]{:S(2)}, u32[]{:S(2)}) %collective-permute-start.15) | collective-permute-done | bytes 163872 | tf_op jit(solution)/shard_map/ppermute | solution.py:224
  48.8 0.6 collective-permute-start.17
  49.4 0.0 collective-permute-done.5
  49.4 0.6 collective-permute-done.6
  50.0 0.0 collective-permute-done.7
  50.0 0.9 %shard_map.103 = (f32[32,640]{1,0:T(8,128)S(1)}, f32[32,640]{1,0:T(8,128)S(1)}) custom-call(s32[4]{0:T(128)S(1)} %copy-done, s32[1]{0:T(128)} %bitcast.1.core_ref, s32[1]{0:T(128)} %bitcast.place_ref, bf16[32,128]{1,0:T(8,128)(2,1)S(1)} %slice.48.refs_0_, bf16[32,128]{1,0:T(8,128)(2,1)S(1)} %slice.58.refs_1_, bf16[32,128]{1,0:T(8,128)(2,1)S(1)} %slice.59.refs_2_, ...), custom_call_target="tpu_custom_call" | custom-call | flops 8589934592 | bytes 33554432 | tf_op jit(solution)/shard_map/pallas_call | solution.py:33
  50.9 0.1 collective-permute-start.18
  51.0 0.1 convert_reduce_fusion
  51.2 0.2 fusion
  51.4 0.7 %multiply_bitcast_fusion = f32[1280,2,16]{0,2,1:T(8,128)} fusion(f32[2,16,1280]{2,1,0:T(8,128)S(1)} %bitcast.34, f32[2]{0:T(128)S(1)} %broadcast_multiply_fusion.1), kind=kLoop, calls=%fused_computation.4 | loop fusion | flops 40960 | bytes 327688 | tf_op jit(solution)/shard_map/transpose | solution.py:319
  52.2 0.0 collective-permute-done.9
  52.2 1.3 %collective-permute-start.10 = (bf16[128,640]{1,0:T(8,128)(2,1)S(1)}, bf16[128,640]{1,0:T(8,128)(2,1)S(1)}, u32[]{:S(2)}, u32[]{:S(2)}) collective-permute-start(bf16[128,640]{1,0:T(8,128)(2,1)S(1)} %add_convert_fusion.3), channel_id=1, source_target_pairs={{0,12},{4,8},{8,4},{12,0},{1,13},{5,9},{9,5},{13,1},{2,14},{6,10},... | collective-permute-start | bytes 491528 | tf_op jit(solution)/shard_map/ppermute | solution.py:224
  53.6 0.0 collective-permute-done.18
  53.6 0.7 %broadcast_multiply_fusion = f32[2,16,640]{2,1,0:T(8,128)} fusion(f32[2,16,640]{2,1,0:T(8,128)S(1)} %bitcast.35, f32[2]{0:T(128)S(1)} %broadcast_multiply_fusion.1), kind=kLoop, calls=%fused_computation.10 | loop fusion | flops 20480 | bytes 163848 | tf_op jit(solution)/shard_map/mul | solution.py:351
  54.3 6.5 %collective-permute-done.10 = bf16[128,640]{1,0:T(8,128)(2,1)S(1)} collective-permute-done((bf16[128,640]{1,0:T(8,128)(2,1)S(1)}, bf16[128,640]{1,0:T(8,128)(2,1)S(1)}, u32[]{:S(2)}, u32[]{:S(2)}) %collective-permute-start.10) | collective-permute-done | bytes 163872 | tf_op jit(solution)/shard_map/ppermute | solution.py:224
  60.8 1.0 %collective-permute-start.13 = (bf16[128,640]{1,0:T(8,128)(2,1)S(1)}, bf16[128,640]{1,0:T(8,128)(2,1)S(1)}, u32[]{:S(2)}, u32[]{:S(2)}) collective-permute-start(bf16[128,640]{1,0:T(8,128)(2,1)S(1)} %get-tuple-element.58), channel_id=1, source_target_pairs={{0,2},{2,0},{1,3},{3,1},{4,6},{6,4},{5,7},{7,5},{8,10},{10,8},{9,1... | collective-permute-start | bytes 491528 | tf_op jit(solution)/shard_map/ppermute | solution.py:224
  61.8 0.0 collective-permute-done.17.refs_7_
  61.8 1.6 %shard_map.101.refs_5_ = bf16[128,2560]{1,0:T(8,128)(2,1)} custom-call(f32[4]{0:T(128)S(1)} %multiply_divide_fusion.weight_ref, s32[1]{0:T(128)} %bitcast.1.core_ref, s32[1]{0:T(128)} %bitcast.13.refs_0_, s32[1]{0:T(128)} %bitcast.14.refs_1_, s32[1]{0:T(128)} %bitcast.15.refs_2_, s32[2,128]{1,0:T(2,128)S(1)} %bitcast.32, ...), custom_call_target="tpu_custom_call" | custom-call | flops 8589934592 | bytes 33554432 | tf_op jit(solution)/shard_map/pallas_call | solution.py:33
  63.4 3.2 %collective-permute-done.13.refs_4_ = bf16[128,640]{1,0:T(8,128)(2,1)S(1)} collective-permute-done((bf16[128,640]{1,0:T(8,128)(2,1)S(1)}, bf16[128,640]{1,0:T(8,128)(2,1)S(1)}, u32[]{:S(2)}, u32[]{:S(2)}) %collective-permute-start.13) | collective-permute-done | bytes 163872 | tf_op jit(solution)/shard_map/ppermute | solution.py:224
  66.6 1.5 %shard_map.102 = bf16[128,2560]{1,0:T(8,128)(2,1)} custom-call(f32[4]{0:T(128)S(1)} %multiply_divide_fusion.weight_ref, s32[1]{0:T(128)} %bitcast.1.core_ref, s32[1]{0:T(128)} %bitcast.12.refs_0_, s32[2,128]{1,0:T(2,128)S(1)} %bitcast.33, bf16[16,128]{1,0:T(8,128)(2,1)S(1)} %get-tuple-element.48.refs_4_.refs_2_, ...), custom_call_target="tpu_custom_call", output_to_operand_aliasing={{}: (7, {})} | custom-call | flops 8589934592 | bytes 33554432 | tf_op jit(solution)/shard_map/pallas_call | solution.py:33
  (27 shorter events, 0.4 us)
Async XLA Ops:
  0.6 5.8 %collective-permute-start.1 = (bf16[640,1280]{1,0:T(8,128)(2,1)}, bf16[640,1280]{1,0:T(8,128)(2,1)S(1)}, u32[]{:S(2)}, u32[]{:S(2)}) collective-permute-start(bf16[640,1280]{1,0:T(8,128)(2,1)} %refs_2_.7), channel_id=1, source_target_pairs={{0,1},{1,0},{2,3},{3,2},{4,5},{5,4},{6,7},{7,6},{8,9},{9,8},{10,11... | collective-permute-start | bytes 4915208 | tf_op jit(solution)/shard_map/ppermute | solution.py:224
  1.1 23.2 %collective-permute-start.4 = (bf16[128,1280]{1,0:T(8,128)(2,1)}, bf16[128,1280]{1,0:T(8,128)(2,1)S(1)}, u32[]{:S(2)}, u32[]{:S(2)}) collective-permute-start(bf16[128,1280]{1,0:T(8,128)(2,1)} %refs_4_.1), channel_id=1, source_target_pairs={{0,8},{4,12},{8,0},{12,4},{1,9},{5,13},{9,1},{13,5},{2,10},{6,14},... | collective-permute-start | bytes 983048 | tf_op jit(solution)/shard_map/ppermute | solution.py:224
  4.8 15.8 %collective-permute-start = (bf16[128,1280]{1,0:T(8,128)(2,1)}, bf16[128,1280]{1,0:T(8,128)(2,1)S(1)}, u32[]{:S(2)}, u32[]{:S(2)}) collective-permute-start(bf16[128,1280]{1,0:T(8,128)(2,1)} %refs_4_.1), channel_id=1, source_target_pairs={{0,4},{4,0},{8,12},{12,8},{1,5},{5,1},{9,13},{13,9},{2,6},{6,2},{1... | collective-permute-start | bytes 983048 | tf_op jit(solution)/shard_map/ppermute | solution.py:224
  6.4 1.4 %copy-start.1 = (bf16[640,1280]{1,0:T(8,128)(2,1)S(1)}, bf16[640,1280]{1,0:T(8,128)(2,1)}, u32[]{:S(2)}) copy-start(bf16[640,1280]{1,0:T(8,128)(2,1)} %refs_2_.7) | copy-start | bytes 4915204
  7.8 1.0 %copy-start.4 = (bf16[128,1280]{1,0:T(8,128)(2,1)S(1)}, bf16[128,1280]{1,0:T(8,128)(2,1)}, u32[]{:S(2)}) copy-start(bf16[128,1280]{1,0:T(8,128)(2,1)} %refs_4_.1) | copy-start | bytes 983044
  8.8 2.7 %copy-start.3 = (bf16[128,2560]{1,0:T(8,128)(2,1)S(1)}, bf16[128,2560]{1,0:T(8,128)(2,1)}, u32[]{:S(2)}) copy-start(bf16[128,2560]{1,0:T(8,128)(2,1)} %x_ref.3) | copy-start | bytes 1966084
  8.8 2.7 %copy-start.5 = (bf16[128,1280]{1,0:T(8,128)(2,1)S(1)}, bf16[128,1280]{1,0:T(8,128)(2,1)}, u32[]{:S(2)}) copy-start(bf16[128,1280]{1,0:T(8,128)(2,1)} %refs_4_.1) | copy-start | bytes 983044
  8.8 2.7 %copy-start.6 = (bf16[2560,4,16]{0,2,1:T(8,128)(2,1)S(1)}, bf16[2560,4,16]{0,2,1:T(8,128)(2,1)}, u32[]{:S(2)}) copy-start(bf16[2560,4,16]{0,2,1:T(8,128)(2,1)} %param.12) | copy-start | bytes 983044
  8.8 2.7 %copy-start.7 = (bf16[4,16,1280]{2,1,0:T(8,128)(2,1)S(1)}, bf16[4,16,1280]{2,1,0:T(8,128)(2,1)}, u32[]{:S(2)}) copy-start(bf16[4,16,1280]{2,1,0:T(8,128)(2,1)} %param.13) | copy-start | bytes 491524
  8.8 2.7 %copy-start.8 = (s32[256]{0:T(256)S(1)}, s32[256]{0:T(256)}, u32[]{:S(2)}) copy-start(s32[256]{0:T(256)} %param.9) | copy-start | bytes 3076
  9.9 19.3 %collective-permute-start.16 = (bf16[128,640]{1,0:T(8,128)(2,1)S(1)}, bf16[128,640]{1,0:T(8,128)(2,1)S(1)}, u32[]{:S(2)}, u32[]{:S(2)}) collective-permute-start(bf16[128,640]{1,0:T(8,128)(2,1)S(1)} %get-tuple-element.31), channel_id=1, source_target_pairs={{0,2},{2,0},{1,3},{3,1},{4,6},{6,4},{5,7},{7,5},{8,10},{10,8},{9,1... | collective-permute-start | bytes 491528 | tf_op jit(solution)/shard_map/ppermute | solution.py:224
  11.5 9.1 %copy-start.2 = (bf16[640,1280]{1,0:T(8,128)(2,1)S(1)}, bf16[640,1280]{1,0:T(8,128)(2,1)}, u32[]{:S(2)}) copy-start(bf16[640,1280]{1,0:T(8,128)(2,1)} %refs_2_.7) | copy-start | bytes 4915204
  12.0 11.4 %copy-start = (s32[4]{0:T(128)S(1)}, s32[4]{0:T(128)}, u32[]{:S(2)}) copy-start(s32[4]{0:T(128)} %slot_ref.3) | copy-start | bytes 52
  12.0 11.3 %collective-permute-start.2 = (f32[32,128]{1,0:T(8,128)S(1)}, f32[32,128]{1,0:T(8,128)S(1)}, u32[]{:S(2)}, u32[]{:S(2)}) collective-permute-start(f32[32,128]{1,0:T(8,128)S(1)} %shard_map.95.rest_0_), channel_id=1, source_target_pairs={{0,2},{2,0},{1,3},{3,1},{4,6},{6,4},{5,7},{7,5},{8,10},{10,8},{9,1... | collective-permute-start | bytes 49160 | tf_op jit(solution)/shard_map/ppermute | solution.py:224
  21.7 5.8 %collective-permute-start.11 = (bf16[128,640]{1,0:T(8,128)(2,1)S(1)}, bf16[128,640]{1,0:T(8,128)(2,1)S(1)}, u32[]{:S(2)}, u32[]{:S(2)}) collective-permute-start(bf16[128,640]{1,0:T(8,128)(2,1)S(1)} %get-tuple-element.35), channel_id=1, source_target_pairs={{0,2},{2,0},{1,3},{3,1},{4,6},{6,4},{5,7},{7,5},{8,10},{10,8},{9,1... | collective-permute-start | bytes 491528 | tf_op jit(solution)/shard_map/ppermute | solution.py:224
  24.2 9.3 %collective-permute-start.3 = (bf16[128,1280]{1,0:T(8,128)(2,1)S(1)}, bf16[128,1280]{1,0:T(8,128)(2,1)S(1)}, u32[]{:S(2)}, u32[]{:S(2)}) collective-permute-start(bf16[128,1280]{1,0:T(8,128)(2,1)S(1)} %get-tuple-element.39), channel_id=1, source_target_pairs={{0,1},{1,0},{2,3},{3,2},{4,5},{5,4},{6,7},{7,6},{8,9},{9,8},{10,11... | collective-permute-start | bytes 983048 | tf_op jit(solution)/shard_map/ppermute | solution.py:224
  24.3 12.7 %collective-permute-start.8 = (bf16[128,1280]{1,0:T(8,128)(2,1)S(1)}, bf16[128,1280]{1,0:T(8,128)(2,1)S(1)}, u32[]{:S(2)}, u32[]{:S(2)}) collective-permute-start(bf16[128,1280]{1,0:T(8,128)(2,1)S(1)} %collective-permute-done.4.refs_1_.refs_6_), channel_id=1, source_target_pairs={{0,4},{4,0},{8,12},{12,8},{1,5},{5,1},{9,13},{13,9},{2,6},{6,2},{1... | collective-permute-start | bytes 983048 | tf_op jit(solution)/shard_map/ppermute | solution.py:224
  26.9 6.3 %collective-permute-start.14 = (bf16[128,640]{1,0:T(8,128)(2,1)S(1)}, bf16[128,640]{1,0:T(8,128)(2,1)S(1)}, u32[]{:S(2)}, u32[]{:S(2)}) collective-permute-start(bf16[128,640]{1,0:T(8,128)(2,1)S(1)} %get-tuple-element.42), channel_id=1, source_target_pairs={{0,2},{2,0},{1,3},{3,1},{4,6},{6,4},{5,7},{7,5},{8,10},{10,8},{9,1... | collective-permute-start | bytes 491528 | tf_op jit(solution)/shard_map/ppermute | solution.py:224
  27.6 13.4 %collective-permute-start.12 = (bf16[128,640]{1,0:T(8,128)(2,1)S(1)}, bf16[128,640]{1,0:T(8,128)(2,1)S(1)}, u32[]{:S(2)}, u32[]{:S(2)}) collective-permute-start(bf16[128,640]{1,0:T(8,128)(2,1)S(1)} %add_convert_fusion.2), channel_id=1, source_target_pairs={{0,4},{4,0},{8,12},{12,8},{1,5},{5,1},{9,13},{13,9},{2,6},{6,2},{1... | collective-permute-start | bytes 491528 | tf_op jit(solution)/shard_map/ppermute | solution.py:224
  33.3 15.5 %collective-permute-start.15 = (bf16[128,640]{1,0:T(8,128)(2,1)S(1)}, bf16[128,640]{1,0:T(8,128)(2,1)S(1)}, u32[]{:S(2)}, u32[]{:S(2)}) collective-permute-start(bf16[128,640]{1,0:T(8,128)(2,1)S(1)} %add_convert_fusion.1), channel_id=1, source_target_pairs={{0,8},{4,12},{8,0},{12,4},{1,9},{5,13},{9,1},{13,5},{2,10},{6,14},... | collective-permute-start | bytes 491528 | tf_op jit(solution)/shard_map/ppermute | solution.py:224
  33.6 15.8 %collective-permute-start.5 = (bf16[32,1408]{1,0:T(8,128)(2,1)S(1)}, bf16[32,1408]{1,0:T(8,128)(2,1)S(1)}, u32[]{:S(2)}, u32[]{:S(2)}) collective-permute-start(bf16[32,1408]{1,0:T(8,128)(2,1)S(1)} %get-tuple-element.45), channel_id=1, source_target_pairs={{0,4},{4,0},{8,12},{12,8},{1,5},{5,1},{9,13},{13,9},{2,6},{6,2},{1... | collective-permute-start | bytes 270344 | tf_op jit(solution)/shard_map/ppermute | solution.py:224
  35.4 14.6 %collective-permute-start.6 = (bf16[32,1408]{1,0:T(8,128)(2,1)S(1)}, bf16[32,1408]{1,0:T(8,128)(2,1)S(1)}, u32[]{:S(2)}, u32[]{:S(2)}) collective-permute-start(bf16[32,1408]{1,0:T(8,128)(2,1)S(1)} %get-tuple-element.46), channel_id=1, source_target_pairs={{0,8},{4,12},{8,0},{12,4},{1,9},{5,13},{9,1},{13,5},{2,10},{6,14},... | collective-permute-start | bytes 270344 | tf_op jit(solution)/shard_map/ppermute | solution.py:224
  38.2 14.0 %collective-permute-start.9 = (bf16[128,640]{1,0:T(8,128)(2,1)S(1)}, bf16[128,640]{1,0:T(8,128)(2,1)S(1)}, u32[]{:S(2)}, u32[]{:S(2)}) collective-permute-start(bf16[128,640]{1,0:T(8,128)(2,1)S(1)} %get-tuple-element.52), channel_id=1, source_target_pairs={{0,2},{2,0},{1,3},{3,1},{4,6},{6,4},{5,7},{7,5},{8,10},{10,8},{9,1... | collective-permute-start | bytes 491528 | tf_op jit(solution)/shard_map/ppermute | solution.py:224
  41.0 9.0 %collective-permute-start.7 = (bf16[32,1408]{1,0:T(8,128)(2,1)S(1)}, bf16[32,1408]{1,0:T(8,128)(2,1)S(1)}, u32[]{:S(2)}, u32[]{:S(2)}) collective-permute-start(bf16[32,1408]{1,0:T(8,128)(2,1)S(1)} %get-tuple-element.47), channel_id=1, source_target_pairs={{0,12},{4,8},{8,4},{12,0},{1,13},{5,9},{9,5},{13,1},{2,14},{6,10},... | collective-permute-start | bytes 270344 | tf_op jit(solution)/shard_map/ppermute | solution.py:224
  48.8 13.0 %collective-permute-start.17 = (bf16[128,640]{1,0:T(8,128)(2,1)S(1)}, bf16[128,640]{1,0:T(8,128)(2,1)S(1)}, u32[]{:S(2)}, u32[]{:S(2)}) collective-permute-start(bf16[128,640]{1,0:T(8,128)(2,1)S(1)} %get-tuple-element.59), channel_id=1, source_target_pairs={{0,2},{2,0},{1,3},{3,1},{4,6},{6,4},{5,7},{7,5},{8,10},{10,8},{9,1... | collective-permute-start | bytes 491528 | tf_op jit(solution)/shard_map/ppermute | solution.py:224
  50.9 2.7 %collective-permute-start.18 = (f32[32,640]{1,0:T(8,128)S(1)}, f32[32,640]{1,0:T(8,128)S(1)}, u32[]{:S(2)}, u32[]{:S(2)}) collective-permute-start(f32[32,640]{1,0:T(8,128)S(1)} %get-tuple-element.56), channel_id=1, source_target_pairs={{0,1},{1,0},{2,3},{3,2},{4,5},{5,4},{6,7},{7,6},{8,9},{9,8},{10,11... | collective-permute-start | bytes 245768 | tf_op jit(solution)/shard_map/ppermute | solution.py:224
  52.2 8.5 %collective-permute-start.10 = (bf16[128,640]{1,0:T(8,128)(2,1)S(1)}, bf16[128,640]{1,0:T(8,128)(2,1)S(1)}, u32[]{:S(2)}, u32[]{:S(2)}) collective-permute-start(bf16[128,640]{1,0:T(8,128)(2,1)S(1)} %add_convert_fusion.3), channel_id=1, source_target_pairs={{0,12},{4,8},{8,4},{12,0},{1,13},{5,9},{9,5},{13,1},{2,14},{6,10},... | collective-permute-start | bytes 491528 | tf_op jit(solution)/shard_map/ppermute | solution.py:224
  60.8 5.8 %collective-permute-start.13 = (bf16[128,640]{1,0:T(8,128)(2,1)S(1)}, bf16[128,640]{1,0:T(8,128)(2,1)S(1)}, u32[]{:S(2)}, u32[]{:S(2)}) collective-permute-start(bf16[128,640]{1,0:T(8,128)(2,1)S(1)} %get-tuple-element.58), channel_id=1, source_target_pairs={{0,2},{2,0},{1,3},{3,1},{4,6},{6,4},{5,7},{7,5},{8,10},{10,8},{9,1... | collective-permute-start | bytes 491528 | tf_op jit(solution)/shard_map/ppermute | solution.py:224

commit v3 on v2

--- a/solution.py
+++ b/solution.py
@@ -134,18 +134,22 @@
     return call(body, shapes, args, {0: SMEM, 1: SMEM}, scratch=scratch)
 
 
-def letters(place, card, mine, got, n):
+def chip_sums(place, card, mine, got, n):
     deep, half, rows = mine.shape[0] // n, mine.shape[1], card.shape[1]
+    top = n // 2
 
     def body(place_ref, card_ref, mine_ref, got_ref, *outs):
-        for s, out in enumerate(outs):
+        for s in range(n):
             at = pl.ds(pl.multiple_of((place_ref[0] ^ s) * deep, 16), deep)
-            total = mine_ref[at].astype(F32) + got_ref[at].astype(F32)
-            out[:, :half] = total.astype(BF16)
-            out[:, half:] = card_ref[...]
-
-    shapes = [array((deep, half + rows), BF16)] * n
-    return call(body, shapes, [place, card, mine, got], {0: SMEM})
+            total = (mine_ref[at].astype(F32) + got_ref[at].astype(F32)).astype(BF16)
+            if s < top:
+                outs[s][...] = total
+            else:
+                outs[top][:, (s - top) * half : (s - top + 1) * half] = total
+        outs[top][:, top * half :] = card_ref[...]
+
+    shapes = [array((deep, half), BF16)] * top + [array((deep, top * half + rows), BF16)]
+    return list(call(body, shapes, [place, card, mine, got], {0: SMEM}))
 
 
 def lift_up(owner_slot, core, place, cards, blocks, rank):
@@ -273,41 +277,52 @@
         w_chip = w_chip.reshape(tensors, chunk, -1)
         w_parts = [pick(w_chip, t ^ k) for k in range(tensors)]
 
-    parts, totals = [], []
+    parts, totals = {}, {}
 
     def product(s, *ready):
         made = multiply(after(blocks[s], *ready), w_parts, first)
         kept = made[0].astype(F32)
         for k in range(1, tensors):
             kept = kept + swap(made[k], "tensor", k).astype(F32)
-        parts.append(made)
-        totals.append(kept.astype(BF16))
-
-    product(0)
+        parts[s], totals[s] = made, kept.astype(BF16)
 
     down_t = down.transpose(1, 2, 0).reshape(adapters * rank, -1)
     up_t = up.reshape(adapters * rank, -1)
-    low = project(core, after(ids, *parts[0]), x, g, down_t, up_t, rank)
+    low = project(core, after(ids, w_other), x, g, down_t, up_t, rank)
     lows = [low] + [swap(low, "tensor", s) for s in range(1, tensors)]
 
-    product(1, low)
-    card, low_out, mine, away = lift_down(
-        owner_slot, core, after(ids, *parts[1]), x, lows, slots
-    )
-    got = swap(away, "seq", 1)
-
-    hand_on(range(top, n), mine)
-    for s in range(2, n - 1):
-        product(s, *parts[s - 1], mine, away)
-
-    sent = letters(place, card, mine, after(got, *parts[n - 2]), n)
-
-    product(n - 1, *parts[n - 2])
-
-    received = [sent[0]] + [swap(sent[s], "dp", s) for s in range(1, n)]
+    product(0, low)
+    card, low_out, mine, away = lift_down(owner_slot, core, ids, x, lows, slots)
     half = mine.shape[1]
-    cards = [v[:, half:] for v in received]
-    down_sum = sum(v[:, :half].astype(F32) for v in received)
+    got = swap(after(away, blocks[top]), "seq", 1)
+    *held, letter = chip_sums(place, card, mine, got, n)
+    cards = {0: card}
+
+    def post(bit, letter):
+        known = list(cards)
+        got = swap(letter, "dp", bit)
+        for s in range(bit):
+            total = held[s].astype(F32) + got[:, s * half : (s + 1) * half].astype(F32)
+            held[s] = total.astype(BF16) if bit > 1 else total
+        for i, s in enumerate(known):
+            at = bit * half + i * rows
+            cards[s ^ bit] = got[:, at : at + rows]
+
+    post(top, letter)
+    hand_on(range(top, n), low, *parts[0])
+    order = [*range(top, n - 1), *range(1, top)]
+    ready = [letter]
+    for s in order:
+        product(s, *ready)
+        ready = parts[s]
+    product(n - 1, *ready, totals[order[0]])
+    bit = top // 2
+    while bit:
+        letter = held[bit : 2 * bit] + [cards[s] for s in cards]
+        post(bit, after(jnp.concatenate(letter, axis=1), totals[n - 1]))
+        bit //= 2
+    cards = [after(cards[s], totals[n - 1]) for s in range(n)]
+    down_sum = after(held[0], totals[n - 1])
     all_ids = jnp.stack([v[rank : rank + cores] for v in cards]).astype(jnp.int32)
     counts = jnp.sum((all_ids.reshape(1, -1) == labels[:, None]).astype(F32), axis=1)
     weight = F32(n * cores * rows) / (F32(adapters) * counts)
@@ -318,13 +333,13 @@
     down_grad = down_sum.reshape(OWN_MAX, rank, half) * slot_weight[:, None, None]
     down_grad = down_grad.transpose(2, 0, 1)
 
-    back = [swap(v, "dp", s) if s else v for s, v in enumerate(totals)]
+    back = [swap(v, "dp", s) if s else v for s, v in sorted(totals.items())]
     span = n // tensors
     low_bits, high_bits = z % span, z // span
     pieces, offsets = [], []
     for r in range(span):
         choices = [back[r + k * span] for k in range(tensors)]
-        choices[0] = after(choices[0], *parts[n - 1])
+        choices[0] = after(choices[0], totals[n - 1])
         for k in range(tensors):
             piece = choose(choices, t ^ k ^ high_bits)
             pieces.append(swap(piece, "tensor", k) if k else piece)

time: 68.4 us -> 61.5 us (0.90)
  waiting for transfers between devices: 30.4 us -> 21.6 us
  local copies, waits for them, and re-layouts: 2.45 us -> 4.67 us
    ppermute x19 -> x18, waiting for transfers between devices: 30.4 us -> 21.6 us  [swap(): return lax.ppermute(value, axis, [(i, i ^ step) for i in range(size)])]
    unnamed x18 -> x22, local copies, waits for them, and re-layouts: 2.43 us -> 4.66 us
    ppermute x19 -> x18, starting transfers between devices: 22.5 us -> 22.3 us  [swap(): return lax.ppermute(value, axis, [(i, i ^ step) for i in range(size)])]
  transfers between devices with their start and end apart: 19 -> 18, of which waited for: 7 -> 9; matrix products, arithmetic and copies ran while one was open for 3% -> 3% of each run, Pallas kernels for 12% -> 13%
where the time goes in v3:
time: 61.5 us; the launch traced here: 61.3 us
  starting transfers between devices  22.3 us (36%)
  waiting for transfers between devices  21.6 us (35%)
  Pallas kernels  9.71 us (16%)
  local copies, waits for them, and re-layouts  4.67 us (8%)
  other arithmetic  2.13 us (3%)
  between operations  0.85 us (1%)
    ppermute x18, starting transfers between devices, swap(): return lax.ppermute(value, axis, [(i, i ^ step) for i in range(size)])  22.3 us
    ppermute x18, waiting for transfers between devices, swap(): return lax.ppermute(value, axis, [(i, i ^ step) for i in range(size)])  21.6 us
    pallas_call x10, Pallas kernels, call(): pl.pallas_call(body, out_shape=out_shape, in_specs=in_specs, out_specs=ou...  9.71 us
    unnamed x22, local copies, waits for them, and re-layouts  4.66 us
  transfers between devices with their start and end apart: 18, of which 9 were waited for; matrix products, arithmetic and copies ran while one was open for 3% of the time, Pallas kernels for 13%

profile of v3, /device:TPU:0, one launch (start us, length us, event | category | flops | bytes accessed | tf_op | source)
XLA Modules:
  0.0 61.3 jit_solution(3802150120630036189)
XLA Ops:
  0.6 0.5 collective-permute-start
  1.1 3.7 %collective-permute-start.2 = (bf16[128,1280]{1,0:T(8,128)(2,1)}, bf16[128,1280]{1,0:T(8,128)(2,1)S(1)}, u32[]{:S(2)}, u32[]{:S(2)}) collective-permute-start(bf16[128,1280]{1,0:T(8,128)(2,1)} %refs_4_.1), channel_id=1, source_target_pairs={{0,8},{4,12},{8,0},{12,4},{1,9},{5,13},{9,1},{13,5},{2,10},{6,14},... | collective-permute-start | bytes 983048 | tf_op jit(solution)/shard_map/ppermute | solution.py:228
  4.8 1.6 %collective-permute-start.4 = (bf16[128,1280]{1,0:T(8,128)(2,1)}, bf16[128,1280]{1,0:T(8,128)(2,1)S(1)}, u32[]{:S(2)}, u32[]{:S(2)}) collective-permute-start(bf16[128,1280]{1,0:T(8,128)(2,1)} %refs_4_.1), channel_id=1, source_target_pairs={{0,4},{4,0},{8,12},{12,8},{1,5},{5,1},{9,13},{13,9},{2,6},{6,2},{1... | collective-permute-start | bytes 983048 | tf_op jit(solution)/shard_map/ppermute | solution.py:228
  6.4 0.0 collective-permute-done.refs_3_
  6.4 1.1 %copy-done.2 = bf16[128,2560]{1,0:T(8,128)(2,1)S(1)} copy-done((bf16[128,2560]{1,0:T(8,128)(2,1)S(1)}, bf16[128,2560]{1,0:T(8,128)(2,1)}, u32[]{:S(2)}) %copy-start.2) | copy-done | bytes 655384
  7.5 1.0 %copy-done.4 = bf16[128,1280]{1,0:T(8,128)(2,1)S(1)} copy-done((bf16[128,1280]{1,0:T(8,128)(2,1)S(1)}, bf16[128,1280]{1,0:T(8,128)(2,1)}, u32[]{:S(2)}) %copy-start.4) | copy-done | bytes 327704
  8.5 1.0 %copy-done.6 = bf16[2560,4,16]{0,2,1:T(8,128)(2,1)S(1)} copy-done((bf16[2560,4,16]{0,2,1:T(8,128)(2,1)S(1)}, bf16[2560,4,16]{0,2,1:T(8,128)(2,1)}, u32[]{:S(2)}) %copy-start.6) | copy-done | bytes 327704
  9.4 0.9 %copy-done.8 = bf16[4,16,1280]{2,1,0:T(8,128)(2,1)S(1)} copy-done((bf16[4,16,1280]{2,1,0:T(8,128)(2,1)S(1)}, bf16[4,16,1280]{2,1,0:T(8,128)(2,1)}, u32[]{:S(2)}) %copy-start.8) | copy-done | bytes 163864
  10.3 0.7 %copy-done.9 = s32[256]{0:T(256)S(1)} copy-done((s32[256]{0:T(256)S(1)}, s32[256]{0:T(256)}, u32[]{:S(2)}) %copy-start.9) | copy-done | bytes 1048
  11.0 0.5 shard_map.94.rest_0_
  11.5 1.6 %collective-permute-start.1 = (f32[32,128]{1,0:T(8,128)S(1)}, f32[32,128]{1,0:T(8,128)S(1)}, u32[]{:S(2)}, u32[]{:S(2)}) collective-permute-start(f32[32,128]{1,0:T(8,128)S(1)} %shard_map.94.rest_0_), channel_id=1, source_target_pairs={{0,2},{2,0},{1,3},{3,1},{4,6},{6,4},{5,7},{7,5},{8,10},{10,8},{9,1... | collective-permute-start | bytes 49160 | tf_op jit(solution)/shard_map/ppermute | solution.py:228
  13.1 0.0 copy-done.1
  13.1 1.1 %shard_map.96 = (bf16[128,640]{1,0:T(8,128)(2,1)S(1)}, bf16[128,640]{1,0:T(8,128)(2,1)S(1)}) custom-call(s32[1]{0:T(128)} %bitcast.5.refs_0_, bf16[128,1280]{1,0:T(8,128)(2,1)S(1)} %copy-done.4, bf16[640,1280]{1,0:T(8,128)(2,1)S(1)} %copy-done.1, bf16[640,1280]{1,0:T(8,128)(2,1)S(1)} %collective-permute-done.refs_3_), custom_call_target="tpu_custom_call" | custom-call | flops 8589934592 | bytes 33554432 | tf_op jit(solution)/shard_map/pallas_call | solution.py:33
  14.2 0.9 %collective-permute-start.15 = (bf16[128,640]{1,0:T(8,128)(2,1)S(1)}, bf16[128,640]{1,0:T(8,128)(2,1)S(1)}, u32[]{:S(2)}, u32[]{:S(2)}) collective-permute-start(bf16[128,640]{1,0:T(8,128)(2,1)S(1)} %get-tuple-element.39), channel_id=1, source_target_pairs={{0,2},{2,0},{1,3},{3,1},{4,6},{6,4},{5,7},{7,5},{8,10},{10,8},{9,1... | collective-permute-start | bytes 491528 | tf_op jit(solution)/shard_map/ppermute | solution.py:228
  15.1 0.2 collective-permute-done.1.rest_1_
  15.3 0.0 copy-done
  15.3 0.0 copy-done.3
  15.3 0.9 %shard_map.95 = (bf16[32,128]{1,0:T(8,128)(2,1)S(1)}, bf16[16,128]{1,0:T(8,128)(2,1)S(1)}, bf16[128,1280]{1,0:T(8,128)(2,1)S(1)}, bf16[128,1280]{1,0:T(8,128)(2,1)S(1)}) custom-call(s32[4]{0:T(128)S(1)} %copy-done, s32[1]{0:T(128)} %bitcast.core_ref, s32[2,128]{1,0:T(2,128)S(1)} %bitcast.31, bf16[128,2560]{1,0:T(8,128)(2,1)S(1)} %copy-done.3, ...), custom_call_target="tpu_custom_call" | custom-call | flops 8589934592 | bytes 33554432 | tf_op jit(solution)/shard_map/pallas_call | solution.py:33
  16.2 4.3 %collective-permute-done.2.refs_1_.refs_6_ = bf16[128,1280]{1,0:T(8,128)(2,1)S(1)} collective-permute-done((bf16[128,1280]{1,0:T(8,128)(2,1)}, bf16[128,1280]{1,0:T(8,128)(2,1)S(1)}, u32[]{:S(2)}, u32[]{:S(2)}) %collective-permute-start.2) | collective-permute-done | bytes 327712 | tf_op jit(solution)/shard_map/ppermute | solution.py:228
  20.5 0.0 collective-permute-start.5
  20.5 0.8 %collective-permute-start.3 = (bf16[128,1280]{1,0:T(8,128)(2,1)S(1)}, bf16[128,1280]{1,0:T(8,128)(2,1)S(1)}, u32[]{:S(2)}, u32[]{:S(2)}) collective-permute-start(bf16[128,1280]{1,0:T(8,128)(2,1)S(1)} %collective-permute-done.2.refs_1_.refs_6_), channel_id=1, source_target_pairs={{0,4},{4,0},{8,12},{12,8},{1,5},{5,1},{9,13},{13,9},{2,6},{6,2},{1... | collective-permute-start | bytes 983048 | tf_op jit(solution)/shard_map/ppermute | solution.py:228
  21.3 0.0 collective-permute-done.15
  21.3 0.8 %collective-permute-done.5.got_ref = bf16[128,1280]{1,0:T(8,128)(2,1)S(1)} collective-permute-done((bf16[128,1280]{1,0:T(8,128)(2,1)S(1)}, bf16[128,1280]{1,0:T(8,128)(2,1)S(1)}, u32[]{:S(2)}, u32[]{:S(2)}) %collective-permute-start.5) | collective-permute-done | bytes 327712 | tf_op jit(solution)/shard_map/ppermute | solution.py:228
  22.1 0.1 shard_map.97
  22.2 2.6 %collective-permute-start.8 = (bf16[32,2688]{1,0:T(8,128)(2,1)S(1)}, bf16[32,2688]{1,0:T(8,128)(2,1)S(1)}, u32[]{:S(2)}, u32[]{:S(2)}) collective-permute-start(bf16[32,2688]{1,0:T(8,128)(2,1)S(1)} %get-tuple-element.44), channel_id=1, source_target_pairs={{0,8},{4,12},{8,0},{12,4},{1,9},{5,13},{9,1},{13,5},{2,10},{6,14},... | collective-permute-start | bytes 516104 | tf_op jit(solution)/shard_map/ppermute | solution.py:228
  24.8 1.1 %shard_map.98 = (bf16[128,640]{1,0:T(8,128)(2,1)S(1)}, bf16[128,640]{1,0:T(8,128)(2,1)S(1)}) custom-call(s32[1]{0:T(128)} %bitcast.5.refs_0_, bf16[128,1280]{1,0:T(8,128)(2,1)S(1)} %collective-permute-done.2.refs_1_.refs_6_, bf16[640,1280]{1,0:T(8,128)(2,1)S(1)} %copy-done.1, bf16[640,1280]{1,0:T(8,128)(2,1)S(1)} %collective-permute-done.refs_3_), custom_call_target="tpu_custom_call" | custom-call | flops 8589934592 | bytes 33554432 | tf_op jit(solution)/shard_map/pallas_call | solution.py:33
  25.8 1.6 %collective-permute-start.6 = (bf16[128,640]{1,0:T(8,128)(2,1)S(1)}, bf16[128,640]{1,0:T(8,128)(2,1)S(1)}, u32[]{:S(2)}, u32[]{:S(2)}) collective-permute-start(bf16[128,640]{1,0:T(8,128)(2,1)S(1)} %get-tuple-element.47), channel_id=1, source_target_pairs={{0,2},{2,0},{1,3},{3,1},{4,6},{6,4},{5,7},{7,5},{8,10},{10,8},{9,1... | collective-permute-start | bytes 491528 | tf_op jit(solution)/shard_map/ppermute | solution.py:228
  27.4 0.0 collective-permute-done.4.refs_1_.refs_5_
  27.4 1.1 %shard_map.99 = (bf16[128,640]{1,0:T(8,128)(2,1)S(1)}, bf16[128,640]{1,0:T(8,128)(2,1)S(1)}) custom-call(s32[1]{0:T(128)} %bitcast.5.refs_0_, bf16[128,1280]{1,0:T(8,128)(2,1)S(1)} %collective-permute-done.4.refs_1_.refs_5_, bf16[640,1280]{1,0:T(8,128)(2,1)S(1)} %copy-done.1, bf16[640,1280]{1,0:T(8,128)(2,1)S(1)} %collective-permute-done.refs_3_), custom_call_target="tpu_custom_call" | custom-call | flops 8589934592 | bytes 33554432 | tf_op jit(solution)/shard_map/pallas_call | solution.py:33
  28.5 0.6 collective-permute-start.11
  29.1 3.9 %collective-permute-done.6 = bf16[128,640]{1,0:T(8,128)(2,1)S(1)} collective-permute-done((bf16[128,640]{1,0:T(8,128)(2,1)S(1)}, bf16[128,640]{1,0:T(8,128)(2,1)S(1)}, u32[]{:S(2)}, u32[]{:S(2)}) %collective-permute-start.6) | collective-permute-done | bytes 163872 | tf_op jit(solution)/shard_map/ppermute | solution.py:228
  33.0 0.4 collective-permute-start.14
  33.4 0.9 %collective-permute-done.3.refs_1_.refs_7_ = bf16[128,1280]{1,0:T(8,128)(2,1)S(1)} collective-permute-done((bf16[128,1280]{1,0:T(8,128)(2,1)S(1)}, bf16[128,1280]{1,0:T(8,128)(2,1)S(1)}, u32[]{:S(2)}, u32[]{:S(2)}) %collective-permute-start.3) | collective-permute-done | bytes 327712 | tf_op jit(solution)/shard_map/ppermute | solution.py:228
  34.3 1.1 %shard_map.100 = (bf16[128,640]{1,0:T(8,128)(2,1)S(1)}, bf16[128,640]{1,0:T(8,128)(2,1)S(1)}) custom-call(s32[1]{0:T(128)} %bitcast.5.refs_0_, bf16[128,1280]{1,0:T(8,128)(2,1)S(1)} %collective-permute-done.3.refs_1_.refs_7_, bf16[640,1280]{1,0:T(8,128)(2,1)S(1)} %copy-done.1, bf16[640,1280]{1,0:T(8,128)(2,1)S(1)} %collective-permute-done.refs_3_), custom_call_target="tpu_custom_call" | custom-call | flops 8589934592 | bytes 33554432 | tf_op jit(solution)/shard_map/pallas_call | solution.py:33
  35.4 0.0 copy-start.5
  35.4 1.6 %collective-permute-start.7 = (bf16[128,640]{1,0:T(8,128)(2,1)S(1)}, bf16[128,640]{1,0:T(8,128)(2,1)S(1)}, u32[]{:S(2)}, u32[]{:S(2)}) collective-permute-start(bf16[128,640]{1,0:T(8,128)(2,1)S(1)} %get-tuple-element.53), channel_id=1, source_target_pairs={{0,2},{2,0},{1,3},{3,1},{4,6},{6,4},{5,7},{7,5},{8,10},{10,8},{9,1... | collective-permute-start | bytes 491528 | tf_op jit(solution)/shard_map/ppermute | solution.py:228
  37.0 0.0 collective-permute-done.11
  37.1 0.3 collective-permute-start.12
  37.4 0.0 collective-permute-done.8
  37.4 3.8 %collective-permute-done.7 = bf16[128,640]{1,0:T(8,128)(2,1)S(1)} collective-permute-done((bf16[128,640]{1,0:T(8,128)(2,1)S(1)}, bf16[128,640]{1,0:T(8,128)(2,1)S(1)}, u32[]{:S(2)}, u32[]{:S(2)}) %collective-permute-start.7) | collective-permute-done | bytes 163872 | tf_op jit(solution)/shard_map/ppermute | solution.py:228
  41.3 3.6 %collective-permute-start.10 = (bf16[128,640]{1,0:T(8,128)(2,1)S(1)}, bf16[128,640]{1,0:T(8,128)(2,1)S(1)}, u32[]{:S(2)}, u32[]{:S(2)}) collective-permute-start(bf16[128,640]{1,0:T(8,128)(2,1)S(1)} %add_convert_fusion.2), channel_id=1, source_target_pairs={{0,12},{4,8},{8,4},{12,0},{1,13},{5,9},{9,5},{13,1},{2,14},{6,10},... | collective-permute-start | bytes 491528 | tf_op jit(solution)/shard_map/ppermute | solution.py:228
  44.9 0.0 collective-permute-start.9
  44.9 0.0 collective-permute-done.14
  44.9 1.6 %collective-permute-start.16 = (bf16[128,640]{1,0:T(8,128)(2,1)S(1)}, bf16[128,640]{1,0:T(8,128)(2,1)S(1)}, u32[]{:S(2)}, u32[]{:S(2)}) collective-permute-start(bf16[128,640]{1,0:T(8,128)(2,1)S(1)} %get-tuple-element.69), channel_id=1, source_target_pairs={{0,2},{2,0},{1,3},{3,1},{4,6},{6,4},{5,7},{7,5},{8,10},{10,8},{9,1... | collective-permute-start | bytes 491528 | tf_op jit(solution)/shard_map/ppermute | solution.py:228
  46.5 2.9 %collective-permute-done.12 = bf16[128,640]{1,0:T(8,128)(2,1)S(1)} collective-permute-done((bf16[128,640]{1,0:T(8,128)(2,1)S(1)}, bf16[128,640]{1,0:T(8,128)(2,1)S(1)}, u32[]{:S(2)}, u32[]{:S(2)}) %collective-permute-start.12) | collective-permute-done | bytes 163872 | tf_op jit(solution)/shard_map/ppermute | solution.py:228
  49.3 1.6 %collective-permute-done.9 = bf16[32,1536]{1,0:T(8,128)(2,1)S(1)} collective-permute-done((bf16[32,1536]{1,0:T(8,128)(2,1)S(1)}, bf16[32,1536]{1,0:T(8,128)(2,1)S(1)}, u32[]{:S(2)}, u32[]{:S(2)}) %collective-permute-start.9) | collective-permute-done | bytes 98336 | tf_op jit(solution)/shard_map/ppermute | solution.py:228
  51.0 0.1 convert_reduce_fusion
  51.2 0.2 fusion
  51.3 0.0 copy-done.5
  51.4 0.0 copy-start.7
  51.4 0.0 copy-start.10
  51.4 0.9 %shard_map.103 = (f32[32,640]{1,0:T(8,128)S(1)}, f32[32,640]{1,0:T(8,128)S(1)}) custom-call(s32[4]{0:T(128)S(1)} %copy-done, s32[1]{0:T(128)} %bitcast.core_ref, s32[1]{0:T(128)} %bitcast.6.place_ref, bf16[32,128]{1,0:T(8,128)(2,1)S(1)} %get-tuple-element.54.card_ref.refs_0_, bf16[32,128]{1,0:T(8,128)(2,1)S(1)} %get-tuple-element.57.refs_1_, ...), custom_call_target="tpu_custom_call" | custom-call | flops 8589934592 | bytes 33554432 | tf_op jit(solution)/shard_map/pallas_call | solution.py:33
  52.3 0.1 collective-permute-start.17
  52.3 0.7 %multiply_bitcast_fusion = f32[1280,2,16]{0,2,1:T(8,128)} fusion(f32[2,16,1280]{2,1,0:T(8,128)S(1)} %bitcast.34, f32[2]{0:T(128)S(1)} %broadcast_multiply_fusion.1), kind=kLoop, calls=%fused_computation.4 | loop fusion | flops 40960 | bytes 327688 | tf_op jit(solution)/shard_map/transpose | solution.py:334
  53.1 0.0 collective-permute-done.10
  53.1 1.0 %collective-permute-start.13 = (bf16[128,640]{1,0:T(8,128)(2,1)S(1)}, bf16[128,640]{1,0:T(8,128)(2,1)S(1)}, u32[]{:S(2)}, u32[]{:S(2)}) collective-permute-start(bf16[128,640]{1,0:T(8,128)(2,1)S(1)} %get-tuple-element.68), channel_id=1, source_target_pairs={{0,2},{2,0},{1,3},{3,1},{4,6},{6,4},{5,7},{7,5},{8,10},{10,8},{9,1... | collective-permute-start | bytes 491528 | tf_op jit(solution)/shard_map/ppermute | solution.py:228
  54.2 0.0 collective-permute-done.16.refs_7_
  54.2 0.0 copy-done.7
  54.2 0.0 copy-done.10
  54.2 1.6 %shard_map.101.refs_5_ = bf16[128,2560]{1,0:T(8,128)(2,1)} custom-call(f32[4]{0:T(128)S(1)} %multiply_divide_fusion.weight_ref, s32[1]{0:T(128)} %bitcast.core_ref, s32[1]{0:T(128)} %bitcast.13.refs_0_, s32[1]{0:T(128)} %bitcast.14.refs_1_, s32[1]{0:T(128)} %bitcast.15.refs_2_, s32[2,128]{1,0:T(2,128)S(1)} %bitcast.32, ...), custom_call_target="tpu_custom_call" | custom-call | flops 8589934592 | bytes 33554432 | tf_op jit(solution)/shard_map/pallas_call | solution.py:33
  55.8 0.0 collective-permute-done.17
  55.8 0.7 %broadcast_multiply_fusion = f32[2,16,640]{2,1,0:T(8,128)} fusion(f32[2,16,640]{2,1,0:T(8,128)S(1)} %bitcast.35, f32[2]{0:T(128)S(1)} %broadcast_multiply_fusion.1), kind=kLoop, calls=%fused_computation.13 | loop fusion | flops 20480 | bytes 163848 | tf_op jit(solution)/shard_map/mul | solution.py:366
  56.5 3.3 %collective-permute-done.13.refs_4_ = bf16[128,640]{1,0:T(8,128)(2,1)S(1)} collective-permute-done((bf16[128,640]{1,0:T(8,128)(2,1)S(1)}, bf16[128,640]{1,0:T(8,128)(2,1)S(1)}, u32[]{:S(2)}, u32[]{:S(2)}) %collective-permute-start.13) | collective-permute-done | bytes 163872 | tf_op jit(solution)/shard_map/ppermute | solution.py:228
  59.8 1.5 %shard_map.102 = bf16[128,2560]{1,0:T(8,128)(2,1)} custom-call(f32[4]{0:T(128)S(1)} %multiply_divide_fusion.weight_ref, s32[1]{0:T(128)} %bitcast.core_ref, s32[1]{0:T(128)} %bitcast.12.refs_0_, s32[2,128]{1,0:T(2,128)S(1)} %bitcast.33, bf16[16,128]{1,0:T(8,128)(2,1)S(1)} %get-tuple-element.60.refs_4_.refs_2_, ...), custom_call_target="tpu_custom_call", output_to_operand_aliasing={{}: (7, {})} | custom-call | flops 8589934592 | bytes 33554432 | tf_op jit(solution)/shard_map/pallas_call | solution.py:33
  (27 shorter events, 0.4 us)
Async XLA Ops:
  0.6 5.8 %collective-permute-start = (bf16[640,1280]{1,0:T(8,128)(2,1)}, bf16[640,1280]{1,0:T(8,128)(2,1)S(1)}, u32[]{:S(2)}, u32[]{:S(2)}) collective-permute-start(bf16[640,1280]{1,0:T(8,128)(2,1)} %refs_2_.7), channel_id=1, source_target_pairs={{0,1},{1,0},{2,3},{3,2},{4,5},{5,4},{6,7},{7,6},{8,9},{9,8},{10,11... | collective-permute-start | bytes 4915208 | tf_op jit(solution)/shard_map/ppermute | solution.py:228
  1.1 19.3 %collective-permute-start.2 = (bf16[128,1280]{1,0:T(8,128)(2,1)}, bf16[128,1280]{1,0:T(8,128)(2,1)S(1)}, u32[]{:S(2)}, u32[]{:S(2)}) collective-permute-start(bf16[128,1280]{1,0:T(8,128)(2,1)} %refs_4_.1), channel_id=1, source_target_pairs={{0,8},{4,12},{8,0},{12,4},{1,9},{5,13},{9,1},{13,5},{2,10},{6,14},... | collective-permute-start | bytes 983048 | tf_op jit(solution)/shard_map/ppermute | solution.py:228
  4.8 22.6 %collective-permute-start.4 = (bf16[128,1280]{1,0:T(8,128)(2,1)}, bf16[128,1280]{1,0:T(8,128)(2,1)S(1)}, u32[]{:S(2)}, u32[]{:S(2)}) collective-permute-start(bf16[128,1280]{1,0:T(8,128)(2,1)} %refs_4_.1), channel_id=1, source_target_pairs={{0,4},{4,0},{8,12},{12,8},{1,5},{5,1},{9,13},{13,9},{2,6},{6,2},{1... | collective-permute-start | bytes 983048 | tf_op jit(solution)/shard_map/ppermute | solution.py:228
  6.4 1.1 %copy-start.2 = (bf16[128,2560]{1,0:T(8,128)(2,1)S(1)}, bf16[128,2560]{1,0:T(8,128)(2,1)}, u32[]{:S(2)}) copy-start(bf16[128,2560]{1,0:T(8,128)(2,1)} %x_ref.3) | copy-start | bytes 1966084
  7.5 1.0 %copy-start.4 = (bf16[128,1280]{1,0:T(8,128)(2,1)S(1)}, bf16[128,1280]{1,0:T(8,128)(2,1)}, u32[]{:S(2)}) copy-start(bf16[128,1280]{1,0:T(8,128)(2,1)} %refs_4_.1) | copy-start | bytes 983044
  8.5 1.0 %copy-start.6 = (bf16[2560,4,16]{0,2,1:T(8,128)(2,1)S(1)}, bf16[2560,4,16]{0,2,1:T(8,128)(2,1)}, u32[]{:S(2)}) copy-start(bf16[2560,4,16]{0,2,1:T(8,128)(2,1)} %param.12) | copy-start | bytes 983044
  9.4 0.9 %copy-start.8 = (bf16[4,16,1280]{2,1,0:T(8,128)(2,1)S(1)}, bf16[4,16,1280]{2,1,0:T(8,128)(2,1)}, u32[]{:S(2)}) copy-start(bf16[4,16,1280]{2,1,0:T(8,128)(2,1)} %param.13) | copy-start | bytes 491524
  10.3 0.7 %copy-start.9 = (s32[256]{0:T(256)S(1)}, s32[256]{0:T(256)}, u32[]{:S(2)}) copy-start(s32[256]{0:T(256)} %param.9) | copy-start | bytes 3076
  11.0 2.0 %copy-start.1 = (bf16[640,1280]{1,0:T(8,128)(2,1)S(1)}, bf16[640,1280]{1,0:T(8,128)(2,1)}, u32[]{:S(2)}) copy-start(bf16[640,1280]{1,0:T(8,128)(2,1)} %refs_2_.7) | copy-start | bytes 4915204
  11.5 3.8 %collective-permute-start.1 = (f32[32,128]{1,0:T(8,128)S(1)}, f32[32,128]{1,0:T(8,128)S(1)}, u32[]{:S(2)}, u32[]{:S(2)}) collective-permute-start(f32[32,128]{1,0:T(8,128)S(1)} %shard_map.94.rest_0_), channel_id=1, source_target_pairs={{0,2},{2,0},{1,3},{3,1},{4,6},{6,4},{5,7},{7,5},{8,10},{10,8},{9,1... | collective-permute-start | bytes 49160 | tf_op jit(solution)/shard_map/ppermute | solution.py:228
  13.1 2.2 %copy-start = (s32[4]{0:T(128)S(1)}, s32[4]{0:T(128)}, u32[]{:S(2)}) copy-start(s32[4]{0:T(128)} %slot_ref.3) | copy-start | bytes 52
  13.1 2.2 %copy-start.3 = (bf16[128,2560]{1,0:T(8,128)(2,1)S(1)}, bf16[128,2560]{1,0:T(8,128)(2,1)}, u32[]{:S(2)}) copy-start(bf16[128,2560]{1,0:T(8,128)(2,1)} %x_ref.3) | copy-start | bytes 1966084
  14.2 7.1 %collective-permute-start.15 = (bf16[128,640]{1,0:T(8,128)(2,1)S(1)}, bf16[128,640]{1,0:T(8,128)(2,1)S(1)}, u32[]{:S(2)}, u32[]{:S(2)}) collective-permute-start(bf16[128,640]{1,0:T(8,128)(2,1)S(1)} %get-tuple-element.39), channel_id=1, source_target_pairs={{0,2},{2,0},{1,3},{3,1},{4,6},{6,4},{5,7},{7,5},{8,10},{10,8},{9,1... | collective-permute-start | bytes 491528 | tf_op jit(solution)/shard_map/ppermute | solution.py:228
  20.5 1.6 %collective-permute-start.5 = (bf16[128,1280]{1,0:T(8,128)(2,1)S(1)}, bf16[128,1280]{1,0:T(8,128)(2,1)S(1)}, u32[]{:S(2)}, u32[]{:S(2)}) collective-permute-start(bf16[128,1280]{1,0:T(8,128)(2,1)S(1)} %get-tuple-element.43), channel_id=1, source_target_pairs={{0,1},{1,0},{2,3},{3,2},{4,5},{5,4},{6,7},{7,6},{8,9},{9,8},{10,11... | collective-permute-start | bytes 983048 | tf_op jit(solution)/shard_map/ppermute | solution.py:228
  20.5 13.8 %collective-permute-start.3 = (bf16[128,1280]{1,0:T(8,128)(2,1)S(1)}, bf16[128,1280]{1,0:T(8,128)(2,1)S(1)}, u32[]{:S(2)}, u32[]{:S(2)}) collective-permute-start(bf16[128,1280]{1,0:T(8,128)(2,1)S(1)} %collective-permute-done.2.refs_1_.refs_6_), channel_id=1, source_target_pairs={{0,4},{4,0},{8,12},{12,8},{1,5},{5,1},{9,13},{13,9},{2,6},{6,2},{1... | collective-permute-start | bytes 983048 | tf_op jit(solution)/shard_map/ppermute | solution.py:228
  22.2 15.2 %collective-permute-start.8 = (bf16[32,2688]{1,0:T(8,128)(2,1)S(1)}, bf16[32,2688]{1,0:T(8,128)(2,1)S(1)}, u32[]{:S(2)}, u32[]{:S(2)}) collective-permute-start(bf16[32,2688]{1,0:T(8,128)(2,1)S(1)} %get-tuple-element.44), channel_id=1, source_target_pairs={{0,8},{4,12},{8,0},{12,4},{1,9},{5,13},{9,1},{13,5},{2,10},{6,14},... | collective-permute-start | bytes 516104 | tf_op jit(solution)/shard_map/ppermute | solution.py:228
  25.8 7.1 %collective-permute-start.6 = (bf16[128,640]{1,0:T(8,128)(2,1)S(1)}, bf16[128,640]{1,0:T(8,128)(2,1)S(1)}, u32[]{:S(2)}, u32[]{:S(2)}) collective-permute-start(bf16[128,640]{1,0:T(8,128)(2,1)S(1)} %get-tuple-element.47), channel_id=1, source_target_pairs={{0,2},{2,0},{1,3},{3,1},{4,6},{6,4},{5,7},{7,5},{8,10},{10,8},{9,1... | collective-permute-start | bytes 491528 | tf_op jit(solution)/shard_map/ppermute | solution.py:228
  28.5 8.5 %collective-permute-start.11 = (bf16[128,640]{1,0:T(8,128)(2,1)S(1)}, bf16[128,640]{1,0:T(8,128)(2,1)S(1)}, u32[]{:S(2)}, u32[]{:S(2)}) collective-permute-start(bf16[128,640]{1,0:T(8,128)(2,1)S(1)} %get-tuple-element.50), channel_id=1, source_target_pairs={{0,2},{2,0},{1,3},{3,1},{4,6},{6,4},{5,7},{7,5},{8,10},{10,8},{9,1... | collective-permute-start | bytes 491528 | tf_op jit(solution)/shard_map/ppermute | solution.py:228
  33.0 11.8 %collective-permute-start.14 = (bf16[128,640]{1,0:T(8,128)(2,1)S(1)}, bf16[128,640]{1,0:T(8,128)(2,1)S(1)}, u32[]{:S(2)}, u32[]{:S(2)}) collective-permute-start(bf16[128,640]{1,0:T(8,128)(2,1)S(1)} %add_convert_fusion.3), channel_id=1, source_target_pairs={{0,8},{4,12},{8,0},{12,4},{1,9},{5,13},{9,1},{13,5},{2,10},{6,14},... | collective-permute-start | bytes 491528 | tf_op jit(solution)/shard_map/ppermute | solution.py:228
  35.4 16.0 %copy-start.5 = (bf16[128,1280]{1,0:T(8,128)(2,1)S(1)}, bf16[128,1280]{1,0:T(8,128)(2,1)}, u32[]{:S(2)}) copy-start(bf16[128,1280]{1,0:T(8,128)(2,1)} %refs_4_.1) | copy-start | bytes 983044
  35.4 5.9 %collective-permute-start.7 = (bf16[128,640]{1,0:T(8,128)(2,1)S(1)}, bf16[128,640]{1,0:T(8,128)(2,1)S(1)}, u32[]{:S(2)}, u32[]{:S(2)}) collective-permute-start(bf16[128,640]{1,0:T(8,128)(2,1)S(1)} %get-tuple-element.53), channel_id=1, source_target_pairs={{0,2},{2,0},{1,3},{3,1},{4,6},{6,4},{5,7},{7,5},{8,10},{10,8},{9,1... | collective-permute-start | bytes 491528 | tf_op jit(solution)/shard_map/ppermute | solution.py:228
  37.1 12.3 %collective-permute-start.12 = (bf16[128,640]{1,0:T(8,128)(2,1)S(1)}, bf16[128,640]{1,0:T(8,128)(2,1)S(1)}, u32[]{:S(2)}, u32[]{:S(2)}) collective-permute-start(bf16[128,640]{1,0:T(8,128)(2,1)S(1)} %add_convert_fusion.1), channel_id=1, source_target_pairs={{0,4},{4,0},{8,12},{12,8},{1,5},{5,1},{9,13},{13,9},{2,6},{6,2},{1... | collective-permute-start | bytes 491528 | tf_op jit(solution)/shard_map/ppermute | solution.py:228
  41.3 11.8 %collective-permute-start.10 = (bf16[128,640]{1,0:T(8,128)(2,1)S(1)}, bf16[128,640]{1,0:T(8,128)(2,1)S(1)}, u32[]{:S(2)}, u32[]{:S(2)}) collective-permute-start(bf16[128,640]{1,0:T(8,128)(2,1)S(1)} %add_convert_fusion.2), channel_id=1, source_target_pairs={{0,12},{4,8},{8,4},{12,0},{1,13},{5,9},{9,5},{13,1},{2,14},{6,10},... | collective-permute-start | bytes 491528 | tf_op jit(solution)/shard_map/ppermute | solution.py:228
  44.9 6.1 %collective-permute-start.9 = (bf16[32,1536]{1,0:T(8,128)(2,1)S(1)}, bf16[32,1536]{1,0:T(8,128)(2,1)S(1)}, u32[]{:S(2)}, u32[]{:S(2)}) collective-permute-start(bf16[32,1536]{1,0:T(8,128)(2,1)S(1)} %pad_maximum_fusion), channel_id=1, source_target_pairs={{0,4},{4,0},{8,12},{12,8},{1,5},{5,1},{9,13},{13,9},{2,6},{6,2},{1... | collective-permute-start | bytes 294920 | tf_op jit(solution)/shard_map/ppermute | solution.py:228
  44.9 9.3 %collective-permute-start.16 = (bf16[128,640]{1,0:T(8,128)(2,1)S(1)}, bf16[128,640]{1,0:T(8,128)(2,1)S(1)}, u32[]{:S(2)}, u32[]{:S(2)}) collective-permute-start(bf16[128,640]{1,0:T(8,128)(2,1)S(1)} %get-tuple-element.69), channel_id=1, source_target_pairs={{0,2},{2,0},{1,3},{3,1},{4,6},{6,4},{5,7},{7,5},{8,10},{10,8},{9,1... | collective-permute-start | bytes 491528 | tf_op jit(solution)/shard_map/ppermute | solution.py:228
  51.4 2.8 %copy-start.7 = (bf16[2560,4,16]{0,2,1:T(8,128)(2,1)S(1)}, bf16[2560,4,16]{0,2,1:T(8,128)(2,1)}, u32[]{:S(2)}) copy-start(bf16[2560,4,16]{0,2,1:T(8,128)(2,1)} %param.12) | copy-start | bytes 983044
  51.4 2.8 %copy-start.10 = (s32[256]{0:T(256)S(1)}, s32[256]{0:T(256)}, u32[]{:S(2)}) copy-start(s32[256]{0:T(256)} %param.9) | copy-start | bytes 3076
  52.3 3.5 %collective-permute-start.17 = (f32[32,640]{1,0:T(8,128)S(1)}, f32[32,640]{1,0:T(8,128)S(1)}, u32[]{:S(2)}, u32[]{:S(2)}) collective-permute-start(f32[32,640]{1,0:T(8,128)S(1)} %get-tuple-element.66), channel_id=1, source_target_pairs={{0,1},{1,0},{2,3},{3,2},{4,5},{5,4},{6,7},{7,6},{8,9},{9,8},{10,11... | collective-permute-start | bytes 245768 | tf_op jit(solution)/shard_map/ppermute | solution.py:228
  53.1 6.7 %collective-permute-start.13 = (bf16[128,640]{1,0:T(8,128)(2,1)S(1)}, bf16[128,640]{1,0:T(8,128)(2,1)S(1)}, u32[]{:S(2)}, u32[]{:S(2)}) collective-permute-start(bf16[128,640]{1,0:T(8,128)(2,1)S(1)} %get-tuple-element.68), channel_id=1, source_target_pairs={{0,2},{2,0},{1,3},{3,1},{4,6},{6,4},{5,7},{7,5},{8,10},{10,8},{9,1... | collective-permute-start | bytes 491528 | tf_op jit(solution)/shard_map/ppermute | solution.py:228

commit v4 on v3

--- a/solution.py
+++ b/solution.py
@@ -6,6 +6,7 @@
 from jax.sharding import PartitionSpec as P
 
 OWN_MAX = 2
+CUTS = 2
 ADAPTER_SCALE = 2.0
 F32 = jnp.float32
 BF16 = jnp.bfloat16
@@ -50,8 +51,10 @@
     return scalar.reshape(1)
 
 
-def multiply(piece, w_parts, first=None):
+def multiply(piece, w_parts, first=None, chosen=None, cuts=1):
     parts = len(w_parts)
+    chosen = range(parts) if chosen is None else chosen
+    rows = piece.shape[0] // cuts
 
     def body(*refs):
         if first is None:
@@ -59,8 +62,10 @@
         piece_ref, ws, outs = refs[1], refs[2 : 2 + parts], refs[2 + parts :]
 
         def work(order):
-            for k in range(parts):
-                outs[k][...] = dot_last(piece_ref[...], ws[order[k]][...]).astype(BF16)
+            for i, k in enumerate(chosen):
+                value = dot_last(piece_ref[...], ws[order[k]][...]).astype(BF16)
+                for j in range(cuts):
+                    outs[i * cuts + j][...] = value[j * rows : (j + 1) * rows]
 
         if first is None:
             work(range(parts))
@@ -68,7 +73,7 @@
             pl.when(refs[0][0] == 0)(lambda: work((0, 1)))
             pl.when(refs[0][0] == 1)(lambda: work((1, 0)))
 
-    shapes = [array((piece.shape[0], w.shape[0]), BF16) for w in w_parts]
+    shapes = [array((rows, w_parts[k].shape[0]), BF16) for k in chosen for _ in range(cuts)]
     head = [] if first is None else [first]
     return list(call(body, shapes, [*head, piece, *w_parts], {i: SMEM for i in range(len(head))}))
 
@@ -184,29 +189,32 @@
     return out
 
 
-def finish(weight, core, offsets, ids, low_out, down_t, pieces, into=None):
+def finish(weight, core, ids, low_out, down_t, pieces, offsets, starts, into=None):
     rows, width = ids.shape[1], down_t.shape[1]
     rank = low_out.shape[0]
-    adapters, chunk, count = weight.shape[0], pieces[0].shape[1], len(pieces)
+    adapters, count = weight.shape[0], len(pieces)
 
     def body(weight_ref, core_ref, *refs):
         offset_refs, (ids_ref, low_ref, down_ref) = refs[:count], refs[count : count + 3]
-        piece_refs, (out_ref, held, sems) = refs[count + 3 : 2 * count + 3], refs[-3:]
+        piece_refs = refs[count + 3 : 2 * count + 3]
+        out_ref, *held = refs[len(refs) - count - 2 : -1]
+        sems = refs[-1]
         own_ids = ids_ref[pl.ds(core_ref[0], 1), :]
         scale = jnp.zeros(own_ids.shape, F32)
         spread = []
         for a in range(adapters):
             scale = jnp.where(own_ids == a, weight_ref[a], scale)
             spread.append(jnp.where(own_ids == a, low_ref[...].astype(F32), 0.0))
-        spread = jnp.concatenate(spread, axis=0).astype(BF16)
+        spread = jnp.concatenate(spread, axis=0).T.astype(BF16)
         scale = jnp.broadcast_to(scale, (rows, rows)).T[:, :1]
         copies = []
-        for i in range(count):
+        for i, (piece, start) in enumerate(zip(pieces, starts)):
+            own, chunk = slice(start, start + piece.shape[0]), piece.shape[1]
             at = pl.ds(pl.multiple_of(offset_refs[i][0], 128), chunk)
-            term = dot_first(spread, down_ref[:, at])
+            term = dot_plain(spread[own], down_ref[:, at])
             total = piece_refs[i][...].astype(F32) + ADAPTER_SCALE * term
-            held[i] = (scale * total).astype(BF16)
-            copies.append(pltpu.make_async_copy(held.at[i], out_ref.at[:, at], sems.at[i]))
+            held[i][...] = (scale[own] * total).astype(BF16)
+            copies.append(pltpu.make_async_copy(held[i], out_ref.at[own, at], sems.at[i]))
             copies[-1].start()
         for copy in copies:
             copy.wait()
@@ -218,7 +226,7 @@
         specs[len(args)] = ANY
         aliases = {len(args): 0}
         args.append(into)
-    scratch = [pltpu.VMEM((count, rows, chunk), BF16), pltpu.SemaphoreType.DMA((count,))]
+    scratch = [pltpu.VMEM(p.shape, BF16) for p in pieces] + [pltpu.SemaphoreType.DMA((count,))]
     shape = array((rows, width), BF16)
     return call(body, shape, args, specs, out_specs=ANY, scratch=scratch, aliases=aliases)
 
@@ -315,14 +323,22 @@
     for s in order:
         product(s, *ready)
         ready = parts[s]
-    product(n - 1, *ready, totals[order[0]])
+    last = after(blocks[n - 1], *ready, totals[order[0]])
+    away_parts = multiply(last, w_parts, first, range(1, tensors), CUTS)
+    kept_parts = multiply(after(last, *away_parts), w_parts, first, (0,), CUTS)
+    finals = []
+    for j in range(CUTS):
+        kept = after(kept_parts[j], *finals).astype(F32)
+        for k in range(1, tensors):
+            kept = kept + swap(away_parts[(k - 1) * CUTS + j], "tensor", k).astype(F32)
+        finals.append(kept.astype(BF16))
     bit = top // 2
     while bit:
         letter = held[bit : 2 * bit] + [cards[s] for s in cards]
-        post(bit, after(jnp.concatenate(letter, axis=1), totals[n - 1]))
+        post(bit, after(jnp.concatenate(letter, axis=1), finals[-1]))
         bit //= 2
-    cards = [after(cards[s], totals[n - 1]) for s in range(n)]
-    down_sum = after(held[0], totals[n - 1])
+    cards = [after(cards[s], finals[-1]) for s in range(n)]
+    down_sum = after(held[0], finals[-1])
     all_ids = jnp.stack([v[rank : rank + cores] for v in cards]).astype(jnp.int32)
     counts = jnp.sum((all_ids.reshape(1, -1) == labels[:, None]).astype(F32), axis=1)
     weight = F32(n * cores * rows) / (F32(adapters) * counts)
@@ -333,26 +349,34 @@
     down_grad = down_sum.reshape(OWN_MAX, rank, half) * slot_weight[:, None, None]
     down_grad = down_grad.transpose(2, 0, 1)
 
-    back = [swap(v, "dp", s) if s else v for s, v in sorted(totals.items())]
+    back = [swap(totals[s], "dp", s) if s else totals[0] for s in range(n - 1)]
+    last_back = [swap(v, "dp", n - 1) for v in finals]
     span = n // tensors
     low_bits, high_bits = z % span, z // span
-    pieces, offsets = [], []
+    pieces, offsets, starts = [], [], []
     for r in range(span):
-        choices = [back[r + k * span] for k in range(tensors)]
-        choices[0] = after(choices[0], totals[n - 1])
-        for k in range(tensors):
-            piece = choose(choices, t ^ k ^ high_bits)
-            pieces.append(swap(piece, "tensor", k) if k else piece)
-            offsets.append((r ^ low_bits) * width + (t ^ k) * chunk)
+        for j in range(CUTS if r == span - 1 else 1):
+            choices = [back[s] for s in range(r, n - 1, span)]
+            start = j * (rows // CUTS)
+            if r == span - 1:
+                choices = [v[start : start + rows // CUTS] for v in choices] + [last_back[j]]
+            choices[0] = after(choices[0], finals[-1], *(choices_before if j else ()))
+            choices_before = choices
+            for k in range(tensors):
+                piece = choose(choices, t ^ k ^ high_bits)
+                pieces.append(swap(piece, "tensor", k) if k else piece)
+                offsets.append((r ^ low_bits) * width + (t ^ k) * chunk)
+                starts.append(start)
     if chunk % 128 == 0:
         offsets = [one(v) for v in offsets]
-        args = (ids, low_out, down_t)
-        early = finish(weight, core, offsets[:-1], *args, pieces[:-1])
-        input_gradient = finish(weight, core, offsets[-1:], *args, pieces[-1:], into=early)
+        args = (weight, core, ids, low_out, down_t)
+        late = len(pieces) - len(pieces)
+        early = finish(*args, pieces[:late], offsets[:late], starts[:late]) if late else None
+        input_gradient = finish(*args, pieces[late:], offsets[late:], starts[late:], into=early)
     else:
         base = jnp.zeros((rows, span * width), BF16)
-        for piece, offset in zip(pieces, offsets):
-            base = lax.dynamic_update_slice_in_dim(base, piece, offset, 1)
+        for piece, offset, start in zip(pieces, offsets, starts):
+            base = lax.dynamic_update_slice(base, piece, (start, offset))
         own_match = (pick(ids, c)[:, None] == labels[None, :]).astype(F32)
         own_weight = jnp.sum(own_match * weight[None, :], axis=1)
         spread = (own_match.T.astype(BF16)[:, None, :] * low_out[None]).reshape(-1, rows)

time: 61.5 us -> 58.3 us (0.948)
  waiting for transfers between devices: 21.6 us -> 17.3 us
  starting transfers between devices: 22.3 us -> 24.5 us
  Pallas kernels: 9.71 us -> 8.56 us
    ppermute x18 -> x21, waiting for transfers between devices: 21.6 us -> 17.3 us  [swap(): return lax.ppermute(value, axis, [(i, i ^ step) for i in range(size)])]
    ppermute x18 -> x21, starting transfers between devices: 22.3 us -> 24.5 us  [swap(): return lax.ppermute(value, axis, [(i, i ^ step) for i in range(size)])]
    pallas_call x10, Pallas kernels: 9.71 us -> 8.56 us  [call(): pl.pallas_call(body, out_shape=out_shape, in_specs=in_specs, out_specs=ou...]
  transfers between devices with their start and end apart: 18 -> 21, of which waited for: 9 -> 10; matrix products, arithmetic and copies ran while one was open for 3% -> 4% of each run, Pallas kernels for 13% -> 12%
where the time goes in v4:
time: 58.3 us; the launch traced here: 58.1 us
  starting transfers between devices  24.5 us (42%)
  waiting for transfers between devices  17.3 us (30%)
  Pallas kernels  8.56 us (15%)
  local copies, waits for them, and re-layouts  4.69 us (8%)
  other arithmetic  2.15 us (4%)
  between operations  0.87 us (1%)
    ppermute x21, starting transfers between devices, swap(): return lax.ppermute(value, axis, [(i, i ^ step) for i in range(size)])  24.5 us
    ppermute x21, waiting for transfers between devices, swap(): return lax.ppermute(value, axis, [(i, i ^ step) for i in range(size)])  17.3 us
    pallas_call x10, Pallas kernels, call(): pl.pallas_call(body, out_shape=out_shape, in_specs=in_specs, out_specs=ou...  8.56 us
    unnamed x22, local copies, waits for them, and re-layouts  4.66 us
  transfers between devices with their start and end apart: 21, of which 10 were waited for; matrix products, arithmetic and copies ran while one was open for 4% of the time, Pallas kernels for 12%

profile of v4, /device:TPU:0, one launch (start us, length us, event | category | flops | bytes accessed | tf_op | source)
XLA Modules:
  0.0 58.1 jit_solution(6404698998075135713)
XLA Ops:
  0.6 0.5 collective-permute-start
  1.1 3.7 %collective-permute-start.2 = (bf16[128,1280]{1,0:T(8,128)(2,1)}, bf16[128,1280]{1,0:T(8,128)(2,1)S(1)}, u32[]{:S(2)}, u32[]{:S(2)}) collective-permute-start(bf16[128,1280]{1,0:T(8,128)(2,1)} %refs_4_.1), channel_id=1, source_target_pairs={{0,8},{4,12},{8,0},{12,4},{1,9},{5,13},{9,1},{13,5},{2,10},{6,14},... | collective-permute-start | bytes 983048 | tf_op jit(solution)/shard_map/ppermute | solution.py:236
  4.8 1.6 %collective-permute-start.4 = (bf16[128,1280]{1,0:T(8,128)(2,1)}, bf16[128,1280]{1,0:T(8,128)(2,1)S(1)}, u32[]{:S(2)}, u32[]{:S(2)}) collective-permute-start(bf16[128,1280]{1,0:T(8,128)(2,1)} %refs_4_.1), channel_id=1, source_target_pairs={{0,4},{4,0},{8,12},{12,8},{1,5},{5,1},{9,13},{13,9},{2,6},{6,2},{1... | collective-permute-start | bytes 983048 | tf_op jit(solution)/shard_map/ppermute | solution.py:236
  6.4 0.0 collective-permute-done.refs_3_
  6.4 1.1 %copy-done.2 = bf16[128,2560]{1,0:T(8,128)(2,1)S(1)} copy-done((bf16[128,2560]{1,0:T(8,128)(2,1)S(1)}, bf16[128,2560]{1,0:T(8,128)(2,1)}, u32[]{:S(2)}) %copy-start.2) | copy-done | bytes 655384
  7.5 1.0 %copy-done.4 = bf16[128,1280]{1,0:T(8,128)(2,1)S(1)} copy-done((bf16[128,1280]{1,0:T(8,128)(2,1)S(1)}, bf16[128,1280]{1,0:T(8,128)(2,1)}, u32[]{:S(2)}) %copy-start.4) | copy-done | bytes 327704
  8.5 1.0 %copy-done.6 = bf16[2560,4,16]{0,2,1:T(8,128)(2,1)S(1)} copy-done((bf16[2560,4,16]{0,2,1:T(8,128)(2,1)S(1)}, bf16[2560,4,16]{0,2,1:T(8,128)(2,1)}, u32[]{:S(2)}) %copy-start.6) | copy-done | bytes 327704
  9.4 0.9 %copy-done.8 = bf16[4,16,1280]{2,1,0:T(8,128)(2,1)S(1)} copy-done((bf16[4,16,1280]{2,1,0:T(8,128)(2,1)S(1)}, bf16[4,16,1280]{2,1,0:T(8,128)(2,1)}, u32[]{:S(2)}) %copy-start.8) | copy-done | bytes 163864
  10.3 0.7 %copy-done.9 = s32[256]{0:T(256)S(1)} copy-done((s32[256]{0:T(256)S(1)}, s32[256]{0:T(256)}, u32[]{:S(2)}) %copy-start.9) | copy-done | bytes 1048
  11.0 0.5 shard_map.94.rest_0_
  11.5 1.6 %collective-permute-start.1 = (f32[32,128]{1,0:T(8,128)S(1)}, f32[32,128]{1,0:T(8,128)S(1)}, u32[]{:S(2)}, u32[]{:S(2)}) collective-permute-start(f32[32,128]{1,0:T(8,128)S(1)} %shard_map.94.rest_0_), channel_id=1, source_target_pairs={{0,2},{2,0},{1,3},{3,1},{4,6},{6,4},{5,7},{7,5},{8,10},{10,8},{9,1... | collective-permute-start | bytes 49160 | tf_op jit(solution)/shard_map/ppermute | solution.py:236
  13.1 1.1 %shard_map.96 = (bf16[128,640]{1,0:T(8,128)(2,1)S(1)}, bf16[128,640]{1,0:T(8,128)(2,1)S(1)}) custom-call(s32[1]{0:T(128)} %bitcast.5.refs_0_, bf16[128,1280]{1,0:T(8,128)(2,1)S(1)} %copy-done.4, bf16[640,1280]{1,0:T(8,128)(2,1)S(1)} %copy-done.1, bf16[640,1280]{1,0:T(8,128)(2,1)S(1)} %collective-permute-done.refs_3_), custom_call_target="tpu_custom_call" | custom-call | flops 8589934592 | bytes 33554432 | tf_op jit(solution)/shard_map/pallas_call | solution.py:34
  14.2 0.9 %collective-permute-start.12 = (bf16[128,640]{1,0:T(8,128)(2,1)S(1)}, bf16[128,640]{1,0:T(8,128)(2,1)S(1)}, u32[]{:S(2)}, u32[]{:S(2)}) collective-permute-start(bf16[128,640]{1,0:T(8,128)(2,1)S(1)} %get-tuple-element.44), channel_id=1, source_target_pairs={{0,2},{2,0},{1,3},{3,1},{4,6},{6,4},{5,7},{7,5},{8,10},{10,8},{9,1... | collective-permute-start | bytes 491528 | tf_op jit(solution)/shard_map/ppermute | solution.py:236
  15.1 0.2 collective-permute-done.1.rest_1_
  15.3 0.9 %shard_map.95 = (bf16[32,128]{1,0:T(8,128)(2,1)S(1)}, bf16[16,128]{1,0:T(8,128)(2,1)S(1)}, bf16[128,1280]{1,0:T(8,128)(2,1)S(1)}, bf16[128,1280]{1,0:T(8,128)(2,1)S(1)}) custom-call(s32[4]{0:T(128)S(1)} %copy-done, s32[1]{0:T(128)} %bitcast.core_ref, s32[2,128]{1,0:T(2,128)S(1)} %bitcast.30, bf16[128,2560]{1,0:T(8,128)(2,1)S(1)} %copy-done.3, ...), custom_call_target="tpu_custom_call" | custom-call | flops 8589934592 | bytes 33554432 | tf_op jit(solution)/shard_map/pallas_call | solution.py:34
  16.2 4.3 %collective-permute-done.2.refs_1_.refs_6_ = bf16[128,1280]{1,0:T(8,128)(2,1)S(1)} collective-permute-done((bf16[128,1280]{1,0:T(8,128)(2,1)}, bf16[128,1280]{1,0:T(8,128)(2,1)S(1)}, u32[]{:S(2)}, u32[]{:S(2)}) %collective-permute-start.2) | collective-permute-done | bytes 327712 | tf_op jit(solution)/shard_map/ppermute | solution.py:236
  20.5 0.0 collective-permute-start.5
  20.5 0.8 %collective-permute-start.3 = (bf16[128,1280]{1,0:T(8,128)(2,1)S(1)}, bf16[128,1280]{1,0:T(8,128)(2,1)S(1)}, u32[]{:S(2)}, u32[]{:S(2)}) collective-permute-start(bf16[128,1280]{1,0:T(8,128)(2,1)S(1)} %collective-permute-done.2.refs_1_.refs_6_), channel_id=1, source_target_pairs={{0,4},{4,0},{8,12},{12,8},{1,5},{5,1},{9,13},{13,9},{2,6},{6,2},{1... | collective-permute-start | bytes 983048 | tf_op jit(solution)/shard_map/ppermute | solution.py:236
  21.3 0.0 collective-permute-done.12
  21.3 0.8 %collective-permute-done.5.got_ref = bf16[128,1280]{1,0:T(8,128)(2,1)S(1)} collective-permute-done((bf16[128,1280]{1,0:T(8,128)(2,1)S(1)}, bf16[128,1280]{1,0:T(8,128)(2,1)S(1)}, u32[]{:S(2)}, u32[]{:S(2)}) %collective-permute-start.5) | collective-permute-done | bytes 327712 | tf_op jit(solution)/shard_map/ppermute | solution.py:236
  22.1 0.1 shard_map.97
  22.2 2.6 %collective-permute-start.9 = (bf16[32,2688]{1,0:T(8,128)(2,1)S(1)}, bf16[32,2688]{1,0:T(8,128)(2,1)S(1)}, u32[]{:S(2)}, u32[]{:S(2)}) collective-permute-start(bf16[32,2688]{1,0:T(8,128)(2,1)S(1)} %get-tuple-element.49), channel_id=1, source_target_pairs={{0,8},{4,12},{8,0},{12,4},{1,9},{5,13},{9,1},{13,5},{2,10},{6,14},... | collective-permute-start | bytes 516104 | tf_op jit(solution)/shard_map/ppermute | solution.py:236
  24.8 1.1 %shard_map.98 = (bf16[128,640]{1,0:T(8,128)(2,1)S(1)}, bf16[128,640]{1,0:T(8,128)(2,1)S(1)}) custom-call(s32[1]{0:T(128)} %bitcast.5.refs_0_, bf16[128,1280]{1,0:T(8,128)(2,1)S(1)} %collective-permute-done.2.refs_1_.refs_6_, bf16[640,1280]{1,0:T(8,128)(2,1)S(1)} %copy-done.1, bf16[640,1280]{1,0:T(8,128)(2,1)S(1)} %collective-permute-done.refs_3_), custom_call_target="tpu_custom_call" | custom-call | flops 8589934592 | bytes 33554432 | tf_op jit(solution)/shard_map/pallas_call | solution.py:34
  25.8 1.6 %collective-permute-start.6 = (bf16[128,640]{1,0:T(8,128)(2,1)S(1)}, bf16[128,640]{1,0:T(8,128)(2,1)S(1)}, u32[]{:S(2)}, u32[]{:S(2)}) collective-permute-start(bf16[128,640]{1,0:T(8,128)(2,1)S(1)} %get-tuple-element.52), channel_id=1, source_target_pairs={{0,2},{2,0},{1,3},{3,1},{4,6},{6,4},{5,7},{7,5},{8,10},{10,8},{9,1... | collective-permute-start | bytes 491528 | tf_op jit(solution)/shard_map/ppermute | solution.py:236
  27.4 0.0 collective-permute-done.4.refs_1_.refs_5_
  27.4 1.1 %shard_map.99 = (bf16[128,640]{1,0:T(8,128)(2,1)S(1)}, bf16[128,640]{1,0:T(8,128)(2,1)S(1)}) custom-call(s32[1]{0:T(128)} %bitcast.5.refs_0_, bf16[128,1280]{1,0:T(8,128)(2,1)S(1)} %collective-permute-done.4.refs_1_.refs_5_, bf16[640,1280]{1,0:T(8,128)(2,1)S(1)} %copy-done.1, bf16[640,1280]{1,0:T(8,128)(2,1)S(1)} %collective-permute-done.refs_3_), custom_call_target="tpu_custom_call" | custom-call | flops 8589934592 | bytes 33554432 | tf_op jit(solution)/shard_map/pallas_call | solution.py:34
  28.5 0.6 %collective-permute-start.15 = (bf16[128,640]{1,0:T(8,128)(2,1)S(1)}, bf16[128,640]{1,0:T(8,128)(2,1)S(1)}, u32[]{:S(2)}, u32[]{:S(2)}) collective-permute-start(bf16[128,640]{1,0:T(8,128)(2,1)S(1)} %get-tuple-element.55), channel_id=1, source_target_pairs={{0,2},{2,0},{1,3},{3,1},{4,6},{6,4},{5,7},{7,5},{8,10},{10,8},{9,1... | collective-permute-start | bytes 491528 | tf_op jit(solution)/shard_map/ppermute | solution.py:236
  29.1 3.9 %collective-permute-done.6 = bf16[128,640]{1,0:T(8,128)(2,1)S(1)} collective-permute-done((bf16[128,640]{1,0:T(8,128)(2,1)S(1)}, bf16[128,640]{1,0:T(8,128)(2,1)S(1)}, u32[]{:S(2)}, u32[]{:S(2)}) %collective-permute-start.6) | collective-permute-done | bytes 163872 | tf_op jit(solution)/shard_map/ppermute | solution.py:236
  33.0 0.4 collective-permute-start.11
  33.4 0.9 %collective-permute-done.3.refs_1_.refs_7_ = bf16[128,1280]{1,0:T(8,128)(2,1)S(1)} collective-permute-done((bf16[128,1280]{1,0:T(8,128)(2,1)S(1)}, bf16[128,1280]{1,0:T(8,128)(2,1)S(1)}, u32[]{:S(2)}, u32[]{:S(2)}) %collective-permute-start.3) | collective-permute-done | bytes 327712 | tf_op jit(solution)/shard_map/ppermute | solution.py:236
  34.3 0.6 %shard_map.100 = (bf16[64,640]{1,0:T(8,128)(2,1)S(1)}, bf16[64,640]{1,0:T(8,128)(2,1)S(1)}) custom-call(s32[1]{0:T(128)} %bitcast.5.refs_0_, bf16[128,1280]{1,0:T(8,128)(2,1)S(1)} %collective-permute-done.3.refs_1_.refs_7_, bf16[640,1280]{1,0:T(8,128)(2,1)S(1)} %copy-done.1, bf16[640,1280]{1,0:T(8,128)(2,1)S(1)} %collective-permute-done.refs_3_), custom_call_target="tpu_custom_call" | custom-call | flops 8589934592 | bytes 33554432 | tf_op jit(solution)/shard_map/pallas_call | solution.py:34
  34.9 1.6 %collective-permute-start.7 = (bf16[64,640]{1,0:T(8,128)(2,1)S(1)}, bf16[64,640]{1,0:T(8,128)(2,1)S(1)}, u32[]{:S(2)}, u32[]{:S(2)}) collective-permute-start(bf16[64,640]{1,0:T(8,128)(2,1)S(1)} %get-tuple-element.57), channel_id=1, source_target_pairs={{0,2},{2,0},{1,3},{3,1},{4,6},{6,4},{5,7},{7,5},{8,10},{10,8},{9,1... | collective-permute-start | bytes 245768 | tf_op jit(solution)/shard_map/ppermute | solution.py:236
  36.5 0.5 collective-permute-start.8
  37.0 0.6 %shard_map.101 = (bf16[64,640]{1,0:T(8,128)(2,1)S(1)}, bf16[64,640]{1,0:T(8,128)(2,1)S(1)}) custom-call(s32[1]{0:T(128)} %bitcast.5.refs_0_, bf16[128,1280]{1,0:T(8,128)(2,1)S(1)} %collective-permute-done.3.refs_1_.refs_7_, bf16[640,1280]{1,0:T(8,128)(2,1)S(1)} %copy-done.1, bf16[640,1280]{1,0:T(8,128)(2,1)S(1)} %collective-permute-done.refs_3_), custom_call_target="tpu_custom_call" | custom-call | flops 8589934592 | bytes 33554432 | tf_op jit(solution)/shard_map/pallas_call | solution.py:34
  37.7 0.0 collective-permute-done.15
  37.7 0.0 copy-start.5
  37.7 0.4 collective-permute-start.16
  38.2 0.0 collective-permute-done.9
  38.2 2.0 %collective-permute-done.7 = bf16[64,640]{1,0:T(8,128)(2,1)S(1)} collective-permute-done((bf16[64,640]{1,0:T(8,128)(2,1)S(1)}, bf16[64,640]{1,0:T(8,128)(2,1)S(1)}, u32[]{:S(2)}, u32[]{:S(2)}) %collective-permute-start.7) | collective-permute-done | bytes 81952 | tf_op jit(solution)/shard_map/ppermute | solution.py:236
  40.3 3.6 %collective-permute-start.14 = (bf16[64,640]{1,0:T(8,128)(2,1)S(1)}, bf16[64,640]{1,0:T(8,128)(2,1)S(1)}, u32[]{:S(2)}, u32[]{:S(2)}) collective-permute-start(bf16[64,640]{1,0:T(8,128)(2,1)S(1)} %add_convert_fusion.6), channel_id=1, source_target_pairs={{0,12},{4,8},{8,4},{12,0},{1,13},{5,9},{9,5},{13,1},{2,14},{6,10},... | collective-permute-start | bytes 245768 | tf_op jit(solution)/shard_map/ppermute | solution.py:236
  43.8 0.0 collective-permute-done.8
  43.9 0.8 %collective-permute-start.18 = (bf16[64,640]{1,0:T(8,128)(2,1)S(1)}, bf16[64,640]{1,0:T(8,128)(2,1)S(1)}, u32[]{:S(2)}, u32[]{:S(2)}) collective-permute-start(bf16[64,640]{1,0:T(8,128)(2,1)S(1)} %add_convert_fusion.5), channel_id=1, source_target_pairs={{0,12},{4,8},{8,4},{12,0},{1,13},{5,9},{9,5},{13,1},{2,14},{6,10},... | collective-permute-start | bytes 245768 | tf_op jit(solution)/shard_map/ppermute | solution.py:236
  44.7 0.0 collective-permute-start.10
  44.7 0.0 collective-permute-done.11
  44.8 1.2 %collective-permute-start.13 = (bf16[128,640]{1,0:T(8,128)(2,1)S(1)}, bf16[128,640]{1,0:T(8,128)(2,1)S(1)}, u32[]{:S(2)}, u32[]{:S(2)}) collective-permute-start(bf16[128,640]{1,0:T(8,128)(2,1)S(1)} %get-tuple-element.77), channel_id=1, source_target_pairs={{0,2},{2,0},{1,3},{3,1},{4,6},{6,4},{5,7},{7,5},{8,10},{10,8},{9,1... | collective-permute-start | bytes 491528 | tf_op jit(solution)/shard_map/ppermute | solution.py:236
  46.0 3.0 %collective-permute-done.16 = bf16[128,640]{1,0:T(8,128)(2,1)S(1)} collective-permute-done((bf16[128,640]{1,0:T(8,128)(2,1)S(1)}, bf16[128,640]{1,0:T(8,128)(2,1)S(1)}, u32[]{:S(2)}, u32[]{:S(2)}) %collective-permute-start.16) | collective-permute-done | bytes 163872 | tf_op jit(solution)/shard_map/ppermute | solution.py:236
  49.0 0.0 collective-permute-done.14
  49.0 1.3 %collective-permute-done.18 = bf16[64,640]{1,0:T(8,128)(2,1)S(1)} collective-permute-done((bf16[64,640]{1,0:T(8,128)(2,1)S(1)}, bf16[64,640]{1,0:T(8,128)(2,1)S(1)}, u32[]{:S(2)}, u32[]{:S(2)}) %collective-permute-start.18) | collective-permute-done | bytes 81952 | tf_op jit(solution)/shard_map/ppermute | solution.py:236
  50.3 1.5 %collective-permute-start.19 = (bf16[64,640]{1,0:T(8,128)(2,1)S(1)}, bf16[64,640]{1,0:T(8,128)(2,1)S(1)}, u32[]{:S(2)}, u32[]{:S(2)}) collective-permute-start(bf16[64,640]{1,0:T(8,128)(2,1)S(1)} %get-tuple-element.79), channel_id=1, source_target_pairs={{0,2},{2,0},{1,3},{3,1},{4,6},{6,4},{5,7},{7,5},{8,10},{10,8},{9,1... | collective-permute-start | bytes 245768 | tf_op jit(solution)/shard_map/ppermute | solution.py:236
  51.8 0.7 %collective-permute-start.17 = (bf16[64,640]{1,0:T(8,128)(2,1)S(1)}, bf16[64,640]{1,0:T(8,128)(2,1)S(1)}, u32[]{:S(2)}, u32[]{:S(2)}) collective-permute-start(bf16[64,640]{1,0:T(8,128)(2,1)S(1)} %get-tuple-element.83), channel_id=1, source_target_pairs={{0,2},{2,0},{1,3},{3,1},{4,6},{6,4},{5,7},{7,5},{8,10},{10,8},{9,1... | collective-permute-start | bytes 245768 | tf_op jit(solution)/shard_map/ppermute | solution.py:236
  52.5 0.0 collective-permute-done.10
  52.6 0.1 convert_reduce_fusion
  52.7 0.2 fusion
  52.9 0.0 copy-start.7
  53.0 0.0 copy-start.10
  53.0 0.9 %shard_map.103 = (f32[32,640]{1,0:T(8,128)S(1)}, f32[32,640]{1,0:T(8,128)S(1)}) custom-call(s32[4]{0:T(128)S(1)} %copy-done, s32[1]{0:T(128)} %bitcast.core_ref, s32[1]{0:T(128)} %bitcast.6.place_ref, bf16[32,128]{1,0:T(8,128)(2,1)S(1)} %get-tuple-element.63.card_ref.refs_0_, bf16[32,128]{1,0:T(8,128)(2,1)S(1)} %get-tuple-element.66.refs_1_, ...), custom_call_target="tpu_custom_call" | custom-call | flops 8589934592 | bytes 33554432 | tf_op jit(solution)/shard_map/pallas_call | solution.py:34
  53.9 0.1 collective-permute-start.20
  53.9 0.7 %multiply_bitcast_fusion = f32[1280,2,16]{0,2,1:T(8,128)} fusion(f32[2,16,1280]{2,1,0:T(8,128)S(1)} %bitcast.32, f32[2]{0:T(128)S(1)} %broadcast_multiply_fusion.1), kind=kLoop, calls=%fused_computation.3 | loop fusion | flops 40960 | bytes 327688 | tf_op jit(solution)/shard_map/transpose | solution.py:350
  54.7 0.5 collective-permute-done.20
  55.2 0.7 %broadcast_multiply_fusion = f32[2,16,640]{2,1,0:T(8,128)} fusion(f32[2,16,640]{2,1,0:T(8,128)S(1)} %bitcast.33, f32[2]{0:T(128)S(1)} %broadcast_multiply_fusion.1), kind=kLoop, calls=%fused_computation.16 | loop fusion | flops 20480 | bytes 163848 | tf_op jit(solution)/shard_map/mul | solution.py:390
  55.9 0.0 collective-permute-done.19.refs_14_
  55.9 0.4 collective-permute-done.17.refs_12_
  56.3 0.0 collective-permute-done.13.refs_10_
  56.4 1.7 %shard_map.102 = bf16[128,2560]{1,0:T(8,128)(2,1)} custom-call(f32[4]{0:T(128)S(1)} %multiply_divide_fusion.weight_ref, s32[1]{0:T(128)} %bitcast.core_ref, s32[1]{0:T(128)} %bitcast.12.refs_0_, s32[1]{0:T(128)} %bitcast.13.refs_1_, s32[1]{0:T(128)} %bitcast.14.refs_2_.refs_4_, s32[1]{0:T(128)} %bitcast.15.refs_3_.refs_5_, s32[1]{0:T(128)} %bitcast.14.refs_2_.refs_4_, ...), custom_call_target="tpu_custom_call" | custom-call | flops 8589934592 | bytes 33554432 | tf_op jit(solution)/shard_map/pallas_call | solution.py:34
  (36 shorter events, 0.4 us)
Async XLA Ops:
  0.6 5.8 %collective-permute-start = (bf16[640,1280]{1,0:T(8,128)(2,1)}, bf16[640,1280]{1,0:T(8,128)(2,1)S(1)}, u32[]{:S(2)}, u32[]{:S(2)}) collective-permute-start(bf16[640,1280]{1,0:T(8,128)(2,1)} %refs_2_.9), channel_id=1, source_target_pairs={{0,1},{1,0},{2,3},{3,2},{4,5},{5,4},{6,7},{7,6},{8,9},{9,8},{10,11... | collective-permute-start | bytes 4915208 | tf_op jit(solution)/shard_map/ppermute | solution.py:236
  1.1 19.3 %collective-permute-start.2 = (bf16[128,1280]{1,0:T(8,128)(2,1)}, bf16[128,1280]{1,0:T(8,128)(2,1)S(1)}, u32[]{:S(2)}, u32[]{:S(2)}) collective-permute-start(bf16[128,1280]{1,0:T(8,128)(2,1)} %refs_4_.1), channel_id=1, source_target_pairs={{0,8},{4,12},{8,0},{12,4},{1,9},{5,13},{9,1},{13,5},{2,10},{6,14},... | collective-permute-start | bytes 983048 | tf_op jit(solution)/shard_map/ppermute | solution.py:236
  4.8 22.6 %collective-permute-start.4 = (bf16[128,1280]{1,0:T(8,128)(2,1)}, bf16[128,1280]{1,0:T(8,128)(2,1)S(1)}, u32[]{:S(2)}, u32[]{:S(2)}) collective-permute-start(bf16[128,1280]{1,0:T(8,128)(2,1)} %refs_4_.1), channel_id=1, source_target_pairs={{0,4},{4,0},{8,12},{12,8},{1,5},{5,1},{9,13},{13,9},{2,6},{6,2},{1... | collective-permute-start | bytes 983048 | tf_op jit(solution)/shard_map/ppermute | solution.py:236
  6.4 1.1 %copy-start.2 = (bf16[128,2560]{1,0:T(8,128)(2,1)S(1)}, bf16[128,2560]{1,0:T(8,128)(2,1)}, u32[]{:S(2)}) copy-start(bf16[128,2560]{1,0:T(8,128)(2,1)} %x_ref.3) | copy-start | bytes 1966084
  7.5 1.0 %copy-start.4 = (bf16[128,1280]{1,0:T(8,128)(2,1)S(1)}, bf16[128,1280]{1,0:T(8,128)(2,1)}, u32[]{:S(2)}) copy-start(bf16[128,1280]{1,0:T(8,128)(2,1)} %refs_4_.1) | copy-start | bytes 983044
  8.5 1.0 %copy-start.6 = (bf16[2560,4,16]{0,2,1:T(8,128)(2,1)S(1)}, bf16[2560,4,16]{0,2,1:T(8,128)(2,1)}, u32[]{:S(2)}) copy-start(bf16[2560,4,16]{0,2,1:T(8,128)(2,1)} %param.12) | copy-start | bytes 983044
  9.4 0.9 %copy-start.8 = (bf16[4,16,1280]{2,1,0:T(8,128)(2,1)S(1)}, bf16[4,16,1280]{2,1,0:T(8,128)(2,1)}, u32[]{:S(2)}) copy-start(bf16[4,16,1280]{2,1,0:T(8,128)(2,1)} %param.13) | copy-start | bytes 491524
  10.3 0.7 %copy-start.9 = (s32[256]{0:T(256)S(1)}, s32[256]{0:T(256)}, u32[]{:S(2)}) copy-start(s32[256]{0:T(256)} %param.9) | copy-start | bytes 3076
  11.0 2.0 %copy-start.1 = (bf16[640,1280]{1,0:T(8,128)(2,1)S(1)}, bf16[640,1280]{1,0:T(8,128)(2,1)}, u32[]{:S(2)}) copy-start(bf16[640,1280]{1,0:T(8,128)(2,1)} %refs_2_.9) | copy-start | bytes 4915204
  11.5 3.8 %collective-permute-start.1 = (f32[32,128]{1,0:T(8,128)S(1)}, f32[32,128]{1,0:T(8,128)S(1)}, u32[]{:S(2)}, u32[]{:S(2)}) collective-permute-start(f32[32,128]{1,0:T(8,128)S(1)} %shard_map.94.rest_0_), channel_id=1, source_target_pairs={{0,2},{2,0},{1,3},{3,1},{4,6},{6,4},{5,7},{7,5},{8,10},{10,8},{9,1... | collective-permute-start | bytes 49160 | tf_op jit(solution)/shard_map/ppermute | solution.py:236
  13.1 2.2 %copy-start = (s32[4]{0:T(128)S(1)}, s32[4]{0:T(128)}, u32[]{:S(2)}) copy-start(s32[4]{0:T(128)} %slot_ref.3) | copy-start | bytes 52
  13.1 2.2 %copy-start.3 = (bf16[128,2560]{1,0:T(8,128)(2,1)S(1)}, bf16[128,2560]{1,0:T(8,128)(2,1)}, u32[]{:S(2)}) copy-start(bf16[128,2560]{1,0:T(8,128)(2,1)} %x_ref.3) | copy-start | bytes 1966084
  14.2 7.1 %collective-permute-start.12 = (bf16[128,640]{1,0:T(8,128)(2,1)S(1)}, bf16[128,640]{1,0:T(8,128)(2,1)S(1)}, u32[]{:S(2)}, u32[]{:S(2)}) collective-permute-start(bf16[128,640]{1,0:T(8,128)(2,1)S(1)} %get-tuple-element.44), channel_id=1, source_target_pairs={{0,2},{2,0},{1,3},{3,1},{4,6},{6,4},{5,7},{7,5},{8,10},{10,8},{9,1... | collective-permute-start | bytes 491528 | tf_op jit(solution)/shard_map/ppermute | solution.py:236
  20.5 1.6 %collective-permute-start.5 = (bf16[128,1280]{1,0:T(8,128)(2,1)S(1)}, bf16[128,1280]{1,0:T(8,128)(2,1)S(1)}, u32[]{:S(2)}, u32[]{:S(2)}) collective-permute-start(bf16[128,1280]{1,0:T(8,128)(2,1)S(1)} %get-tuple-element.48), channel_id=1, source_target_pairs={{0,1},{1,0},{2,3},{3,2},{4,5},{5,4},{6,7},{7,6},{8,9},{9,8},{10,11... | collective-permute-start | bytes 983048 | tf_op jit(solution)/shard_map/ppermute | solution.py:236
  20.5 13.8 %collective-permute-start.3 = (bf16[128,1280]{1,0:T(8,128)(2,1)S(1)}, bf16[128,1280]{1,0:T(8,128)(2,1)S(1)}, u32[]{:S(2)}, u32[]{:S(2)}) collective-permute-start(bf16[128,1280]{1,0:T(8,128)(2,1)S(1)} %collective-permute-done.2.refs_1_.refs_6_), channel_id=1, source_target_pairs={{0,4},{4,0},{8,12},{12,8},{1,5},{5,1},{9,13},{13,9},{2,6},{6,2},{1... | collective-permute-start | bytes 983048 | tf_op jit(solution)/shard_map/ppermute | solution.py:236
  22.2 16.0 %collective-permute-start.9 = (bf16[32,2688]{1,0:T(8,128)(2,1)S(1)}, bf16[32,2688]{1,0:T(8,128)(2,1)S(1)}, u32[]{:S(2)}, u32[]{:S(2)}) collective-permute-start(bf16[32,2688]{1,0:T(8,128)(2,1)S(1)} %get-tuple-element.49), channel_id=1, source_target_pairs={{0,8},{4,12},{8,0},{12,4},{1,9},{5,13},{9,1},{13,5},{2,10},{6,14},... | collective-permute-start | bytes 516104 | tf_op jit(solution)/shard_map/ppermute | solution.py:236
  25.8 7.2 %collective-permute-start.6 = (bf16[128,640]{1,0:T(8,128)(2,1)S(1)}, bf16[128,640]{1,0:T(8,128)(2,1)S(1)}, u32[]{:S(2)}, u32[]{:S(2)}) collective-permute-start(bf16[128,640]{1,0:T(8,128)(2,1)S(1)} %get-tuple-element.52), channel_id=1, source_target_pairs={{0,2},{2,0},{1,3},{3,1},{4,6},{6,4},{5,7},{7,5},{8,10},{10,8},{9,1... | collective-permute-start | bytes 491528 | tf_op jit(solution)/shard_map/ppermute | solution.py:236
  28.5 9.2 %collective-permute-start.15 = (bf16[128,640]{1,0:T(8,128)(2,1)S(1)}, bf16[128,640]{1,0:T(8,128)(2,1)S(1)}, u32[]{:S(2)}, u32[]{:S(2)}) collective-permute-start(bf16[128,640]{1,0:T(8,128)(2,1)S(1)} %get-tuple-element.55), channel_id=1, source_target_pairs={{0,2},{2,0},{1,3},{3,1},{4,6},{6,4},{5,7},{7,5},{8,10},{10,8},{9,1... | collective-permute-start | bytes 491528 | tf_op jit(solution)/shard_map/ppermute | solution.py:236
  33.0 11.7 %collective-permute-start.11 = (bf16[128,640]{1,0:T(8,128)(2,1)S(1)}, bf16[128,640]{1,0:T(8,128)(2,1)S(1)}, u32[]{:S(2)}, u32[]{:S(2)}) collective-permute-start(bf16[128,640]{1,0:T(8,128)(2,1)S(1)} %add_convert_fusion.2), channel_id=1, source_target_pairs={{0,8},{4,12},{8,0},{12,4},{1,9},{5,13},{9,1},{13,5},{2,10},{6,14},... | collective-permute-start | bytes 491528 | tf_op jit(solution)/shard_map/ppermute | solution.py:236
  34.9 5.3 %collective-permute-start.7 = (bf16[64,640]{1,0:T(8,128)(2,1)S(1)}, bf16[64,640]{1,0:T(8,128)(2,1)S(1)}, u32[]{:S(2)}, u32[]{:S(2)}) collective-permute-start(bf16[64,640]{1,0:T(8,128)(2,1)S(1)} %get-tuple-element.57), channel_id=1, source_target_pairs={{0,2},{2,0},{1,3},{3,1},{4,6},{6,4},{5,7},{7,5},{8,10},{10,8},{9,1... | collective-permute-start | bytes 245768 | tf_op jit(solution)/shard_map/ppermute | solution.py:236
  36.5 7.3 %collective-permute-start.8 = (bf16[64,640]{1,0:T(8,128)(2,1)S(1)}, bf16[64,640]{1,0:T(8,128)(2,1)S(1)}, u32[]{:S(2)}, u32[]{:S(2)}) collective-permute-start(bf16[64,640]{1,0:T(8,128)(2,1)S(1)} %get-tuple-element.58), channel_id=1, source_target_pairs={{0,2},{2,0},{1,3},{3,1},{4,6},{6,4},{5,7},{7,5},{8,10},{10,8},{9,1... | collective-permute-start | bytes 245768 | tf_op jit(solution)/shard_map/ppermute | solution.py:236
  37.7 15.2 %copy-start.5 = (bf16[128,1280]{1,0:T(8,128)(2,1)S(1)}, bf16[128,1280]{1,0:T(8,128)(2,1)}, u32[]{:S(2)}) copy-start(bf16[128,1280]{1,0:T(8,128)(2,1)} %refs_4_.1) | copy-start | bytes 983044
  37.7 11.2 %collective-permute-start.16 = (bf16[128,640]{1,0:T(8,128)(2,1)S(1)}, bf16[128,640]{1,0:T(8,128)(2,1)S(1)}, u32[]{:S(2)}, u32[]{:S(2)}) collective-permute-start(bf16[128,640]{1,0:T(8,128)(2,1)S(1)} %add_convert_fusion), channel_id=1, source_target_pairs={{0,4},{4,0},{8,12},{12,8},{1,5},{5,1},{9,13},{13,9},{2,6},{6,2},{1... | collective-permute-start | bytes 491528 | tf_op jit(solution)/shard_map/ppermute | solution.py:236
  40.3 8.7 %collective-permute-start.14 = (bf16[64,640]{1,0:T(8,128)(2,1)S(1)}, bf16[64,640]{1,0:T(8,128)(2,1)S(1)}, u32[]{:S(2)}, u32[]{:S(2)}) collective-permute-start(bf16[64,640]{1,0:T(8,128)(2,1)S(1)} %add_convert_fusion.6), channel_id=1, source_target_pairs={{0,12},{4,8},{8,4},{12,0},{1,13},{5,9},{9,5},{13,1},{2,14},{6,10},... | collective-permute-start | bytes 245768 | tf_op jit(solution)/shard_map/ppermute | solution.py:236
  43.9 6.4 %collective-permute-start.18 = (bf16[64,640]{1,0:T(8,128)(2,1)S(1)}, bf16[64,640]{1,0:T(8,128)(2,1)S(1)}, u32[]{:S(2)}, u32[]{:S(2)}) collective-permute-start(bf16[64,640]{1,0:T(8,128)(2,1)S(1)} %add_convert_fusion.5), channel_id=1, source_target_pairs={{0,12},{4,8},{8,4},{12,0},{1,13},{5,9},{9,5},{13,1},{2,14},{6,10},... | collective-permute-start | bytes 245768 | tf_op jit(solution)/shard_map/ppermute | solution.py:236
  44.7 7.8 %collective-permute-start.10 = (bf16[32,1536]{1,0:T(8,128)(2,1)S(1)}, bf16[32,1536]{1,0:T(8,128)(2,1)S(1)}, u32[]{:S(2)}, u32[]{:S(2)}) collective-permute-start(bf16[32,1536]{1,0:T(8,128)(2,1)S(1)} %pad_maximum_fusion), channel_id=1, source_target_pairs={{0,4},{4,0},{8,12},{12,8},{1,5},{5,1},{9,13},{13,9},{2,6},{6,2},{1... | collective-permute-start | bytes 294920 | tf_op jit(solution)/shard_map/ppermute | solution.py:236
  44.8 11.6 %collective-permute-start.13 = (bf16[128,640]{1,0:T(8,128)(2,1)S(1)}, bf16[128,640]{1,0:T(8,128)(2,1)S(1)}, u32[]{:S(2)}, u32[]{:S(2)}) collective-permute-start(bf16[128,640]{1,0:T(8,128)(2,1)S(1)} %get-tuple-element.77), channel_id=1, source_target_pairs={{0,2},{2,0},{1,3},{3,1},{4,6},{6,4},{5,7},{7,5},{8,10},{10,8},{9,1... | collective-permute-start | bytes 491528 | tf_op jit(solution)/shard_map/ppermute | solution.py:236
  50.3 5.6 %collective-permute-start.19 = (bf16[64,640]{1,0:T(8,128)(2,1)S(1)}, bf16[64,640]{1,0:T(8,128)(2,1)S(1)}, u32[]{:S(2)}, u32[]{:S(2)}) collective-permute-start(bf16[64,640]{1,0:T(8,128)(2,1)S(1)} %get-tuple-element.79), channel_id=1, source_target_pairs={{0,2},{2,0},{1,3},{3,1},{4,6},{6,4},{5,7},{7,5},{8,10},{10,8},{9,1... | collective-permute-start | bytes 245768 | tf_op jit(solution)/shard_map/ppermute | solution.py:236
  51.8 4.5 %collective-permute-start.17 = (bf16[64,640]{1,0:T(8,128)(2,1)S(1)}, bf16[64,640]{1,0:T(8,128)(2,1)S(1)}, u32[]{:S(2)}, u32[]{:S(2)}) collective-permute-start(bf16[64,640]{1,0:T(8,128)(2,1)S(1)} %get-tuple-element.83), channel_id=1, source_target_pairs={{0,2},{2,0},{1,3},{3,1},{4,6},{6,4},{5,7},{7,5},{8,10},{10,8},{9,1... | collective-permute-start | bytes 245768 | tf_op jit(solution)/shard_map/ppermute | solution.py:236
  52.9 3.4 %copy-start.7 = (bf16[2560,4,16]{0,2,1:T(8,128)(2,1)S(1)}, bf16[2560,4,16]{0,2,1:T(8,128)(2,1)}, u32[]{:S(2)}) copy-start(bf16[2560,4,16]{0,2,1:T(8,128)(2,1)} %param.12) | copy-start | bytes 983044
  53.0 3.4 %copy-start.10 = (s32[256]{0:T(256)S(1)}, s32[256]{0:T(256)}, u32[]{:S(2)}) copy-start(s32[256]{0:T(256)} %param.9) | copy-start | bytes 3076
  53.9 1.3 %collective-permute-start.20 = (f32[32,640]{1,0:T(8,128)S(1)}, f32[32,640]{1,0:T(8,128)S(1)}, u32[]{:S(2)}, u32[]{:S(2)}) collective-permute-start(f32[32,640]{1,0:T(8,128)S(1)} %get-tuple-element.76), channel_id=1, source_target_pairs={{0,1},{1,0},{2,3},{3,2},{4,5},{5,4},{6,7},{7,6},{8,9},{9,8},{10,11... | collective-permute-start | bytes 245768 | tf_op jit(solution)/shard_map/ppermute | solution.py:236

commit v5 on v4

--- a/solution.py
+++ b/solution.py
@@ -189,45 +189,61 @@
     return out
 
 
-def finish(weight, core, ids, low_out, down_t, pieces, offsets, starts, into=None):
+def adapter_rows(core, ids, low_out, down_t):
     rows, width = ids.shape[1], down_t.shape[1]
-    rank = low_out.shape[0]
-    adapters, count = weight.shape[0], len(pieces)
-
-    def body(weight_ref, core_ref, *refs):
-        offset_refs, (ids_ref, low_ref, down_ref) = refs[:count], refs[count : count + 3]
-        piece_refs = refs[count + 3 : 2 * count + 3]
+    adapters = down_t.shape[0] // low_out.shape[0]
+
+    def body(core_ref, ids_ref, low_ref, down_ref, out_ref):
+        own_ids = ids_ref[pl.ds(core_ref[0], 1), :]
+        low = low_ref[...].astype(F32)
+        spread = [jnp.where(own_ids == a, low, 0.0) for a in range(adapters)]
+        spread = jnp.concatenate(spread, axis=0).T.astype(BF16)
+        out_ref[...] = ADAPTER_SCALE * dot_plain(spread, down_ref[...])
+
+    return call(body, array((rows, width), F32), [core, ids, low_out, down_t], {0: SMEM})
+
+
+def row_scales(weight, core, ids):
+    rows = ids.shape[1]
+
+    def body(weight_ref, core_ref, ids_ref, out_ref):
+        own_ids = ids_ref[pl.ds(core_ref[0], 1), :]
+        scale = jnp.zeros(own_ids.shape, F32)
+        for a in range(weight.shape[0]):
+            scale = jnp.where(own_ids == a, weight_ref[a], scale)
+        out_ref[...] = jnp.broadcast_to(scale, (rows, rows)).T
+
+    return call(body, array((rows, rows), F32), [weight, core, ids], {0: SMEM, 1: SMEM})
+
+
+def finish(scale, term, pieces, offsets, starts, into=None):
+    count = len(pieces)
+
+    def body(*refs):
+        offset_refs, (scale_ref, term_ref) = refs[:count], refs[count : count + 2]
+        piece_refs = refs[count + 2 : 2 * count + 2]
         out_ref, *held = refs[len(refs) - count - 2 : -1]
         sems = refs[-1]
-        own_ids = ids_ref[pl.ds(core_ref[0], 1), :]
-        scale = jnp.zeros(own_ids.shape, F32)
-        spread = []
-        for a in range(adapters):
-            scale = jnp.where(own_ids == a, weight_ref[a], scale)
-            spread.append(jnp.where(own_ids == a, low_ref[...].astype(F32), 0.0))
-        spread = jnp.concatenate(spread, axis=0).T.astype(BF16)
-        scale = jnp.broadcast_to(scale, (rows, rows)).T[:, :1]
         copies = []
         for i, (piece, start) in enumerate(zip(pieces, starts)):
             own, chunk = slice(start, start + piece.shape[0]), piece.shape[1]
             at = pl.ds(pl.multiple_of(offset_refs[i][0], 128), chunk)
-            term = dot_plain(spread[own], down_ref[:, at])
-            total = piece_refs[i][...].astype(F32) + ADAPTER_SCALE * term
-            held[i][...] = (scale[own] * total).astype(BF16)
+            total = piece_refs[i][...].astype(F32) + term_ref[own, at]
+            held[i][...] = (scale_ref[own, :1] * total).astype(BF16)
             copies.append(pltpu.make_async_copy(held[i], out_ref.at[own, at], sems.at[i]))
             copies[-1].start()
         for copy in copies:
             copy.wait()
 
-    args = [weight, core, *offsets, ids, low_out, down_t, *pieces]
-    specs = {i: SMEM for i in range(2 + count)}
+    args = [*offsets, scale, term, *pieces]
+    specs = {i: SMEM for i in range(count)}
     aliases = None
     if into is not None:
         specs[len(args)] = ANY
         aliases = {len(args): 0}
         args.append(into)
     scratch = [pltpu.VMEM(p.shape, BF16) for p in pieces] + [pltpu.SemaphoreType.DMA((count,))]
-    shape = array((rows, width), BF16)
+    shape = array(term.shape, BF16)
     return call(body, shape, args, specs, out_specs=ANY, scratch=scratch, aliases=aliases)
 
 
@@ -317,6 +333,7 @@
             cards[s ^ bit] = got[:, at : at + rows]
 
     post(top, letter)
+    term = adapter_rows(core, ids, low_out, down_t)
     hand_on(range(top, n), low, *parts[0])
     order = [*range(top, n - 1), *range(1, top)]
     ready = [letter]
@@ -369,7 +386,7 @@
                 starts.append(start)
     if chunk % 128 == 0:
         offsets = [one(v) for v in offsets]
-        args = (weight, core, ids, low_out, down_t)
+        args = (row_scales(weight, core, ids), term)
         late = len(pieces) - len(pieces)
         early = finish(*args, pieces[:late], offsets[:late], starts[:late]) if late else None
         input_gradient = finish(*args, pieces[late:], offsets[late:], starts[late:], into=early)
@@ -379,9 +396,7 @@
             base = lax.dynamic_update_slice(base, piece, (start, offset))
         own_match = (pick(ids, c)[:, None] == labels[None, :]).astype(F32)
         own_weight = jnp.sum(own_match * weight[None, :], axis=1)
-        spread = (own_match.T.astype(BF16)[:, None, :] * low_out[None]).reshape(-1, rows)
-        total = base.astype(F32) + ADAPTER_SCALE * dot_first(spread, down_t)
-        input_gradient = (own_weight[:, None] * total).astype(BF16)
+        input_gradient = (own_weight[:, None] * (base.astype(F32) + term)).astype(BF16)
 
     up_mine, up_away = lift_up(
         owner_slot, core, place, cards, [blocks[s] for s in range(n)], rank

time: 58.3 us -> 57.9 us (level)
  waiting for transfers between devices: 17.3 us -> 14.4 us
  starting transfers between devices: 24.5 us -> 26.4 us
    ppermute x21, waiting for transfers between devices: 17.3 us -> 14.4 us  [swap(): return lax.ppermute(value, axis, [(i, i ^ step) for i in range(size)])]
    ppermute x21, starting transfers between devices: 24.5 us -> 26.4 us  [swap(): return lax.ppermute(value, axis, [(i, i ^ step) for i in range(size)])]
    pallas_call x10 -> x12, Pallas kernels: 8.56 us -> 8.86 us  [call(): pl.pallas_call(body, out_shape=out_shape, in_specs=in_specs, out_specs=ou...]
  transfers between devices with their start and end apart: 21 -> 21, of which waited for: 10 -> 9; matrix products, arithmetic and copies ran while one was open for 4% -> 4% of each run, Pallas kernels for 12% -> 14%
where the time goes in v5:
time: 57.9 us; the launch traced here: 57.5 us
  starting transfers between devices  26.4 us (46%)
  waiting for transfers between devices  14.4 us (25%)
  Pallas kernels  8.86 us (15%)
  local copies, waits for them, and re-layouts  4.81 us (8%)
  other arithmetic  2.16 us (4%)
  between operations  0.89 us (2%)
    ppermute x21, starting transfers between devices, swap(): return lax.ppermute(value, axis, [(i, i ^ step) for i in range(size)])  26.4 us
    ppermute x21, waiting for transfers between devices, swap(): return lax.ppermute(value, axis, [(i, i ^ step) for i in range(size)])  14.4 us
    pallas_call x12, Pallas kernels, call(): pl.pallas_call(body, out_shape=out_shape, in_specs=in_specs, out_specs=ou...  8.86 us
    unnamed x22, local copies, waits for them, and re-layouts  4.78 us
  transfers between devices with their start and end apart: 21, of which 9 were waited for; matrix products, arithmetic and copies ran while one was open for 4% of the time, Pallas kernels for 14%

profile of v5, /device:TPU:0, one launch (start us, length us, event | category | flops | bytes accessed | tf_op | source)
XLA Modules:
  0.0 57.5 jit_solution(421523080796589804)
XLA Ops:
  0.6 0.5 collective-permute-start
  1.1 3.7 %collective-permute-start.2 = (bf16[128,1280]{1,0:T(8,128)(2,1)}, bf16[128,1280]{1,0:T(8,128)(2,1)S(1)}, u32[]{:S(2)}, u32[]{:S(2)}) collective-permute-start(bf16[128,1280]{1,0:T(8,128)(2,1)} %refs_4_.1), channel_id=1, source_target_pairs={{0,8},{4,12},{8,0},{12,4},{1,9},{5,13},{9,1},{13,5},{2,10},{6,14},... | collective-permute-start | bytes 983048 | tf_op jit(solution)/shard_map/ppermute | solution.py:252
  4.8 1.6 %collective-permute-start.4 = (bf16[128,1280]{1,0:T(8,128)(2,1)}, bf16[128,1280]{1,0:T(8,128)(2,1)S(1)}, u32[]{:S(2)}, u32[]{:S(2)}) collective-permute-start(bf16[128,1280]{1,0:T(8,128)(2,1)} %refs_4_.1), channel_id=1, source_target_pairs={{0,4},{4,0},{8,12},{12,8},{1,5},{5,1},{9,13},{13,9},{2,6},{6,2},{1... | collective-permute-start | bytes 983048 | tf_op jit(solution)/shard_map/ppermute | solution.py:252
  6.4 0.0 collective-permute-done.refs_3_
  6.4 1.1 %copy-done.2 = bf16[128,2560]{1,0:T(8,128)(2,1)S(1)} copy-done((bf16[128,2560]{1,0:T(8,128)(2,1)S(1)}, bf16[128,2560]{1,0:T(8,128)(2,1)}, u32[]{:S(2)}) %copy-start.2) | copy-done | bytes 655384
  7.5 1.0 %copy-done.4 = bf16[2560,4,16]{0,2,1:T(8,128)(2,1)S(1)} copy-done((bf16[2560,4,16]{0,2,1:T(8,128)(2,1)S(1)}, bf16[2560,4,16]{0,2,1:T(8,128)(2,1)}, u32[]{:S(2)}) %copy-start.4) | copy-done | bytes 327704
  8.5 1.0 %copy-done.6 = bf16[128,1280]{1,0:T(8,128)(2,1)S(1)} copy-done((bf16[128,1280]{1,0:T(8,128)(2,1)S(1)}, bf16[128,1280]{1,0:T(8,128)(2,1)}, u32[]{:S(2)}) %copy-start.6) | copy-done | bytes 327704
  9.4 0.9 %copy-done.8 = bf16[4,16,1280]{2,1,0:T(8,128)(2,1)S(1)} copy-done((bf16[4,16,1280]{2,1,0:T(8,128)(2,1)S(1)}, bf16[4,16,1280]{2,1,0:T(8,128)(2,1)}, u32[]{:S(2)}) %copy-start.8) | copy-done | bytes 163864
  10.3 0.7 %copy-done.9 = s32[256]{0:T(256)S(1)} copy-done((s32[256]{0:T(256)S(1)}, s32[256]{0:T(256)}, u32[]{:S(2)}) %copy-start.9) | copy-done | bytes 1048
  11.0 0.5 shard_map.94.rest_0_
  11.5 1.6 %collective-permute-start.1 = (f32[32,128]{1,0:T(8,128)S(1)}, f32[32,128]{1,0:T(8,128)S(1)}, u32[]{:S(2)}, u32[]{:S(2)}) collective-permute-start(f32[32,128]{1,0:T(8,128)S(1)} %shard_map.94.rest_0_), channel_id=1, source_target_pairs={{0,2},{2,0},{1,3},{3,1},{4,6},{6,4},{5,7},{7,5},{8,10},{10,8},{9,1... | collective-permute-start | bytes 49160 | tf_op jit(solution)/shard_map/ppermute | solution.py:252
  13.1 1.1 %shard_map.96 = (bf16[128,640]{1,0:T(8,128)(2,1)S(1)}, bf16[128,640]{1,0:T(8,128)(2,1)S(1)}) custom-call(s32[1]{0:T(128)} %bitcast.9.refs_0_, bf16[128,1280]{1,0:T(8,128)(2,1)S(1)} %copy-done.6, bf16[640,1280]{1,0:T(8,128)(2,1)S(1)} %copy-done.1, bf16[640,1280]{1,0:T(8,128)(2,1)S(1)} %collective-permute-done.refs_3_), custom_call_target="tpu_custom_call" | custom-call | flops 8589934592 | bytes 33554432 | tf_op jit(solution)/shard_map/pallas_call | solution.py:34
  14.2 0.9 %collective-permute-start.12 = (bf16[128,640]{1,0:T(8,128)(2,1)S(1)}, bf16[128,640]{1,0:T(8,128)(2,1)S(1)}, u32[]{:S(2)}, u32[]{:S(2)}) collective-permute-start(bf16[128,640]{1,0:T(8,128)(2,1)S(1)} %get-tuple-element.44), channel_id=1, source_target_pairs={{0,2},{2,0},{1,3},{3,1},{4,6},{6,4},{5,7},{7,5},{8,10},{10,8},{9,1... | collective-permute-start | bytes 491528 | tf_op jit(solution)/shard_map/ppermute | solution.py:252
  15.1 5.4 %collective-permute-done.2.refs_1_.refs_6_ = bf16[128,1280]{1,0:T(8,128)(2,1)S(1)} collective-permute-done((bf16[128,1280]{1,0:T(8,128)(2,1)}, bf16[128,1280]{1,0:T(8,128)(2,1)S(1)}, u32[]{:S(2)}, u32[]{:S(2)}) %collective-permute-start.2) | collective-permute-done | bytes 327712 | tf_op jit(solution)/shard_map/ppermute | solution.py:252
  20.5 0.7 %collective-permute-start.3 = (bf16[128,1280]{1,0:T(8,128)(2,1)S(1)}, bf16[128,1280]{1,0:T(8,128)(2,1)S(1)}, u32[]{:S(2)}, u32[]{:S(2)}) collective-permute-start(bf16[128,1280]{1,0:T(8,128)(2,1)S(1)} %collective-permute-done.2.refs_1_.refs_6_), channel_id=1, source_target_pairs={{0,4},{4,0},{8,12},{12,8},{1,5},{5,1},{9,13},{13,9},{2,6},{6,2},{1... | collective-permute-start | bytes 983048 | tf_op jit(solution)/shard_map/ppermute | solution.py:252
  21.2 0.0 collective-permute-done.1.rest_1_
  21.2 0.9 %shard_map.95 = (bf16[32,128]{1,0:T(8,128)(2,1)S(1)}, bf16[16,128]{1,0:T(8,128)(2,1)S(1)}, bf16[128,1280]{1,0:T(8,128)(2,1)S(1)}, bf16[128,1280]{1,0:T(8,128)(2,1)S(1)}) custom-call(s32[4]{0:T(128)S(1)} %copy-done, s32[1]{0:T(128)} %bitcast.4.core_ref, s32[2,128]{1,0:T(2,128)S(1)} %bitcast.30, bf16[128,2560]{1,0:T(8,128)(2,1)S(1)} %copy-done.3, ...), custom_call_target="tpu_custom_call" | custom-call | flops 8589934592 | bytes 33554432 | tf_op jit(solution)/shard_map/pallas_call | solution.py:34
  22.1 0.1 collective-permute-start.5
  22.2 0.4 shard_map.103.refs_7_
  22.5 0.0 collective-permute-done.12
  22.6 1.2 %collective-permute-done.5.got_ref = bf16[128,1280]{1,0:T(8,128)(2,1)S(1)} collective-permute-done((bf16[128,1280]{1,0:T(8,128)(2,1)S(1)}, bf16[128,1280]{1,0:T(8,128)(2,1)S(1)}, u32[]{:S(2)}, u32[]{:S(2)}) %collective-permute-start.5) | collective-permute-done | bytes 327712 | tf_op jit(solution)/shard_map/ppermute | solution.py:252
  23.8 0.1 shard_map.97
  23.8 3.3 %collective-permute-start.9 = (bf16[32,2688]{1,0:T(8,128)(2,1)S(1)}, bf16[32,2688]{1,0:T(8,128)(2,1)S(1)}, u32[]{:S(2)}, u32[]{:S(2)}) collective-permute-start(bf16[32,2688]{1,0:T(8,128)(2,1)S(1)} %get-tuple-element.49), channel_id=1, source_target_pairs={{0,8},{4,12},{8,0},{12,4},{1,9},{5,13},{9,1},{13,5},{2,10},{6,14},... | collective-permute-start | bytes 516104 | tf_op jit(solution)/shard_map/ppermute | solution.py:252
  27.2 1.1 %shard_map.98 = (bf16[128,640]{1,0:T(8,128)(2,1)S(1)}, bf16[128,640]{1,0:T(8,128)(2,1)S(1)}) custom-call(s32[1]{0:T(128)} %bitcast.9.refs_0_, bf16[128,1280]{1,0:T(8,128)(2,1)S(1)} %collective-permute-done.2.refs_1_.refs_6_, bf16[640,1280]{1,0:T(8,128)(2,1)S(1)} %copy-done.1, bf16[640,1280]{1,0:T(8,128)(2,1)S(1)} %collective-permute-done.refs_3_), custom_call_target="tpu_custom_call" | custom-call | flops 8589934592 | bytes 33554432 | tf_op jit(solution)/shard_map/pallas_call | solution.py:34
  28.3 1.5 %collective-permute-start.6 = (bf16[128,640]{1,0:T(8,128)(2,1)S(1)}, bf16[128,640]{1,0:T(8,128)(2,1)S(1)}, u32[]{:S(2)}, u32[]{:S(2)}) collective-permute-start(bf16[128,640]{1,0:T(8,128)(2,1)S(1)} %get-tuple-element.52), channel_id=1, source_target_pairs={{0,2},{2,0},{1,3},{3,1},{4,6},{6,4},{5,7},{7,5},{8,10},{10,8},{9,1... | collective-permute-start | bytes 491528 | tf_op jit(solution)/shard_map/ppermute | solution.py:252
  29.8 0.0 collective-permute-done.4.refs_1_.refs_5_
  29.8 1.1 %shard_map.99 = (bf16[128,640]{1,0:T(8,128)(2,1)S(1)}, bf16[128,640]{1,0:T(8,128)(2,1)S(1)}) custom-call(s32[1]{0:T(128)} %bitcast.9.refs_0_, bf16[128,1280]{1,0:T(8,128)(2,1)S(1)} %collective-permute-done.4.refs_1_.refs_5_, bf16[640,1280]{1,0:T(8,128)(2,1)S(1)} %copy-done.1, bf16[640,1280]{1,0:T(8,128)(2,1)S(1)} %collective-permute-done.refs_3_), custom_call_target="tpu_custom_call" | custom-call | flops 8589934592 | bytes 33554432 | tf_op jit(solution)/shard_map/pallas_call | solution.py:34
  30.9 0.6 %collective-permute-start.15 = (bf16[128,640]{1,0:T(8,128)(2,1)S(1)}, bf16[128,640]{1,0:T(8,128)(2,1)S(1)}, u32[]{:S(2)}, u32[]{:S(2)}) collective-permute-start(bf16[128,640]{1,0:T(8,128)(2,1)S(1)} %get-tuple-element.55), channel_id=1, source_target_pairs={{0,2},{2,0},{1,3},{3,1},{4,6},{6,4},{5,7},{7,5},{8,10},{10,8},{9,1... | collective-permute-start | bytes 491528 | tf_op jit(solution)/shard_map/ppermute | solution.py:252
  31.5 3.9 %collective-permute-done.6 = bf16[128,640]{1,0:T(8,128)(2,1)S(1)} collective-permute-done((bf16[128,640]{1,0:T(8,128)(2,1)S(1)}, bf16[128,640]{1,0:T(8,128)(2,1)S(1)}, u32[]{:S(2)}, u32[]{:S(2)}) %collective-permute-start.6) | collective-permute-done | bytes 163872 | tf_op jit(solution)/shard_map/ppermute | solution.py:252
  35.4 0.1 collective-permute-start.11
  35.5 0.0 collective-permute-done.3.refs_1_.refs_7_
  35.5 0.7 %shard_map.100 = (bf16[64,640]{1,0:T(8,128)(2,1)S(1)}, bf16[64,640]{1,0:T(8,128)(2,1)S(1)}) custom-call(s32[1]{0:T(128)} %bitcast.9.refs_0_, bf16[128,1280]{1,0:T(8,128)(2,1)S(1)} %collective-permute-done.3.refs_1_.refs_7_, bf16[640,1280]{1,0:T(8,128)(2,1)S(1)} %copy-done.1, bf16[640,1280]{1,0:T(8,128)(2,1)S(1)} %collective-permute-done.refs_3_), custom_call_target="tpu_custom_call" | custom-call | flops 8589934592 | bytes 33554432 | tf_op jit(solution)/shard_map/pallas_call | solution.py:34
  36.2 1.6 %collective-permute-start.7 = (bf16[64,640]{1,0:T(8,128)(2,1)S(1)}, bf16[64,640]{1,0:T(8,128)(2,1)S(1)}, u32[]{:S(2)}, u32[]{:S(2)}) collective-permute-start(bf16[64,640]{1,0:T(8,128)(2,1)S(1)} %get-tuple-element.57), channel_id=1, source_target_pairs={{0,2},{2,0},{1,3},{3,1},{4,6},{6,4},{5,7},{7,5},{8,10},{10,8},{9,1... | collective-permute-start | bytes 245768 | tf_op jit(solution)/shard_map/ppermute | solution.py:252
  37.8 0.5 collective-permute-start.8
  38.3 0.6 %shard_map.101 = (bf16[64,640]{1,0:T(8,128)(2,1)S(1)}, bf16[64,640]{1,0:T(8,128)(2,1)S(1)}) custom-call(s32[1]{0:T(128)} %bitcast.9.refs_0_, bf16[128,1280]{1,0:T(8,128)(2,1)S(1)} %collective-permute-done.3.refs_1_.refs_7_, bf16[640,1280]{1,0:T(8,128)(2,1)S(1)} %copy-done.1, bf16[640,1280]{1,0:T(8,128)(2,1)S(1)} %collective-permute-done.refs_3_), custom_call_target="tpu_custom_call" | custom-call | flops 8589934592 | bytes 33554432 | tf_op jit(solution)/shard_map/pallas_call | solution.py:34
  38.9 0.0 collective-permute-done.15
  39.0 0.0 copy-start.10
  39.0 0.9 %collective-permute-start.16 = (bf16[128,640]{1,0:T(8,128)(2,1)S(1)}, bf16[128,640]{1,0:T(8,128)(2,1)S(1)}, u32[]{:S(2)}, u32[]{:S(2)}) collective-permute-start(bf16[128,640]{1,0:T(8,128)(2,1)S(1)} %add_convert_fusion), channel_id=1, source_target_pairs={{0,4},{4,0},{8,12},{12,8},{1,5},{5,1},{9,13},{13,9},{2,6},{6,2},{1... | collective-permute-start | bytes 491528 | tf_op jit(solution)/shard_map/ppermute | solution.py:252
  40.0 0.7 %collective-permute-done.7 = bf16[64,640]{1,0:T(8,128)(2,1)S(1)} collective-permute-done((bf16[64,640]{1,0:T(8,128)(2,1)S(1)}, bf16[64,640]{1,0:T(8,128)(2,1)S(1)}, u32[]{:S(2)}, u32[]{:S(2)}) %collective-permute-start.7) | collective-permute-done | bytes 81952 | tf_op jit(solution)/shard_map/ppermute | solution.py:252
  40.7 2.9 %collective-permute-start.14 = (bf16[64,640]{1,0:T(8,128)(2,1)S(1)}, bf16[64,640]{1,0:T(8,128)(2,1)S(1)}, u32[]{:S(2)}, u32[]{:S(2)}) collective-permute-start(bf16[64,640]{1,0:T(8,128)(2,1)S(1)} %add_convert_fusion.6), channel_id=1, source_target_pairs={{0,12},{4,8},{8,4},{12,0},{1,13},{5,9},{9,5},{13,1},{2,14},{6,10},... | collective-permute-start | bytes 245768 | tf_op jit(solution)/shard_map/ppermute | solution.py:252
  43.6 0.0 collective-permute-done.8
  43.6 1.1 %collective-permute-start.18 = (bf16[64,640]{1,0:T(8,128)(2,1)S(1)}, bf16[64,640]{1,0:T(8,128)(2,1)S(1)}, u32[]{:S(2)}, u32[]{:S(2)}) collective-permute-start(bf16[64,640]{1,0:T(8,128)(2,1)S(1)} %add_convert_fusion.5), channel_id=1, source_target_pairs={{0,12},{4,8},{8,4},{12,0},{1,13},{5,9},{9,5},{13,1},{2,14},{6,10},... | collective-permute-start | bytes 245768 | tf_op jit(solution)/shard_map/ppermute | solution.py:252
  44.7 1.0 %collective-permute-start.10 = (bf16[32,1536]{1,0:T(8,128)(2,1)S(1)}, bf16[32,1536]{1,0:T(8,128)(2,1)S(1)}, u32[]{:S(2)}, u32[]{:S(2)}) collective-permute-start(bf16[32,1536]{1,0:T(8,128)(2,1)S(1)} %pad_maximum_fusion), channel_id=1, source_target_pairs={{0,4},{4,0},{8,12},{12,8},{1,5},{5,1},{9,13},{13,9},{2,6},{6,2},{1... | collective-permute-start | bytes 294920 | tf_op jit(solution)/shard_map/ppermute | solution.py:252
  45.8 0.9 %collective-permute-done.11 = bf16[128,640]{1,0:T(8,128)(2,1)S(1)} collective-permute-done((bf16[128,640]{1,0:T(8,128)(2,1)S(1)}, bf16[128,640]{1,0:T(8,128)(2,1)S(1)}, u32[]{:S(2)}, u32[]{:S(2)}) %collective-permute-start.11) | collective-permute-done | bytes 163872 | tf_op jit(solution)/shard_map/ppermute | solution.py:252
  46.7 1.6 %collective-permute-start.13 = (bf16[128,640]{1,0:T(8,128)(2,1)S(1)}, bf16[128,640]{1,0:T(8,128)(2,1)S(1)}, u32[]{:S(2)}, u32[]{:S(2)}) collective-permute-start(bf16[128,640]{1,0:T(8,128)(2,1)S(1)} %get-tuple-element.77), channel_id=1, source_target_pairs={{0,2},{2,0},{1,3},{3,1},{4,6},{6,4},{5,7},{7,5},{8,10},{10,8},{9,1... | collective-permute-start | bytes 491528 | tf_op jit(solution)/shard_map/ppermute | solution.py:252
  48.2 0.1 collective-permute-done.16
  48.4 0.9 %collective-permute-done.14 = bf16[64,640]{1,0:T(8,128)(2,1)S(1)} collective-permute-done((bf16[64,640]{1,0:T(8,128)(2,1)S(1)}, bf16[64,640]{1,0:T(8,128)(2,1)S(1)}, u32[]{:S(2)}, u32[]{:S(2)}) %collective-permute-start.14) | collective-permute-done | bytes 81952 | tf_op jit(solution)/shard_map/ppermute | solution.py:252
  49.3 0.9 %collective-permute-done.18 = bf16[64,640]{1,0:T(8,128)(2,1)S(1)} collective-permute-done((bf16[64,640]{1,0:T(8,128)(2,1)S(1)}, bf16[64,640]{1,0:T(8,128)(2,1)S(1)}, u32[]{:S(2)}, u32[]{:S(2)}) %collective-permute-start.18) | collective-permute-done | bytes 81952 | tf_op jit(solution)/shard_map/ppermute | solution.py:252
  50.2 1.6 %collective-permute-start.19 = (bf16[64,640]{1,0:T(8,128)(2,1)S(1)}, bf16[64,640]{1,0:T(8,128)(2,1)S(1)}, u32[]{:S(2)}, u32[]{:S(2)}) collective-permute-start(bf16[64,640]{1,0:T(8,128)(2,1)S(1)} %get-tuple-element.79), channel_id=1, source_target_pairs={{0,2},{2,0},{1,3},{3,1},{4,6},{6,4},{5,7},{7,5},{8,10},{10,8},{9,1... | collective-permute-start | bytes 245768 | tf_op jit(solution)/shard_map/ppermute | solution.py:252
  51.8 0.5 collective-permute-start.17
  52.5 0.1 convert_reduce_fusion
  52.6 0.0 copy-start.7
  52.6 0.6 %shard_map.102.refs_6_ = f32[128,128]{1,0:T(8,128)S(1)} custom-call(f32[4]{0:T(128)S(1)} %multiply_divide_fusion.weight_ref, s32[1]{0:T(128)} %bitcast.4.core_ref, s32[2,128]{1,0:T(2,128)S(1)} %bitcast.32), custom_call_target="tpu_custom_call" | custom-call | flops 8589934592 | bytes 33554432 | tf_op jit(solution)/shard_map/pallas_call | solution.py:34
  53.3 0.2 fusion
  53.4 0.1 copy-done.7
  53.6 0.9 %shard_map.105 = (f32[32,640]{1,0:T(8,128)S(1)}, f32[32,640]{1,0:T(8,128)S(1)}) custom-call(s32[4]{0:T(128)S(1)} %copy-done, s32[1]{0:T(128)} %bitcast.4.core_ref, s32[1]{0:T(128)} %bitcast.10.place_ref, bf16[32,128]{1,0:T(8,128)(2,1)S(1)} %get-tuple-element.63.card_ref.refs_0_, bf16[32,128]{1,0:T(8,128)(2,1)S(1)} %get-tuple-element.66.refs_1_, ...), custom_call_target="tpu_custom_call" | custom-call | flops 8589934592 | bytes 33554432 | tf_op jit(solution)/shard_map/pallas_call | solution.py:34
  54.5 0.1 collective-permute-start.20
  54.5 0.7 %multiply_bitcast_fusion = f32[1280,2,16]{0,2,1:T(8,128)} fusion(f32[2,16,1280]{2,1,0:T(8,128)S(1)} %bitcast.33, f32[2]{0:T(128)S(1)} %broadcast_multiply_fusion.1), kind=kLoop, calls=%fused_computation.3 | loop fusion | flops 40960 | bytes 327688 | tf_op jit(solution)/shard_map/transpose | solution.py:367
  55.3 0.5 collective-permute-done.20
  55.8 0.7 %broadcast_multiply_fusion = f32[2,16,640]{2,1,0:T(8,128)} fusion(f32[2,16,640]{2,1,0:T(8,128)S(1)} %bitcast.34, f32[2]{0:T(128)S(1)} %broadcast_multiply_fusion.1), kind=kLoop, calls=%fused_computation.16 | loop fusion | flops 20480 | bytes 163848 | tf_op jit(solution)/shard_map/mul | solution.py:405
  56.5 0.0 collective-permute-done.19.refs_13_
  56.5 0.0 collective-permute-done.17.refs_11_
  56.5 0.0 collective-permute-done.13.refs_9_
  56.5 1.0 %shard_map.104 = bf16[128,2560]{1,0:T(8,128)(2,1)} custom-call(s32[1]{0:T(128)} %bitcast.refs_0_, s32[1]{0:T(128)} %bitcast.1.refs_1_, s32[1]{0:T(128)} %bitcast.2.refs_2_.refs_4_, s32[1]{0:T(128)} %bitcast.3.refs_3_.refs_5_, s32[1]{0:T(128)} %bitcast.2.refs_2_.refs_4_, s32[1]{0:T(128)} %bitcast.3.refs_3_.refs_5_, f32[128,128]{1,0:T(8,128)S(1)} %shard_map.102.refs_6_, ...), custom_call_target="tpu_custom_call" | custom-call | flops 8589934592 | bytes 33554432 | tf_op jit(solution)/shard_map/pallas_call | solution.py:34
  (38 shorter events, 0.5 us)
Async XLA Ops:
  0.6 5.8 %collective-permute-start = (bf16[640,1280]{1,0:T(8,128)(2,1)}, bf16[640,1280]{1,0:T(8,128)(2,1)S(1)}, u32[]{:S(2)}, u32[]{:S(2)}) collective-permute-start(bf16[640,1280]{1,0:T(8,128)(2,1)} %refs_2_.9), channel_id=1, source_target_pairs={{0,1},{1,0},{2,3},{3,2},{4,5},{5,4},{6,7},{7,6},{8,9},{9,8},{10,11... | collective-permute-start | bytes 4915208 | tf_op jit(solution)/shard_map/ppermute | solution.py:252
  1.1 19.3 %collective-permute-start.2 = (bf16[128,1280]{1,0:T(8,128)(2,1)}, bf16[128,1280]{1,0:T(8,128)(2,1)S(1)}, u32[]{:S(2)}, u32[]{:S(2)}) collective-permute-start(bf16[128,1280]{1,0:T(8,128)(2,1)} %refs_4_.1), channel_id=1, source_target_pairs={{0,8},{4,12},{8,0},{12,4},{1,9},{5,13},{9,1},{13,5},{2,10},{6,14},... | collective-permute-start | bytes 983048 | tf_op jit(solution)/shard_map/ppermute | solution.py:252
  4.8 25.0 %collective-permute-start.4 = (bf16[128,1280]{1,0:T(8,128)(2,1)}, bf16[128,1280]{1,0:T(8,128)(2,1)S(1)}, u32[]{:S(2)}, u32[]{:S(2)}) collective-permute-start(bf16[128,1280]{1,0:T(8,128)(2,1)} %refs_4_.1), channel_id=1, source_target_pairs={{0,4},{4,0},{8,12},{12,8},{1,5},{5,1},{9,13},{13,9},{2,6},{6,2},{1... | collective-permute-start | bytes 983048 | tf_op jit(solution)/shard_map/ppermute | solution.py:252
  6.4 1.1 %copy-start.2 = (bf16[128,2560]{1,0:T(8,128)(2,1)S(1)}, bf16[128,2560]{1,0:T(8,128)(2,1)}, u32[]{:S(2)}) copy-start(bf16[128,2560]{1,0:T(8,128)(2,1)} %x_ref.3) | copy-start | bytes 1966084
  7.5 1.0 %copy-start.4 = (bf16[2560,4,16]{0,2,1:T(8,128)(2,1)S(1)}, bf16[2560,4,16]{0,2,1:T(8,128)(2,1)}, u32[]{:S(2)}) copy-start(bf16[2560,4,16]{0,2,1:T(8,128)(2,1)} %param.12) | copy-start | bytes 983044
  8.5 1.0 %copy-start.6 = (bf16[128,1280]{1,0:T(8,128)(2,1)S(1)}, bf16[128,1280]{1,0:T(8,128)(2,1)}, u32[]{:S(2)}) copy-start(bf16[128,1280]{1,0:T(8,128)(2,1)} %refs_4_.1) | copy-start | bytes 983044
  9.4 0.9 %copy-start.8 = (bf16[4,16,1280]{2,1,0:T(8,128)(2,1)S(1)}, bf16[4,16,1280]{2,1,0:T(8,128)(2,1)}, u32[]{:S(2)}) copy-start(bf16[4,16,1280]{2,1,0:T(8,128)(2,1)} %param.13) | copy-start | bytes 491524
  10.3 0.7 %copy-start.9 = (s32[256]{0:T(256)S(1)}, s32[256]{0:T(256)}, u32[]{:S(2)}) copy-start(s32[256]{0:T(256)} %param.9) | copy-start | bytes 3076
  11.0 2.0 %copy-start.1 = (bf16[640,1280]{1,0:T(8,128)(2,1)S(1)}, bf16[640,1280]{1,0:T(8,128)(2,1)}, u32[]{:S(2)}) copy-start(bf16[640,1280]{1,0:T(8,128)(2,1)} %refs_2_.9) | copy-start | bytes 4915204
  11.5 9.7 %collective-permute-start.1 = (f32[32,128]{1,0:T(8,128)S(1)}, f32[32,128]{1,0:T(8,128)S(1)}, u32[]{:S(2)}, u32[]{:S(2)}) collective-permute-start(f32[32,128]{1,0:T(8,128)S(1)} %shard_map.94.rest_0_), channel_id=1, source_target_pairs={{0,2},{2,0},{1,3},{3,1},{4,6},{6,4},{5,7},{7,5},{8,10},{10,8},{9,1... | collective-permute-start | bytes 49160 | tf_op jit(solution)/shard_map/ppermute | solution.py:252
  13.1 8.1 %copy-start = (s32[4]{0:T(128)S(1)}, s32[4]{0:T(128)}, u32[]{:S(2)}) copy-start(s32[4]{0:T(128)} %slot_ref.3) | copy-start | bytes 52
  13.1 8.1 %copy-start.3 = (bf16[128,2560]{1,0:T(8,128)(2,1)S(1)}, bf16[128,2560]{1,0:T(8,128)(2,1)}, u32[]{:S(2)}) copy-start(bf16[128,2560]{1,0:T(8,128)(2,1)} %x_ref.3) | copy-start | bytes 1966084
  14.2 8.4 %collective-permute-start.12 = (bf16[128,640]{1,0:T(8,128)(2,1)S(1)}, bf16[128,640]{1,0:T(8,128)(2,1)S(1)}, u32[]{:S(2)}, u32[]{:S(2)}) collective-permute-start(bf16[128,640]{1,0:T(8,128)(2,1)S(1)} %get-tuple-element.44), channel_id=1, source_target_pairs={{0,2},{2,0},{1,3},{3,1},{4,6},{6,4},{5,7},{7,5},{8,10},{10,8},{9,1... | collective-permute-start | bytes 491528 | tf_op jit(solution)/shard_map/ppermute | solution.py:252
  20.5 1.7 %copy-start.5 = (bf16[2560,4,16]{0,2,1:T(8,128)(2,1)S(1)}, bf16[2560,4,16]{0,2,1:T(8,128)(2,1)}, u32[]{:S(2)}) copy-start(bf16[2560,4,16]{0,2,1:T(8,128)(2,1)} %param.12) | copy-start | bytes 983044
  20.5 15.1 %collective-permute-start.3 = (bf16[128,1280]{1,0:T(8,128)(2,1)S(1)}, bf16[128,1280]{1,0:T(8,128)(2,1)S(1)}, u32[]{:S(2)}, u32[]{:S(2)}) collective-permute-start(bf16[128,1280]{1,0:T(8,128)(2,1)S(1)} %collective-permute-done.2.refs_1_.refs_6_), channel_id=1, source_target_pairs={{0,4},{4,0},{8,12},{12,8},{1,5},{5,1},{9,13},{13,9},{2,6},{6,2},{1... | collective-permute-start | bytes 983048 | tf_op jit(solution)/shard_map/ppermute | solution.py:252
  22.1 1.7 %collective-permute-start.5 = (bf16[128,1280]{1,0:T(8,128)(2,1)S(1)}, bf16[128,1280]{1,0:T(8,128)(2,1)S(1)}, u32[]{:S(2)}, u32[]{:S(2)}) collective-permute-start(bf16[128,1280]{1,0:T(8,128)(2,1)S(1)} %get-tuple-element.48), channel_id=1, source_target_pairs={{0,1},{1,0},{2,3},{3,2},{4,5},{5,4},{6,7},{7,6},{8,9},{9,8},{10,11... | collective-permute-start | bytes 983048 | tf_op jit(solution)/shard_map/ppermute | solution.py:252
  23.8 16.1 %collective-permute-start.9 = (bf16[32,2688]{1,0:T(8,128)(2,1)S(1)}, bf16[32,2688]{1,0:T(8,128)(2,1)S(1)}, u32[]{:S(2)}, u32[]{:S(2)}) collective-permute-start(bf16[32,2688]{1,0:T(8,128)(2,1)S(1)} %get-tuple-element.49), channel_id=1, source_target_pairs={{0,8},{4,12},{8,0},{12,4},{1,9},{5,13},{9,1},{13,5},{2,10},{6,14},... | collective-permute-start | bytes 516104 | tf_op jit(solution)/shard_map/ppermute | solution.py:252
  28.3 7.1 %collective-permute-start.6 = (bf16[128,640]{1,0:T(8,128)(2,1)S(1)}, bf16[128,640]{1,0:T(8,128)(2,1)S(1)}, u32[]{:S(2)}, u32[]{:S(2)}) collective-permute-start(bf16[128,640]{1,0:T(8,128)(2,1)S(1)} %get-tuple-element.52), channel_id=1, source_target_pairs={{0,2},{2,0},{1,3},{3,1},{4,6},{6,4},{5,7},{7,5},{8,10},{10,8},{9,1... | collective-permute-start | bytes 491528 | tf_op jit(solution)/shard_map/ppermute | solution.py:252
  30.9 8.0 %collective-permute-start.15 = (bf16[128,640]{1,0:T(8,128)(2,1)S(1)}, bf16[128,640]{1,0:T(8,128)(2,1)S(1)}, u32[]{:S(2)}, u32[]{:S(2)}) collective-permute-start(bf16[128,640]{1,0:T(8,128)(2,1)S(1)} %get-tuple-element.55), channel_id=1, source_target_pairs={{0,2},{2,0},{1,3},{3,1},{4,6},{6,4},{5,7},{7,5},{8,10},{10,8},{9,1... | collective-permute-start | bytes 491528 | tf_op jit(solution)/shard_map/ppermute | solution.py:252
  35.4 11.2 %collective-permute-start.11 = (bf16[128,640]{1,0:T(8,128)(2,1)S(1)}, bf16[128,640]{1,0:T(8,128)(2,1)S(1)}, u32[]{:S(2)}, u32[]{:S(2)}) collective-permute-start(bf16[128,640]{1,0:T(8,128)(2,1)S(1)} %add_convert_fusion.2), channel_id=1, source_target_pairs={{0,8},{4,12},{8,0},{12,4},{1,9},{5,13},{9,1},{13,5},{2,10},{6,14},... | collective-permute-start | bytes 491528 | tf_op jit(solution)/shard_map/ppermute | solution.py:252
  36.2 4.5 %collective-permute-start.7 = (bf16[64,640]{1,0:T(8,128)(2,1)S(1)}, bf16[64,640]{1,0:T(8,128)(2,1)S(1)}, u32[]{:S(2)}, u32[]{:S(2)}) collective-permute-start(bf16[64,640]{1,0:T(8,128)(2,1)S(1)} %get-tuple-element.57), channel_id=1, source_target_pairs={{0,2},{2,0},{1,3},{3,1},{4,6},{6,4},{5,7},{7,5},{8,10},{10,8},{9,1... | collective-permute-start | bytes 245768 | tf_op jit(solution)/shard_map/ppermute | solution.py:252
  37.8 5.8 %collective-permute-start.8 = (bf16[64,640]{1,0:T(8,128)(2,1)S(1)}, bf16[64,640]{1,0:T(8,128)(2,1)S(1)}, u32[]{:S(2)}, u32[]{:S(2)}) collective-permute-start(bf16[64,640]{1,0:T(8,128)(2,1)S(1)} %get-tuple-element.58), channel_id=1, source_target_pairs={{0,2},{2,0},{1,3},{3,1},{4,6},{6,4},{5,7},{7,5},{8,10},{10,8},{9,1... | collective-permute-start | bytes 245768 | tf_op jit(solution)/shard_map/ppermute | solution.py:252
  39.0 13.6 %copy-start.10 = (s32[256]{0:T(256)S(1)}, s32[256]{0:T(256)}, u32[]{:S(2)}) copy-start(s32[256]{0:T(256)} %param.9) | copy-start | bytes 3076
  39.0 9.3 %collective-permute-start.16 = (bf16[128,640]{1,0:T(8,128)(2,1)S(1)}, bf16[128,640]{1,0:T(8,128)(2,1)S(1)}, u32[]{:S(2)}, u32[]{:S(2)}) collective-permute-start(bf16[128,640]{1,0:T(8,128)(2,1)S(1)} %add_convert_fusion), channel_id=1, source_target_pairs={{0,4},{4,0},{8,12},{12,8},{1,5},{5,1},{9,13},{13,9},{2,6},{6,2},{1... | collective-permute-start | bytes 491528 | tf_op jit(solution)/shard_map/ppermute | solution.py:252
  40.7 8.5 %collective-permute-start.14 = (bf16[64,640]{1,0:T(8,128)(2,1)S(1)}, bf16[64,640]{1,0:T(8,128)(2,1)S(1)}, u32[]{:S(2)}, u32[]{:S(2)}) collective-permute-start(bf16[64,640]{1,0:T(8,128)(2,1)S(1)} %add_convert_fusion.6), channel_id=1, source_target_pairs={{0,12},{4,8},{8,4},{12,0},{1,13},{5,9},{9,5},{13,1},{2,14},{6,10},... | collective-permute-start | bytes 245768 | tf_op jit(solution)/shard_map/ppermute | solution.py:252
  43.6 6.5 %collective-permute-start.18 = (bf16[64,640]{1,0:T(8,128)(2,1)S(1)}, bf16[64,640]{1,0:T(8,128)(2,1)S(1)}, u32[]{:S(2)}, u32[]{:S(2)}) collective-permute-start(bf16[64,640]{1,0:T(8,128)(2,1)S(1)} %add_convert_fusion.5), channel_id=1, source_target_pairs={{0,12},{4,8},{8,4},{12,0},{1,13},{5,9},{9,5},{13,1},{2,14},{6,10},... | collective-permute-start | bytes 245768 | tf_op jit(solution)/shard_map/ppermute | solution.py:252
  44.7 7.6 %collective-permute-start.10 = (bf16[32,1536]{1,0:T(8,128)(2,1)S(1)}, bf16[32,1536]{1,0:T(8,128)(2,1)S(1)}, u32[]{:S(2)}, u32[]{:S(2)}) collective-permute-start(bf16[32,1536]{1,0:T(8,128)(2,1)S(1)} %pad_maximum_fusion), channel_id=1, source_target_pairs={{0,4},{4,0},{8,12},{12,8},{1,5},{5,1},{9,13},{13,9},{2,6},{6,2},{1... | collective-permute-start | bytes 294920 | tf_op jit(solution)/shard_map/ppermute | solution.py:252
  46.7 9.9 %collective-permute-start.13 = (bf16[128,640]{1,0:T(8,128)(2,1)S(1)}, bf16[128,640]{1,0:T(8,128)(2,1)S(1)}, u32[]{:S(2)}, u32[]{:S(2)}) collective-permute-start(bf16[128,640]{1,0:T(8,128)(2,1)S(1)} %get-tuple-element.77), channel_id=1, source_target_pairs={{0,2},{2,0},{1,3},{3,1},{4,6},{6,4},{5,7},{7,5},{8,10},{10,8},{9,1... | collective-permute-start | bytes 491528 | tf_op jit(solution)/shard_map/ppermute | solution.py:252
  50.2 6.4 %collective-permute-start.19 = (bf16[64,640]{1,0:T(8,128)(2,1)S(1)}, bf16[64,640]{1,0:T(8,128)(2,1)S(1)}, u32[]{:S(2)}, u32[]{:S(2)}) collective-permute-start(bf16[64,640]{1,0:T(8,128)(2,1)S(1)} %get-tuple-element.79), channel_id=1, source_target_pairs={{0,2},{2,0},{1,3},{3,1},{4,6},{6,4},{5,7},{7,5},{8,10},{10,8},{9,1... | collective-permute-start | bytes 245768 | tf_op jit(solution)/shard_map/ppermute | solution.py:252
  51.8 4.7 %collective-permute-start.17 = (bf16[64,640]{1,0:T(8,128)(2,1)S(1)}, bf16[64,640]{1,0:T(8,128)(2,1)S(1)}, u32[]{:S(2)}, u32[]{:S(2)}) collective-permute-start(bf16[64,640]{1,0:T(8,128)(2,1)S(1)} %get-tuple-element.83), channel_id=1, source_target_pairs={{0,2},{2,0},{1,3},{3,1},{4,6},{6,4},{5,7},{7,5},{8,10},{10,8},{9,1... | collective-permute-start | bytes 245768 | tf_op jit(solution)/shard_map/ppermute | solution.py:252
  52.6 1.0 %copy-start.7 = (bf16[128,1280]{1,0:T(8,128)(2,1)S(1)}, bf16[128,1280]{1,0:T(8,128)(2,1)}, u32[]{:S(2)}) copy-start(bf16[128,1280]{1,0:T(8,128)(2,1)} %refs_4_.1) | copy-start | bytes 983044
  54.5 1.3 %collective-permute-start.20 = (f32[32,640]{1,0:T(8,128)S(1)}, f32[32,640]{1,0:T(8,128)S(1)}, u32[]{:S(2)}, u32[]{:S(2)}) collective-permute-start(f32[32,640]{1,0:T(8,128)S(1)} %get-tuple-element.76), channel_id=1, source_target_pairs={{0,1},{1,0},{2,3},{3,2},{4,5},{5,4},{6,7},{7,6},{8,9},{9,8},{10,11... | collective-permute-start | bytes 245768 | tf_op jit(solution)/shard_map/ppermute | solution.py:252

commit v6 on v5

--- a/solution.py
+++ b/solution.py
@@ -334,7 +334,7 @@
 
     post(top, letter)
     term = adapter_rows(core, ids, low_out, down_t)
-    hand_on(range(top, n), low, *parts[0])
+    hand_on(range(top, n), card, *parts[0])
     order = [*range(top, n - 1), *range(1, top)]
     ready = [letter]
     for s in order:

time: 57.9 us -> 57.4 us (level)
  no operation moved by 1% of the time
where the time goes in v6:
time: 57.4 us; the launch traced here: 57.1 us
  starting transfers between devices  26.3 us (46%)
  waiting for transfers between devices  14.2 us (25%)
  Pallas kernels  8.85 us (15%)
  local copies, waits for them, and re-layouts  4.81 us (8%)
  other arithmetic  2.15 us (4%)
  between operations  0.89 us (2%)
    ppermute x21, starting transfers between devices, swap(): return lax.ppermute(value, axis, [(i, i ^ step) for i in range(size)])  26.3 us
    ppermute x21, waiting for transfers between devices, swap(): return lax.ppermute(value, axis, [(i, i ^ step) for i in range(size)])  14.2 us
    pallas_call x12, Pallas kernels, call(): pl.pallas_call(body, out_shape=out_shape, in_specs=in_specs, out_specs=ou...  8.85 us
    unnamed x22, local copies, waits for them, and re-layouts  4.78 us
  transfers between devices with their start and end apart: 21, of which 9 were waited for; matrix products, arithmetic and copies ran while one was open for 4% of the time, Pallas kernels for 14%

profile of v6, /device:TPU:0, one launch (start us, length us, event | category | flops | bytes accessed | tf_op | source)
XLA Modules:
  0.0 57.1 jit_solution(13996970976961374244)
XLA Ops:
  0.6 0.5 collective-permute-start
  1.1 3.7 %collective-permute-start.2 = (bf16[128,1280]{1,0:T(8,128)(2,1)}, bf16[128,1280]{1,0:T(8,128)(2,1)S(1)}, u32[]{:S(2)}, u32[]{:S(2)}) collective-permute-start(bf16[128,1280]{1,0:T(8,128)(2,1)} %refs_4_.1), channel_id=1, source_target_pairs={{0,8},{4,12},{8,0},{12,4},{1,9},{5,13},{9,1},{13,5},{2,10},{6,14},... | collective-permute-start | bytes 983048 | tf_op jit(solution)/shard_map/ppermute | solution.py:252
  4.8 1.6 %collective-permute-start.4 = (bf16[128,1280]{1,0:T(8,128)(2,1)}, bf16[128,1280]{1,0:T(8,128)(2,1)S(1)}, u32[]{:S(2)}, u32[]{:S(2)}) collective-permute-start(bf16[128,1280]{1,0:T(8,128)(2,1)} %refs_4_.1), channel_id=1, source_target_pairs={{0,4},{4,0},{8,12},{12,8},{1,5},{5,1},{9,13},{13,9},{2,6},{6,2},{1... | collective-permute-start | bytes 983048 | tf_op jit(solution)/shard_map/ppermute | solution.py:252
  6.4 0.0 collective-permute-done.refs_3_
  6.4 1.1 %copy-done.2 = bf16[128,2560]{1,0:T(8,128)(2,1)S(1)} copy-done((bf16[128,2560]{1,0:T(8,128)(2,1)S(1)}, bf16[128,2560]{1,0:T(8,128)(2,1)}, u32[]{:S(2)}) %copy-start.2) | copy-done | bytes 655384
  7.5 1.0 %copy-done.4 = bf16[2560,4,16]{0,2,1:T(8,128)(2,1)S(1)} copy-done((bf16[2560,4,16]{0,2,1:T(8,128)(2,1)S(1)}, bf16[2560,4,16]{0,2,1:T(8,128)(2,1)}, u32[]{:S(2)}) %copy-start.4) | copy-done | bytes 327704
  8.5 1.0 %copy-done.6 = bf16[128,1280]{1,0:T(8,128)(2,1)S(1)} copy-done((bf16[128,1280]{1,0:T(8,128)(2,1)S(1)}, bf16[128,1280]{1,0:T(8,128)(2,1)}, u32[]{:S(2)}) %copy-start.6) | copy-done | bytes 327704
  9.4 0.9 %copy-done.8 = bf16[4,16,1280]{2,1,0:T(8,128)(2,1)S(1)} copy-done((bf16[4,16,1280]{2,1,0:T(8,128)(2,1)S(1)}, bf16[4,16,1280]{2,1,0:T(8,128)(2,1)}, u32[]{:S(2)}) %copy-start.8) | copy-done | bytes 163864
  10.3 0.7 %copy-done.9 = s32[256]{0:T(256)S(1)} copy-done((s32[256]{0:T(256)S(1)}, s32[256]{0:T(256)}, u32[]{:S(2)}) %copy-start.9) | copy-done | bytes 1048
  11.0 0.5 shard_map.94.rest_0_
  11.5 1.6 %collective-permute-start.1 = (f32[32,128]{1,0:T(8,128)S(1)}, f32[32,128]{1,0:T(8,128)S(1)}, u32[]{:S(2)}, u32[]{:S(2)}) collective-permute-start(f32[32,128]{1,0:T(8,128)S(1)} %shard_map.94.rest_0_), channel_id=1, source_target_pairs={{0,2},{2,0},{1,3},{3,1},{4,6},{6,4},{5,7},{7,5},{8,10},{10,8},{9,1... | collective-permute-start | bytes 49160 | tf_op jit(solution)/shard_map/ppermute | solution.py:252
  13.1 1.1 %shard_map.96 = (bf16[128,640]{1,0:T(8,128)(2,1)S(1)}, bf16[128,640]{1,0:T(8,128)(2,1)S(1)}) custom-call(s32[1]{0:T(128)} %bitcast.9.refs_0_, bf16[128,1280]{1,0:T(8,128)(2,1)S(1)} %copy-done.6, bf16[640,1280]{1,0:T(8,128)(2,1)S(1)} %copy-done.1, bf16[640,1280]{1,0:T(8,128)(2,1)S(1)} %collective-permute-done.refs_3_), custom_call_target="tpu_custom_call" | custom-call | flops 8589934592 | bytes 33554432 | tf_op jit(solution)/shard_map/pallas_call | solution.py:34
  14.2 0.0 copy-start.5
  14.2 0.9 %collective-permute-start.12 = (bf16[128,640]{1,0:T(8,128)(2,1)S(1)}, bf16[128,640]{1,0:T(8,128)(2,1)S(1)}, u32[]{:S(2)}, u32[]{:S(2)}) collective-permute-start(bf16[128,640]{1,0:T(8,128)(2,1)S(1)} %get-tuple-element.44), channel_id=1, source_target_pairs={{0,2},{2,0},{1,3},{3,1},{4,6},{6,4},{5,7},{7,5},{8,10},{10,8},{9,1... | collective-permute-start | bytes 491528 | tf_op jit(solution)/shard_map/ppermute | solution.py:252
  15.1 0.2 collective-permute-done.1.rest_1_
  15.3 0.9 %shard_map.95 = (bf16[32,128]{1,0:T(8,128)(2,1)S(1)}, bf16[16,128]{1,0:T(8,128)(2,1)S(1)}, bf16[128,1280]{1,0:T(8,128)(2,1)S(1)}, bf16[128,1280]{1,0:T(8,128)(2,1)S(1)}) custom-call(s32[4]{0:T(128)S(1)} %copy-done, s32[1]{0:T(128)} %bitcast.4.core_ref, s32[2,128]{1,0:T(2,128)S(1)} %bitcast.30, bf16[128,2560]{1,0:T(8,128)(2,1)S(1)} %copy-done.3, ...), custom_call_target="tpu_custom_call" | custom-call | flops 8589934592 | bytes 33554432 | tf_op jit(solution)/shard_map/pallas_call | solution.py:34
  16.2 4.3 %collective-permute-done.2.refs_1_.refs_6_ = bf16[128,1280]{1,0:T(8,128)(2,1)S(1)} collective-permute-done((bf16[128,1280]{1,0:T(8,128)(2,1)}, bf16[128,1280]{1,0:T(8,128)(2,1)S(1)}, u32[]{:S(2)}, u32[]{:S(2)}) %collective-permute-start.2) | collective-permute-done | bytes 327712 | tf_op jit(solution)/shard_map/ppermute | solution.py:252
  20.5 0.7 %collective-permute-start.3 = (bf16[128,1280]{1,0:T(8,128)(2,1)S(1)}, bf16[128,1280]{1,0:T(8,128)(2,1)S(1)}, u32[]{:S(2)}, u32[]{:S(2)}) collective-permute-start(bf16[128,1280]{1,0:T(8,128)(2,1)S(1)} %collective-permute-done.2.refs_1_.refs_6_), channel_id=1, source_target_pairs={{0,4},{4,0},{8,12},{12,8},{1,5},{5,1},{9,13},{13,9},{2,6},{6,2},{1... | collective-permute-start | bytes 983048 | tf_op jit(solution)/shard_map/ppermute | solution.py:252
  21.2 0.0 collective-permute-start.5
  21.2 0.4 shard_map.103.refs_7_
  21.6 0.0 collective-permute-done.12
  21.6 1.2 %collective-permute-done.5.got_ref = bf16[128,1280]{1,0:T(8,128)(2,1)S(1)} collective-permute-done((bf16[128,1280]{1,0:T(8,128)(2,1)S(1)}, bf16[128,1280]{1,0:T(8,128)(2,1)S(1)}, u32[]{:S(2)}, u32[]{:S(2)}) %collective-permute-start.5) | collective-permute-done | bytes 327712 | tf_op jit(solution)/shard_map/ppermute | solution.py:252
  22.8 0.1 shard_map.97
  22.9 3.3 %collective-permute-start.9 = (bf16[32,2688]{1,0:T(8,128)(2,1)S(1)}, bf16[32,2688]{1,0:T(8,128)(2,1)S(1)}, u32[]{:S(2)}, u32[]{:S(2)}) collective-permute-start(bf16[32,2688]{1,0:T(8,128)(2,1)S(1)} %get-tuple-element.49), channel_id=1, source_target_pairs={{0,8},{4,12},{8,0},{12,4},{1,9},{5,13},{9,1},{13,5},{2,10},{6,14},... | collective-permute-start | bytes 516104 | tf_op jit(solution)/shard_map/ppermute | solution.py:252
  26.2 1.1 %shard_map.98 = (bf16[128,640]{1,0:T(8,128)(2,1)S(1)}, bf16[128,640]{1,0:T(8,128)(2,1)S(1)}) custom-call(s32[1]{0:T(128)} %bitcast.9.refs_0_, bf16[128,1280]{1,0:T(8,128)(2,1)S(1)} %collective-permute-done.2.refs_1_.refs_6_, bf16[640,1280]{1,0:T(8,128)(2,1)S(1)} %copy-done.1, bf16[640,1280]{1,0:T(8,128)(2,1)S(1)} %collective-permute-done.refs_3_), custom_call_target="tpu_custom_call" | custom-call | flops 8589934592 | bytes 33554432 | tf_op jit(solution)/shard_map/pallas_call | solution.py:34
  27.3 1.6 %collective-permute-start.6 = (bf16[128,640]{1,0:T(8,128)(2,1)S(1)}, bf16[128,640]{1,0:T(8,128)(2,1)S(1)}, u32[]{:S(2)}, u32[]{:S(2)}) collective-permute-start(bf16[128,640]{1,0:T(8,128)(2,1)S(1)} %get-tuple-element.52), channel_id=1, source_target_pairs={{0,2},{2,0},{1,3},{3,1},{4,6},{6,4},{5,7},{7,5},{8,10},{10,8},{9,1... | collective-permute-start | bytes 491528 | tf_op jit(solution)/shard_map/ppermute | solution.py:252
  28.9 0.0 collective-permute-done.4.refs_1_.refs_5_
  28.9 1.1 %shard_map.99 = (bf16[128,640]{1,0:T(8,128)(2,1)S(1)}, bf16[128,640]{1,0:T(8,128)(2,1)S(1)}) custom-call(s32[1]{0:T(128)} %bitcast.9.refs_0_, bf16[128,1280]{1,0:T(8,128)(2,1)S(1)} %collective-permute-done.4.refs_1_.refs_5_, bf16[640,1280]{1,0:T(8,128)(2,1)S(1)} %copy-done.1, bf16[640,1280]{1,0:T(8,128)(2,1)S(1)} %collective-permute-done.refs_3_), custom_call_target="tpu_custom_call" | custom-call | flops 8589934592 | bytes 33554432 | tf_op jit(solution)/shard_map/pallas_call | solution.py:34
  30.0 0.6 %collective-permute-start.15 = (bf16[128,640]{1,0:T(8,128)(2,1)S(1)}, bf16[128,640]{1,0:T(8,128)(2,1)S(1)}, u32[]{:S(2)}, u32[]{:S(2)}) collective-permute-start(bf16[128,640]{1,0:T(8,128)(2,1)S(1)} %get-tuple-element.55), channel_id=1, source_target_pairs={{0,2},{2,0},{1,3},{3,1},{4,6},{6,4},{5,7},{7,5},{8,10},{10,8},{9,1... | collective-permute-start | bytes 491528 | tf_op jit(solution)/shard_map/ppermute | solution.py:252
  30.6 3.9 %collective-permute-done.6 = bf16[128,640]{1,0:T(8,128)(2,1)S(1)} collective-permute-done((bf16[128,640]{1,0:T(8,128)(2,1)S(1)}, bf16[128,640]{1,0:T(8,128)(2,1)S(1)}, u32[]{:S(2)}, u32[]{:S(2)}) %collective-permute-start.6) | collective-permute-done | bytes 163872 | tf_op jit(solution)/shard_map/ppermute | solution.py:252
  34.5 0.1 collective-permute-start.11
  34.6 0.0 collective-permute-done.3.refs_1_.refs_7_
  34.6 0.7 %shard_map.100 = (bf16[64,640]{1,0:T(8,128)(2,1)S(1)}, bf16[64,640]{1,0:T(8,128)(2,1)S(1)}) custom-call(s32[1]{0:T(128)} %bitcast.9.refs_0_, bf16[128,1280]{1,0:T(8,128)(2,1)S(1)} %collective-permute-done.3.refs_1_.refs_7_, bf16[640,1280]{1,0:T(8,128)(2,1)S(1)} %copy-done.1, bf16[640,1280]{1,0:T(8,128)(2,1)S(1)} %collective-permute-done.refs_3_), custom_call_target="tpu_custom_call" | custom-call | flops 8589934592 | bytes 33554432 | tf_op jit(solution)/shard_map/pallas_call | solution.py:34
  35.3 1.6 %collective-permute-start.7 = (bf16[64,640]{1,0:T(8,128)(2,1)S(1)}, bf16[64,640]{1,0:T(8,128)(2,1)S(1)}, u32[]{:S(2)}, u32[]{:S(2)}) collective-permute-start(bf16[64,640]{1,0:T(8,128)(2,1)S(1)} %get-tuple-element.57), channel_id=1, source_target_pairs={{0,2},{2,0},{1,3},{3,1},{4,6},{6,4},{5,7},{7,5},{8,10},{10,8},{9,1... | collective-permute-start | bytes 245768 | tf_op jit(solution)/shard_map/ppermute | solution.py:252
  36.8 0.5 collective-permute-start.8
  37.4 0.6 %shard_map.101 = (bf16[64,640]{1,0:T(8,128)(2,1)S(1)}, bf16[64,640]{1,0:T(8,128)(2,1)S(1)}) custom-call(s32[1]{0:T(128)} %bitcast.9.refs_0_, bf16[128,1280]{1,0:T(8,128)(2,1)S(1)} %collective-permute-done.3.refs_1_.refs_7_, bf16[640,1280]{1,0:T(8,128)(2,1)S(1)} %copy-done.1, bf16[640,1280]{1,0:T(8,128)(2,1)S(1)} %collective-permute-done.refs_3_), custom_call_target="tpu_custom_call" | custom-call | flops 8589934592 | bytes 33554432 | tf_op jit(solution)/shard_map/pallas_call | solution.py:34
  38.1 0.0 copy-start.10
  38.1 0.9 %collective-permute-start.16 = (bf16[128,640]{1,0:T(8,128)(2,1)S(1)}, bf16[128,640]{1,0:T(8,128)(2,1)S(1)}, u32[]{:S(2)}, u32[]{:S(2)}) collective-permute-start(bf16[128,640]{1,0:T(8,128)(2,1)S(1)} %add_convert_fusion), channel_id=1, source_target_pairs={{0,4},{4,0},{8,12},{12,8},{1,5},{5,1},{9,13},{13,9},{2,6},{6,2},{1... | collective-permute-start | bytes 491528 | tf_op jit(solution)/shard_map/ppermute | solution.py:252
  39.0 0.0 collective-permute-done.9
  39.0 0.7 %collective-permute-done.7 = bf16[64,640]{1,0:T(8,128)(2,1)S(1)} collective-permute-done((bf16[64,640]{1,0:T(8,128)(2,1)S(1)}, bf16[64,640]{1,0:T(8,128)(2,1)S(1)}, u32[]{:S(2)}, u32[]{:S(2)}) %collective-permute-start.7) | collective-permute-done | bytes 81952 | tf_op jit(solution)/shard_map/ppermute | solution.py:252
  39.8 3.5 %collective-permute-start.14 = (bf16[64,640]{1,0:T(8,128)(2,1)S(1)}, bf16[64,640]{1,0:T(8,128)(2,1)S(1)}, u32[]{:S(2)}, u32[]{:S(2)}) collective-permute-start(bf16[64,640]{1,0:T(8,128)(2,1)S(1)} %add_convert_fusion.6), channel_id=1, source_target_pairs={{0,12},{4,8},{8,4},{12,0},{1,13},{5,9},{9,5},{13,1},{2,14},{6,10},... | collective-permute-start | bytes 245768 | tf_op jit(solution)/shard_map/ppermute | solution.py:252
  43.3 0.0 collective-permute-done.8
  43.4 1.4 %collective-permute-start.18 = (bf16[64,640]{1,0:T(8,128)(2,1)S(1)}, bf16[64,640]{1,0:T(8,128)(2,1)S(1)}, u32[]{:S(2)}, u32[]{:S(2)}) collective-permute-start(bf16[64,640]{1,0:T(8,128)(2,1)S(1)} %add_convert_fusion.5), channel_id=1, source_target_pairs={{0,12},{4,8},{8,4},{12,0},{1,13},{5,9},{9,5},{13,1},{2,14},{6,10},... | collective-permute-start | bytes 245768 | tf_op jit(solution)/shard_map/ppermute | solution.py:252
  44.8 0.0 collective-permute-start.10
  44.9 1.5 %collective-permute-start.13 = (bf16[128,640]{1,0:T(8,128)(2,1)S(1)}, bf16[128,640]{1,0:T(8,128)(2,1)S(1)}, u32[]{:S(2)}, u32[]{:S(2)}) collective-permute-start(bf16[128,640]{1,0:T(8,128)(2,1)S(1)} %get-tuple-element.77), channel_id=1, source_target_pairs={{0,2},{2,0},{1,3},{3,1},{4,6},{6,4},{5,7},{7,5},{8,10},{10,8},{9,1... | collective-permute-start | bytes 491528 | tf_op jit(solution)/shard_map/ppermute | solution.py:252
  46.4 1.2 %collective-permute-done.16 = bf16[128,640]{1,0:T(8,128)(2,1)S(1)} collective-permute-done((bf16[128,640]{1,0:T(8,128)(2,1)S(1)}, bf16[128,640]{1,0:T(8,128)(2,1)S(1)}, u32[]{:S(2)}, u32[]{:S(2)}) %collective-permute-start.16) | collective-permute-done | bytes 163872 | tf_op jit(solution)/shard_map/ppermute | solution.py:252
  47.6 0.9 %collective-permute-done.14 = bf16[64,640]{1,0:T(8,128)(2,1)S(1)} collective-permute-done((bf16[64,640]{1,0:T(8,128)(2,1)S(1)}, bf16[64,640]{1,0:T(8,128)(2,1)S(1)}, u32[]{:S(2)}, u32[]{:S(2)}) %collective-permute-start.14) | collective-permute-done | bytes 81952 | tf_op jit(solution)/shard_map/ppermute | solution.py:252
  48.6 1.1 %collective-permute-done.18 = bf16[64,640]{1,0:T(8,128)(2,1)S(1)} collective-permute-done((bf16[64,640]{1,0:T(8,128)(2,1)S(1)}, bf16[64,640]{1,0:T(8,128)(2,1)S(1)}, u32[]{:S(2)}, u32[]{:S(2)}) %collective-permute-start.18) | collective-permute-done | bytes 81952 | tf_op jit(solution)/shard_map/ppermute | solution.py:252
  49.7 1.5 %collective-permute-start.19 = (bf16[64,640]{1,0:T(8,128)(2,1)S(1)}, bf16[64,640]{1,0:T(8,128)(2,1)S(1)}, u32[]{:S(2)}, u32[]{:S(2)}) collective-permute-start(bf16[64,640]{1,0:T(8,128)(2,1)S(1)} %get-tuple-element.79), channel_id=1, source_target_pairs={{0,2},{2,0},{1,3},{3,1},{4,6},{6,4},{5,7},{7,5},{8,10},{10,8},{9,1... | collective-permute-start | bytes 245768 | tf_op jit(solution)/shard_map/ppermute | solution.py:252
  51.3 0.6 %collective-permute-start.17 = (bf16[64,640]{1,0:T(8,128)(2,1)S(1)}, bf16[64,640]{1,0:T(8,128)(2,1)S(1)}, u32[]{:S(2)}, u32[]{:S(2)}) collective-permute-start(bf16[64,640]{1,0:T(8,128)(2,1)S(1)} %get-tuple-element.83), channel_id=1, source_target_pairs={{0,2},{2,0},{1,3},{3,1},{4,6},{6,4},{5,7},{7,5},{8,10},{10,8},{9,1... | collective-permute-start | bytes 245768 | tf_op jit(solution)/shard_map/ppermute | solution.py:252
  51.9 0.0 collective-permute-done.10
  52.0 0.1 convert_reduce_fusion
  52.2 0.0 copy-start.7
  52.2 0.6 %shard_map.102.refs_6_ = f32[128,128]{1,0:T(8,128)S(1)} custom-call(f32[4]{0:T(128)S(1)} %multiply_divide_fusion.weight_ref, s32[1]{0:T(128)} %bitcast.4.core_ref, s32[2,128]{1,0:T(2,128)S(1)} %bitcast.32), custom_call_target="tpu_custom_call" | custom-call | flops 8589934592 | bytes 33554432 | tf_op jit(solution)/shard_map/pallas_call | solution.py:34
  52.8 0.2 fusion
  53.0 0.1 copy-done.7
  53.1 0.9 %shard_map.105 = (f32[32,640]{1,0:T(8,128)S(1)}, f32[32,640]{1,0:T(8,128)S(1)}) custom-call(s32[4]{0:T(128)S(1)} %copy-done, s32[1]{0:T(128)} %bitcast.4.core_ref, s32[1]{0:T(128)} %bitcast.10.place_ref, bf16[32,128]{1,0:T(8,128)(2,1)S(1)} %get-tuple-element.63.card_ref.refs_0_, bf16[32,128]{1,0:T(8,128)(2,1)S(1)} %get-tuple-element.66.refs_1_, ...), custom_call_target="tpu_custom_call" | custom-call | flops 8589934592 | bytes 33554432 | tf_op jit(solution)/shard_map/pallas_call | solution.py:34
  54.0 0.1 collective-permute-start.20
  54.1 0.7 %multiply_bitcast_fusion = f32[1280,2,16]{0,2,1:T(8,128)} fusion(f32[2,16,1280]{2,1,0:T(8,128)S(1)} %bitcast.33, f32[2]{0:T(128)S(1)} %broadcast_multiply_fusion.1), kind=kLoop, calls=%fused_computation.3 | loop fusion | flops 40960 | bytes 327688 | tf_op jit(solution)/shard_map/transpose | solution.py:367
  54.9 0.5 collective-permute-done.20
  55.4 0.7 %broadcast_multiply_fusion = f32[2,16,640]{2,1,0:T(8,128)} fusion(f32[2,16,640]{2,1,0:T(8,128)S(1)} %bitcast.34, f32[2]{0:T(128)S(1)} %broadcast_multiply_fusion.1), kind=kLoop, calls=%fused_computation.16 | loop fusion | flops 20480 | bytes 163848 | tf_op jit(solution)/shard_map/mul | solution.py:405
  56.1 0.0 collective-permute-done.17.refs_11_
  56.1 0.0 collective-permute-done.13.refs_9_
  56.1 1.0 %shard_map.104 = bf16[128,2560]{1,0:T(8,128)(2,1)} custom-call(s32[1]{0:T(128)} %bitcast.refs_0_, s32[1]{0:T(128)} %bitcast.1.refs_1_, s32[1]{0:T(128)} %bitcast.2.refs_2_.refs_4_, s32[1]{0:T(128)} %bitcast.3.refs_3_.refs_5_, s32[1]{0:T(128)} %bitcast.2.refs_2_.refs_4_, s32[1]{0:T(128)} %bitcast.3.refs_3_.refs_5_, f32[128,128]{1,0:T(8,128)S(1)} %shard_map.102.refs_6_, ...), custom_call_target="tpu_custom_call" | custom-call | flops 8589934592 | bytes 33554432 | tf_op jit(solution)/shard_map/pallas_call | solution.py:34
  (38 shorter events, 0.4 us)
Async XLA Ops:
  0.6 5.8 %collective-permute-start = (bf16[640,1280]{1,0:T(8,128)(2,1)}, bf16[640,1280]{1,0:T(8,128)(2,1)S(1)}, u32[]{:S(2)}, u32[]{:S(2)}) collective-permute-start(bf16[640,1280]{1,0:T(8,128)(2,1)} %refs_2_.9), channel_id=1, source_target_pairs={{0,1},{1,0},{2,3},{3,2},{4,5},{5,4},{6,7},{7,6},{8,9},{9,8},{10,11... | collective-permute-start | bytes 4915208 | tf_op jit(solution)/shard_map/ppermute | solution.py:252
  1.1 19.3 %collective-permute-start.2 = (bf16[128,1280]{1,0:T(8,128)(2,1)}, bf16[128,1280]{1,0:T(8,128)(2,1)S(1)}, u32[]{:S(2)}, u32[]{:S(2)}) collective-permute-start(bf16[128,1280]{1,0:T(8,128)(2,1)} %refs_4_.1), channel_id=1, source_target_pairs={{0,8},{4,12},{8,0},{12,4},{1,9},{5,13},{9,1},{13,5},{2,10},{6,14},... | collective-permute-start | bytes 983048 | tf_op jit(solution)/shard_map/ppermute | solution.py:252
  4.8 24.1 %collective-permute-start.4 = (bf16[128,1280]{1,0:T(8,128)(2,1)}, bf16[128,1280]{1,0:T(8,128)(2,1)S(1)}, u32[]{:S(2)}, u32[]{:S(2)}) collective-permute-start(bf16[128,1280]{1,0:T(8,128)(2,1)} %refs_4_.1), channel_id=1, source_target_pairs={{0,4},{4,0},{8,12},{12,8},{1,5},{5,1},{9,13},{13,9},{2,6},{6,2},{1... | collective-permute-start | bytes 983048 | tf_op jit(solution)/shard_map/ppermute | solution.py:252
  6.4 1.1 %copy-start.2 = (bf16[128,2560]{1,0:T(8,128)(2,1)S(1)}, bf16[128,2560]{1,0:T(8,128)(2,1)}, u32[]{:S(2)}) copy-start(bf16[128,2560]{1,0:T(8,128)(2,1)} %x_ref.3) | copy-start | bytes 1966084
  7.5 1.0 %copy-start.4 = (bf16[2560,4,16]{0,2,1:T(8,128)(2,1)S(1)}, bf16[2560,4,16]{0,2,1:T(8,128)(2,1)}, u32[]{:S(2)}) copy-start(bf16[2560,4,16]{0,2,1:T(8,128)(2,1)} %param.12) | copy-start | bytes 983044
  8.5 1.0 %copy-start.6 = (bf16[128,1280]{1,0:T(8,128)(2,1)S(1)}, bf16[128,1280]{1,0:T(8,128)(2,1)}, u32[]{:S(2)}) copy-start(bf16[128,1280]{1,0:T(8,128)(2,1)} %refs_4_.1) | copy-start | bytes 983044
  9.4 0.9 %copy-start.8 = (bf16[4,16,1280]{2,1,0:T(8,128)(2,1)S(1)}, bf16[4,16,1280]{2,1,0:T(8,128)(2,1)}, u32[]{:S(2)}) copy-start(bf16[4,16,1280]{2,1,0:T(8,128)(2,1)} %param.13) | copy-start | bytes 491524
  10.3 0.7 %copy-start.9 = (s32[256]{0:T(256)S(1)}, s32[256]{0:T(256)}, u32[]{:S(2)}) copy-start(s32[256]{0:T(256)} %param.9) | copy-start | bytes 3076
  11.0 2.0 %copy-start.1 = (bf16[640,1280]{1,0:T(8,128)(2,1)S(1)}, bf16[640,1280]{1,0:T(8,128)(2,1)}, u32[]{:S(2)}) copy-start(bf16[640,1280]{1,0:T(8,128)(2,1)} %refs_2_.9) | copy-start | bytes 4915204
  11.5 3.8 %collective-permute-start.1 = (f32[32,128]{1,0:T(8,128)S(1)}, f32[32,128]{1,0:T(8,128)S(1)}, u32[]{:S(2)}, u32[]{:S(2)}) collective-permute-start(f32[32,128]{1,0:T(8,128)S(1)} %shard_map.94.rest_0_), channel_id=1, source_target_pairs={{0,2},{2,0},{1,3},{3,1},{4,6},{6,4},{5,7},{7,5},{8,10},{10,8},{9,1... | collective-permute-start | bytes 49160 | tf_op jit(solution)/shard_map/ppermute | solution.py:252
  13.1 2.2 %copy-start = (s32[4]{0:T(128)S(1)}, s32[4]{0:T(128)}, u32[]{:S(2)}) copy-start(s32[4]{0:T(128)} %slot_ref.3) | copy-start | bytes 52
  13.1 2.2 %copy-start.3 = (bf16[128,2560]{1,0:T(8,128)(2,1)S(1)}, bf16[128,2560]{1,0:T(8,128)(2,1)}, u32[]{:S(2)}) copy-start(bf16[128,2560]{1,0:T(8,128)(2,1)} %x_ref.3) | copy-start | bytes 1966084
  14.2 7.0 %copy-start.5 = (bf16[2560,4,16]{0,2,1:T(8,128)(2,1)S(1)}, bf16[2560,4,16]{0,2,1:T(8,128)(2,1)}, u32[]{:S(2)}) copy-start(bf16[2560,4,16]{0,2,1:T(8,128)(2,1)} %param.12) | copy-start | bytes 983044
  14.2 7.4 %collective-permute-start.12 = (bf16[128,640]{1,0:T(8,128)(2,1)S(1)}, bf16[128,640]{1,0:T(8,128)(2,1)S(1)}, u32[]{:S(2)}, u32[]{:S(2)}) collective-permute-start(bf16[128,640]{1,0:T(8,128)(2,1)S(1)} %get-tuple-element.44), channel_id=1, source_target_pairs={{0,2},{2,0},{1,3},{3,1},{4,6},{6,4},{5,7},{7,5},{8,10},{10,8},{9,1... | collective-permute-start | bytes 491528 | tf_op jit(solution)/shard_map/ppermute | solution.py:252
  20.5 14.2 %collective-permute-start.3 = (bf16[128,1280]{1,0:T(8,128)(2,1)S(1)}, bf16[128,1280]{1,0:T(8,128)(2,1)S(1)}, u32[]{:S(2)}, u32[]{:S(2)}) collective-permute-start(bf16[128,1280]{1,0:T(8,128)(2,1)S(1)} %collective-permute-done.2.refs_1_.refs_6_), channel_id=1, source_target_pairs={{0,4},{4,0},{8,12},{12,8},{1,5},{5,1},{9,13},{13,9},{2,6},{6,2},{1... | collective-permute-start | bytes 983048 | tf_op jit(solution)/shard_map/ppermute | solution.py:252
  21.2 1.6 %collective-permute-start.5 = (bf16[128,1280]{1,0:T(8,128)(2,1)S(1)}, bf16[128,1280]{1,0:T(8,128)(2,1)S(1)}, u32[]{:S(2)}, u32[]{:S(2)}) collective-permute-start(bf16[128,1280]{1,0:T(8,128)(2,1)S(1)} %get-tuple-element.48), channel_id=1, source_target_pairs={{0,1},{1,0},{2,3},{3,2},{4,5},{5,4},{6,7},{7,6},{8,9},{9,8},{10,11... | collective-permute-start | bytes 983048 | tf_op jit(solution)/shard_map/ppermute | solution.py:252
  22.9 16.1 %collective-permute-start.9 = (bf16[32,2688]{1,0:T(8,128)(2,1)S(1)}, bf16[32,2688]{1,0:T(8,128)(2,1)S(1)}, u32[]{:S(2)}, u32[]{:S(2)}) collective-permute-start(bf16[32,2688]{1,0:T(8,128)(2,1)S(1)} %get-tuple-element.49), channel_id=1, source_target_pairs={{0,8},{4,12},{8,0},{12,4},{1,9},{5,13},{9,1},{13,5},{2,10},{6,14},... | collective-permute-start | bytes 516104 | tf_op jit(solution)/shard_map/ppermute | solution.py:252
  27.3 7.2 %collective-permute-start.6 = (bf16[128,640]{1,0:T(8,128)(2,1)S(1)}, bf16[128,640]{1,0:T(8,128)(2,1)S(1)}, u32[]{:S(2)}, u32[]{:S(2)}) collective-permute-start(bf16[128,640]{1,0:T(8,128)(2,1)S(1)} %get-tuple-element.52), channel_id=1, source_target_pairs={{0,2},{2,0},{1,3},{3,1},{4,6},{6,4},{5,7},{7,5},{8,10},{10,8},{9,1... | collective-permute-start | bytes 491528 | tf_op jit(solution)/shard_map/ppermute | solution.py:252
  30.0 8.0 %collective-permute-start.15 = (bf16[128,640]{1,0:T(8,128)(2,1)S(1)}, bf16[128,640]{1,0:T(8,128)(2,1)S(1)}, u32[]{:S(2)}, u32[]{:S(2)}) collective-permute-start(bf16[128,640]{1,0:T(8,128)(2,1)S(1)} %get-tuple-element.55), channel_id=1, source_target_pairs={{0,2},{2,0},{1,3},{3,1},{4,6},{6,4},{5,7},{7,5},{8,10},{10,8},{9,1... | collective-permute-start | bytes 491528 | tf_op jit(solution)/shard_map/ppermute | solution.py:252
  34.5 10.3 %collective-permute-start.11 = (bf16[128,640]{1,0:T(8,128)(2,1)S(1)}, bf16[128,640]{1,0:T(8,128)(2,1)S(1)}, u32[]{:S(2)}, u32[]{:S(2)}) collective-permute-start(bf16[128,640]{1,0:T(8,128)(2,1)S(1)} %add_convert_fusion.2), channel_id=1, source_target_pairs={{0,8},{4,12},{8,0},{12,4},{1,9},{5,13},{9,1},{13,5},{2,10},{6,14},... | collective-permute-start | bytes 491528 | tf_op jit(solution)/shard_map/ppermute | solution.py:252
  35.3 4.5 %collective-permute-start.7 = (bf16[64,640]{1,0:T(8,128)(2,1)S(1)}, bf16[64,640]{1,0:T(8,128)(2,1)S(1)}, u32[]{:S(2)}, u32[]{:S(2)}) collective-permute-start(bf16[64,640]{1,0:T(8,128)(2,1)S(1)} %get-tuple-element.57), channel_id=1, source_target_pairs={{0,2},{2,0},{1,3},{3,1},{4,6},{6,4},{5,7},{7,5},{8,10},{10,8},{9,1... | collective-permute-start | bytes 245768 | tf_op jit(solution)/shard_map/ppermute | solution.py:252
  36.8 6.5 %collective-permute-start.8 = (bf16[64,640]{1,0:T(8,128)(2,1)S(1)}, bf16[64,640]{1,0:T(8,128)(2,1)S(1)}, u32[]{:S(2)}, u32[]{:S(2)}) collective-permute-start(bf16[64,640]{1,0:T(8,128)(2,1)S(1)} %get-tuple-element.58), channel_id=1, source_target_pairs={{0,2},{2,0},{1,3},{3,1},{4,6},{6,4},{5,7},{7,5},{8,10},{10,8},{9,1... | collective-permute-start | bytes 245768 | tf_op jit(solution)/shard_map/ppermute | solution.py:252
  38.1 14.1 %copy-start.10 = (s32[256]{0:T(256)S(1)}, s32[256]{0:T(256)}, u32[]{:S(2)}) copy-start(s32[256]{0:T(256)} %param.9) | copy-start | bytes 3076
  38.1 9.5 %collective-permute-start.16 = (bf16[128,640]{1,0:T(8,128)(2,1)S(1)}, bf16[128,640]{1,0:T(8,128)(2,1)S(1)}, u32[]{:S(2)}, u32[]{:S(2)}) collective-permute-start(bf16[128,640]{1,0:T(8,128)(2,1)S(1)} %add_convert_fusion), channel_id=1, source_target_pairs={{0,4},{4,0},{8,12},{12,8},{1,5},{5,1},{9,13},{13,9},{2,6},{6,2},{1... | collective-permute-start | bytes 491528 | tf_op jit(solution)/shard_map/ppermute | solution.py:252
  39.8 8.8 %collective-permute-start.14 = (bf16[64,640]{1,0:T(8,128)(2,1)S(1)}, bf16[64,640]{1,0:T(8,128)(2,1)S(1)}, u32[]{:S(2)}, u32[]{:S(2)}) collective-permute-start(bf16[64,640]{1,0:T(8,128)(2,1)S(1)} %add_convert_fusion.6), channel_id=1, source_target_pairs={{0,12},{4,8},{8,4},{12,0},{1,13},{5,9},{9,5},{13,1},{2,14},{6,10},... | collective-permute-start | bytes 245768 | tf_op jit(solution)/shard_map/ppermute | solution.py:252
  43.4 6.4 %collective-permute-start.18 = (bf16[64,640]{1,0:T(8,128)(2,1)S(1)}, bf16[64,640]{1,0:T(8,128)(2,1)S(1)}, u32[]{:S(2)}, u32[]{:S(2)}) collective-permute-start(bf16[64,640]{1,0:T(8,128)(2,1)S(1)} %add_convert_fusion.5), channel_id=1, source_target_pairs={{0,12},{4,8},{8,4},{12,0},{1,13},{5,9},{9,5},{13,1},{2,14},{6,10},... | collective-permute-start | bytes 245768 | tf_op jit(solution)/shard_map/ppermute | solution.py:252
  44.8 7.1 %collective-permute-start.10 = (bf16[32,1536]{1,0:T(8,128)(2,1)S(1)}, bf16[32,1536]{1,0:T(8,128)(2,1)S(1)}, u32[]{:S(2)}, u32[]{:S(2)}) collective-permute-start(bf16[32,1536]{1,0:T(8,128)(2,1)S(1)} %pad_maximum_fusion), channel_id=1, source_target_pairs={{0,4},{4,0},{8,12},{12,8},{1,5},{5,1},{9,13},{13,9},{2,6},{6,2},{1... | collective-permute-start | bytes 294920 | tf_op jit(solution)/shard_map/ppermute | solution.py:252
  44.9 11.2 %collective-permute-start.13 = (bf16[128,640]{1,0:T(8,128)(2,1)S(1)}, bf16[128,640]{1,0:T(8,128)(2,1)S(1)}, u32[]{:S(2)}, u32[]{:S(2)}) collective-permute-start(bf16[128,640]{1,0:T(8,128)(2,1)S(1)} %get-tuple-element.77), channel_id=1, source_target_pairs={{0,2},{2,0},{1,3},{3,1},{4,6},{6,4},{5,7},{7,5},{8,10},{10,8},{9,1... | collective-permute-start | bytes 491528 | tf_op jit(solution)/shard_map/ppermute | solution.py:252
  49.7 6.4 %collective-permute-start.19 = (bf16[64,640]{1,0:T(8,128)(2,1)S(1)}, bf16[64,640]{1,0:T(8,128)(2,1)S(1)}, u32[]{:S(2)}, u32[]{:S(2)}) collective-permute-start(bf16[64,640]{1,0:T(8,128)(2,1)S(1)} %get-tuple-element.79), channel_id=1, source_target_pairs={{0,2},{2,0},{1,3},{3,1},{4,6},{6,4},{5,7},{7,5},{8,10},{10,8},{9,1... | collective-permute-start | bytes 245768 | tf_op jit(solution)/shard_map/ppermute | solution.py:252
  51.3 4.8 %collective-permute-start.17 = (bf16[64,640]{1,0:T(8,128)(2,1)S(1)}, bf16[64,640]{1,0:T(8,128)(2,1)S(1)}, u32[]{:S(2)}, u32[]{:S(2)}) collective-permute-start(bf16[64,640]{1,0:T(8,128)(2,1)S(1)} %get-tuple-element.83), channel_id=1, source_target_pairs={{0,2},{2,0},{1,3},{3,1},{4,6},{6,4},{5,7},{7,5},{8,10},{10,8},{9,1... | collective-permute-start | bytes 245768 | tf_op jit(solution)/shard_map/ppermute | solution.py:252
  52.2 1.0 %copy-start.7 = (bf16[128,1280]{1,0:T(8,128)(2,1)S(1)}, bf16[128,1280]{1,0:T(8,128)(2,1)}, u32[]{:S(2)}) copy-start(bf16[128,1280]{1,0:T(8,128)(2,1)} %refs_4_.1) | copy-start | bytes 983044
  54.0 1.3 %collective-permute-start.20 = (f32[32,640]{1,0:T(8,128)S(1)}, f32[32,640]{1,0:T(8,128)S(1)}, u32[]{:S(2)}, u32[]{:S(2)}) collective-permute-start(f32[32,640]{1,0:T(8,128)S(1)} %get-tuple-element.76), channel_id=1, source_target_pairs={{0,1},{1,0},{2,3},{3,2},{4,5},{5,4},{6,7},{7,6},{8,9},{9,8},{10,11... | collective-permute-start | bytes 245768 | tf_op jit(solution)/shard_map/ppermute | solution.py:252

commit v7 on v6

--- a/solution.py
+++ b/solution.py
@@ -193,50 +193,44 @@
     rows, width = ids.shape[1], down_t.shape[1]
     adapters = down_t.shape[0] // low_out.shape[0]
 
-    def body(core_ref, ids_ref, low_ref, down_ref, out_ref):
+    def body(core_ref, ids_ref, low_ref, down_ref, out_ref, column_ref):
         own_ids = ids_ref[pl.ds(core_ref[0], 1), :]
         low = low_ref[...].astype(F32)
         spread = [jnp.where(own_ids == a, low, 0.0) for a in range(adapters)]
         spread = jnp.concatenate(spread, axis=0).T.astype(BF16)
         out_ref[...] = ADAPTER_SCALE * dot_plain(spread, down_ref[...])
-
-    return call(body, array((rows, width), F32), [core, ids, low_out, down_t], {0: SMEM})
-
-
-def row_scales(weight, core, ids):
-    rows = ids.shape[1]
-
-    def body(weight_ref, core_ref, ids_ref, out_ref):
-        own_ids = ids_ref[pl.ds(core_ref[0], 1), :]
-        scale = jnp.zeros(own_ids.shape, F32)
-        for a in range(weight.shape[0]):
-            scale = jnp.where(own_ids == a, weight_ref[a], scale)
-        out_ref[...] = jnp.broadcast_to(scale, (rows, rows)).T
-
-    return call(body, array((rows, rows), F32), [weight, core, ids], {0: SMEM, 1: SMEM})
-
-
-def finish(scale, term, pieces, offsets, starts, into=None):
+        column_ref[...] = jnp.broadcast_to(own_ids.astype(F32), (rows, rows)).T
+
+    shapes = [array((rows, width), F32), array((rows, rows), F32)]
+    return call(body, shapes, [core, ids, low_out, down_t], {0: SMEM})
+
+
+def finish(weight, id_column, term, pieces, offsets, starts, into=None):
     count = len(pieces)
 
     def body(*refs):
-        offset_refs, (scale_ref, term_ref) = refs[:count], refs[count : count + 2]
-        piece_refs = refs[count + 2 : 2 * count + 2]
+        weight_ref, column_ref, *refs = refs
+        offset_refs, term_ref = refs[:count], refs[count]
+        piece_refs = refs[count + 1 : 2 * count + 1]
         out_ref, *held = refs[len(refs) - count - 2 : -1]
         sems = refs[-1]
+        own_ids = column_ref[:, :1]
+        scale = jnp.zeros(own_ids.shape, F32)
+        for a in range(weight.shape[1]):
+            scale = jnp.where(own_ids == a, weight_ref[:, a : a + 1], scale)
         copies = []
         for i, (piece, start) in enumerate(zip(pieces, starts)):
             own, chunk = slice(start, start + piece.shape[0]), piece.shape[1]
             at = pl.ds(pl.multiple_of(offset_refs[i][0], 128), chunk)
             total = piece_refs[i][...].astype(F32) + term_ref[own, at]
-            held[i][...] = (scale_ref[own, :1] * total).astype(BF16)
+            held[i][...] = (scale[own] * total).astype(BF16)
             copies.append(pltpu.make_async_copy(held[i], out_ref.at[own, at], sems.at[i]))
             copies[-1].start()
         for copy in copies:
             copy.wait()
 
-    args = [*offsets, scale, term, *pieces]
-    specs = {i: SMEM for i in range(count)}
+    args = [weight, id_column, *offsets, term, *pieces]
+    specs = {i: SMEM for i in range(2, 2 + count)}
     aliases = None
     if into is not None:
         specs[len(args)] = ANY
@@ -333,7 +327,7 @@
             cards[s ^ bit] = got[:, at : at + rows]
 
     post(top, letter)
-    term = adapter_rows(core, ids, low_out, down_t)
+    term, id_column = adapter_rows(core, ids, low_out, down_t)
     hand_on(range(top, n), card, *parts[0])
     order = [*range(top, n - 1), *range(1, top)]
     ready = [letter]
@@ -386,7 +380,7 @@
                 starts.append(start)
     if chunk % 128 == 0:
         offsets = [one(v) for v in offsets]
-        args = (row_scales(weight, core, ids), term)
+        args = (weight[None, :], id_column, term)
         late = len(pieces) - len(pieces)
         early = finish(*args, pieces[:late], offsets[:late], starts[:late]) if late else None
         input_gradient = finish(*args, pieces[late:], offsets[late:], starts[late:], into=early)

time: 57.4 us -> 57.2 us (level)
    pallas_call x12 -> x11, Pallas kernels: 8.85 us -> 8.37 us  [call(): pl.pallas_call(body, out_shape=out_shape, in_specs=in_specs, out_specs=ou...]
    unnamed x22 -> x20, local copies, waits for them, and re-layouts: 4.78 us -> 4.65 us
  transfers between devices with their start and end apart: 21 -> 21, of which waited for: 9 -> 10; matrix products, arithmetic and copies ran while one was open for 4% -> 4% of each run, Pallas kernels for 14% -> 13%
where the time goes in v7:
time: 57.2 us; the launch traced here: 56.9 us
  starting transfers between devices  26.3 us (46%)
  waiting for transfers between devices  14.6 us (26%)
  Pallas kernels  8.37 us (15%)
  local copies, waits for them, and re-layouts  4.68 us (8%)
  other arithmetic  2.15 us (4%)
  between operations  0.88 us (2%)
    ppermute x21, starting transfers between devices, swap(): return lax.ppermute(value, axis, [(i, i ^ step) for i in range(size)])  26.3 us
    ppermute x21, waiting for transfers between devices, swap(): return lax.ppermute(value, axis, [(i, i ^ step) for i in range(size)])  14.6 us
    pallas_call x11, Pallas kernels, call(): pl.pallas_call(body, out_shape=out_shape, in_specs=in_specs, out_specs=ou...  8.37 us
    unnamed x20, local copies, waits for them, and re-layouts  4.65 us
  transfers between devices with their start and end apart: 21, of which 10 were waited for; matrix products, arithmetic and copies ran while one was open for 4% of the time, Pallas kernels for 13%

profile of v7, /device:TPU:0, one launch (start us, length us, event | category | flops | bytes accessed | tf_op | source)
XLA Modules:
  0.0 56.9 jit_solution(940419746867019060)
XLA Ops:
  0.6 0.5 collective-permute-start
  1.1 3.7 %collective-permute-start.2 = (bf16[128,1280]{1,0:T(8,128)(2,1)}, bf16[128,1280]{1,0:T(8,128)(2,1)S(1)}, u32[]{:S(2)}, u32[]{:S(2)}) collective-permute-start(bf16[128,1280]{1,0:T(8,128)(2,1)} %refs_4_.1), channel_id=1, source_target_pairs={{0,8},{4,12},{8,0},{12,4},{1,9},{5,13},{9,1},{13,5},{2,10},{6,14},... | collective-permute-start | bytes 983048 | tf_op jit(solution)/shard_map/ppermute | solution.py:246
  4.8 1.6 %collective-permute-start.4 = (bf16[128,1280]{1,0:T(8,128)(2,1)}, bf16[128,1280]{1,0:T(8,128)(2,1)S(1)}, u32[]{:S(2)}, u32[]{:S(2)}) collective-permute-start(bf16[128,1280]{1,0:T(8,128)(2,1)} %refs_4_.1), channel_id=1, source_target_pairs={{0,4},{4,0},{8,12},{12,8},{1,5},{5,1},{9,13},{13,9},{2,6},{6,2},{1... | collective-permute-start | bytes 983048 | tf_op jit(solution)/shard_map/ppermute | solution.py:246
  6.4 0.0 collective-permute-done.refs_3_
  6.4 1.1 %copy-done.2 = bf16[128,2560]{1,0:T(8,128)(2,1)S(1)} copy-done((bf16[128,2560]{1,0:T(8,128)(2,1)S(1)}, bf16[128,2560]{1,0:T(8,128)(2,1)}, u32[]{:S(2)}) %copy-start.2) | copy-done | bytes 655384
  7.5 1.0 %copy-done.4 = bf16[2560,4,16]{0,2,1:T(8,128)(2,1)S(1)} copy-done((bf16[2560,4,16]{0,2,1:T(8,128)(2,1)S(1)}, bf16[2560,4,16]{0,2,1:T(8,128)(2,1)}, u32[]{:S(2)}) %copy-start.4) | copy-done | bytes 327704
  8.5 1.0 %copy-done.6 = bf16[128,1280]{1,0:T(8,128)(2,1)S(1)} copy-done((bf16[128,1280]{1,0:T(8,128)(2,1)S(1)}, bf16[128,1280]{1,0:T(8,128)(2,1)}, u32[]{:S(2)}) %copy-start.6) | copy-done | bytes 327704
  9.4 0.9 %copy-done.8 = bf16[4,16,1280]{2,1,0:T(8,128)(2,1)S(1)} copy-done((bf16[4,16,1280]{2,1,0:T(8,128)(2,1)S(1)}, bf16[4,16,1280]{2,1,0:T(8,128)(2,1)}, u32[]{:S(2)}) %copy-start.8) | copy-done | bytes 163864
  10.3 0.7 %copy-done.9 = s32[256]{0:T(256)S(1)} copy-done((s32[256]{0:T(256)S(1)}, s32[256]{0:T(256)}, u32[]{:S(2)}) %copy-start.9) | copy-done | bytes 1048
  11.0 0.5 shard_map.94.rest_0_
  11.5 1.6 %collective-permute-start.1 = (f32[32,128]{1,0:T(8,128)S(1)}, f32[32,128]{1,0:T(8,128)S(1)}, u32[]{:S(2)}, u32[]{:S(2)}) collective-permute-start(f32[32,128]{1,0:T(8,128)S(1)} %shard_map.94.rest_0_), channel_id=1, source_target_pairs={{0,2},{2,0},{1,3},{3,1},{4,6},{6,4},{5,7},{7,5},{8,10},{10,8},{9,1... | collective-permute-start | bytes 49160 | tf_op jit(solution)/shard_map/ppermute | solution.py:246
  13.1 1.1 %shard_map.96 = (bf16[128,640]{1,0:T(8,128)(2,1)S(1)}, bf16[128,640]{1,0:T(8,128)(2,1)S(1)}) custom-call(s32[1]{0:T(128)} %bitcast.5.refs_0_, bf16[128,1280]{1,0:T(8,128)(2,1)S(1)} %copy-done.6, bf16[640,1280]{1,0:T(8,128)(2,1)S(1)} %copy-done.1, bf16[640,1280]{1,0:T(8,128)(2,1)S(1)} %collective-permute-done.refs_3_), custom_call_target="tpu_custom_call" | custom-call | flops 8589934592 | bytes 33554432 | tf_op jit(solution)/shard_map/pallas_call | solution.py:34
  14.2 0.0 copy-start.5
  14.2 0.9 %collective-permute-start.12 = (bf16[128,640]{1,0:T(8,128)(2,1)S(1)}, bf16[128,640]{1,0:T(8,128)(2,1)S(1)}, u32[]{:S(2)}, u32[]{:S(2)}) collective-permute-start(bf16[128,640]{1,0:T(8,128)(2,1)S(1)} %get-tuple-element.46), channel_id=1, source_target_pairs={{0,2},{2,0},{1,3},{3,1},{4,6},{6,4},{5,7},{7,5},{8,10},{10,8},{9,1... | collective-permute-start | bytes 491528 | tf_op jit(solution)/shard_map/ppermute | solution.py:246
  15.1 0.2 collective-permute-done.1.rest_1_
  15.3 0.9 %shard_map.95 = (bf16[32,128]{1,0:T(8,128)(2,1)S(1)}, bf16[16,128]{1,0:T(8,128)(2,1)S(1)}, bf16[128,1280]{1,0:T(8,128)(2,1)S(1)}, bf16[128,1280]{1,0:T(8,128)(2,1)S(1)}) custom-call(s32[4]{0:T(128)S(1)} %copy-done, s32[1]{0:T(128)} %bitcast.core_ref, s32[2,128]{1,0:T(2,128)S(1)} %bitcast.32, bf16[128,2560]{1,0:T(8,128)(2,1)S(1)} %copy-done.3, ...), custom_call_target="tpu_custom_call" | custom-call | flops 8589934592 | bytes 33554432 | tf_op jit(solution)/shard_map/pallas_call | solution.py:34
  16.2 4.3 %collective-permute-done.2.refs_1_.refs_6_ = bf16[128,1280]{1,0:T(8,128)(2,1)S(1)} collective-permute-done((bf16[128,1280]{1,0:T(8,128)(2,1)}, bf16[128,1280]{1,0:T(8,128)(2,1)S(1)}, u32[]{:S(2)}, u32[]{:S(2)}) %collective-permute-start.2) | collective-permute-done | bytes 327712 | tf_op jit(solution)/shard_map/ppermute | solution.py:246
  20.5 0.7 %collective-permute-start.3 = (bf16[128,1280]{1,0:T(8,128)(2,1)S(1)}, bf16[128,1280]{1,0:T(8,128)(2,1)S(1)}, u32[]{:S(2)}, u32[]{:S(2)}) collective-permute-start(bf16[128,1280]{1,0:T(8,128)(2,1)S(1)} %collective-permute-done.2.refs_1_.refs_6_), channel_id=1, source_target_pairs={{0,4},{4,0},{8,12},{12,8},{1,5},{5,1},{9,13},{13,9},{2,6},{6,2},{1... | collective-permute-start | bytes 983048 | tf_op jit(solution)/shard_map/ppermute | solution.py:246
  21.2 0.0 collective-permute-start.5
  21.2 0.4 shard_map.102
  21.6 0.0 collective-permute-done.12
  21.6 1.2 %collective-permute-done.5.got_ref = bf16[128,1280]{1,0:T(8,128)(2,1)S(1)} collective-permute-done((bf16[128,1280]{1,0:T(8,128)(2,1)S(1)}, bf16[128,1280]{1,0:T(8,128)(2,1)S(1)}, u32[]{:S(2)}, u32[]{:S(2)}) %collective-permute-start.5) | collective-permute-done | bytes 327712 | tf_op jit(solution)/shard_map/ppermute | solution.py:246
  22.8 0.1 shard_map.97
  22.9 3.3 %collective-permute-start.9 = (bf16[32,2688]{1,0:T(8,128)(2,1)S(1)}, bf16[32,2688]{1,0:T(8,128)(2,1)S(1)}, u32[]{:S(2)}, u32[]{:S(2)}) collective-permute-start(bf16[32,2688]{1,0:T(8,128)(2,1)S(1)} %get-tuple-element.51), channel_id=1, source_target_pairs={{0,8},{4,12},{8,0},{12,4},{1,9},{5,13},{9,1},{13,5},{2,10},{6,14},... | collective-permute-start | bytes 516104 | tf_op jit(solution)/shard_map/ppermute | solution.py:246
  26.3 1.1 %shard_map.98 = (bf16[128,640]{1,0:T(8,128)(2,1)S(1)}, bf16[128,640]{1,0:T(8,128)(2,1)S(1)}) custom-call(s32[1]{0:T(128)} %bitcast.5.refs_0_, bf16[128,1280]{1,0:T(8,128)(2,1)S(1)} %collective-permute-done.2.refs_1_.refs_6_, bf16[640,1280]{1,0:T(8,128)(2,1)S(1)} %copy-done.1, bf16[640,1280]{1,0:T(8,128)(2,1)S(1)} %collective-permute-done.refs_3_), custom_call_target="tpu_custom_call" | custom-call | flops 8589934592 | bytes 33554432 | tf_op jit(solution)/shard_map/pallas_call | solution.py:34
  27.3 1.6 %collective-permute-start.6 = (bf16[128,640]{1,0:T(8,128)(2,1)S(1)}, bf16[128,640]{1,0:T(8,128)(2,1)S(1)}, u32[]{:S(2)}, u32[]{:S(2)}) collective-permute-start(bf16[128,640]{1,0:T(8,128)(2,1)S(1)} %get-tuple-element.54), channel_id=1, source_target_pairs={{0,2},{2,0},{1,3},{3,1},{4,6},{6,4},{5,7},{7,5},{8,10},{10,8},{9,1... | collective-permute-start | bytes 491528 | tf_op jit(solution)/shard_map/ppermute | solution.py:246
  28.9 0.0 collective-permute-done.4.refs_1_.refs_5_
  28.9 1.1 %shard_map.99 = (bf16[128,640]{1,0:T(8,128)(2,1)S(1)}, bf16[128,640]{1,0:T(8,128)(2,1)S(1)}) custom-call(s32[1]{0:T(128)} %bitcast.5.refs_0_, bf16[128,1280]{1,0:T(8,128)(2,1)S(1)} %collective-permute-done.4.refs_1_.refs_5_, bf16[640,1280]{1,0:T(8,128)(2,1)S(1)} %copy-done.1, bf16[640,1280]{1,0:T(8,128)(2,1)S(1)} %collective-permute-done.refs_3_), custom_call_target="tpu_custom_call" | custom-call | flops 8589934592 | bytes 33554432 | tf_op jit(solution)/shard_map/pallas_call | solution.py:34
  30.0 0.6 %collective-permute-start.15 = (bf16[128,640]{1,0:T(8,128)(2,1)S(1)}, bf16[128,640]{1,0:T(8,128)(2,1)S(1)}, u32[]{:S(2)}, u32[]{:S(2)}) collective-permute-start(bf16[128,640]{1,0:T(8,128)(2,1)S(1)} %get-tuple-element.57), channel_id=1, source_target_pairs={{0,2},{2,0},{1,3},{3,1},{4,6},{6,4},{5,7},{7,5},{8,10},{10,8},{9,1... | collective-permute-start | bytes 491528 | tf_op jit(solution)/shard_map/ppermute | solution.py:246
  30.6 3.9 %collective-permute-done.6 = bf16[128,640]{1,0:T(8,128)(2,1)S(1)} collective-permute-done((bf16[128,640]{1,0:T(8,128)(2,1)S(1)}, bf16[128,640]{1,0:T(8,128)(2,1)S(1)}, u32[]{:S(2)}, u32[]{:S(2)}) %collective-permute-start.6) | collective-permute-done | bytes 163872 | tf_op jit(solution)/shard_map/ppermute | solution.py:246
  34.5 0.1 collective-permute-start.11
  34.6 0.0 collective-permute-done.3.refs_1_.refs_7_
  34.6 0.7 %shard_map.100 = (bf16[64,640]{1,0:T(8,128)(2,1)S(1)}, bf16[64,640]{1,0:T(8,128)(2,1)S(1)}) custom-call(s32[1]{0:T(128)} %bitcast.5.refs_0_, bf16[128,1280]{1,0:T(8,128)(2,1)S(1)} %collective-permute-done.3.refs_1_.refs_7_, bf16[640,1280]{1,0:T(8,128)(2,1)S(1)} %copy-done.1, bf16[640,1280]{1,0:T(8,128)(2,1)S(1)} %collective-permute-done.refs_3_), custom_call_target="tpu_custom_call" | custom-call | flops 8589934592 | bytes 33554432 | tf_op jit(solution)/shard_map/pallas_call | solution.py:34
  35.3 1.6 %collective-permute-start.7 = (bf16[64,640]{1,0:T(8,128)(2,1)S(1)}, bf16[64,640]{1,0:T(8,128)(2,1)S(1)}, u32[]{:S(2)}, u32[]{:S(2)}) collective-permute-start(bf16[64,640]{1,0:T(8,128)(2,1)S(1)} %get-tuple-element.59), channel_id=1, source_target_pairs={{0,2},{2,0},{1,3},{3,1},{4,6},{6,4},{5,7},{7,5},{8,10},{10,8},{9,1... | collective-permute-start | bytes 245768 | tf_op jit(solution)/shard_map/ppermute | solution.py:246
  36.8 0.5 collective-permute-start.8
  37.3 0.6 %shard_map.101 = (bf16[64,640]{1,0:T(8,128)(2,1)S(1)}, bf16[64,640]{1,0:T(8,128)(2,1)S(1)}) custom-call(s32[1]{0:T(128)} %bitcast.5.refs_0_, bf16[128,1280]{1,0:T(8,128)(2,1)S(1)} %collective-permute-done.3.refs_1_.refs_7_, bf16[640,1280]{1,0:T(8,128)(2,1)S(1)} %copy-done.1, bf16[640,1280]{1,0:T(8,128)(2,1)S(1)} %collective-permute-done.refs_3_), custom_call_target="tpu_custom_call" | custom-call | flops 8589934592 | bytes 33554432 | tf_op jit(solution)/shard_map/pallas_call | solution.py:34
  38.0 0.0 collective-permute-done.15
  38.1 0.0 copy-start.7
  38.1 0.9 %collective-permute-start.16 = (bf16[128,640]{1,0:T(8,128)(2,1)S(1)}, bf16[128,640]{1,0:T(8,128)(2,1)S(1)}, u32[]{:S(2)}, u32[]{:S(2)}) collective-permute-start(bf16[128,640]{1,0:T(8,128)(2,1)S(1)} %add_convert_fusion), channel_id=1, source_target_pairs={{0,4},{4,0},{8,12},{12,8},{1,5},{5,1},{9,13},{13,9},{2,6},{6,2},{1... | collective-permute-start | bytes 491528 | tf_op jit(solution)/shard_map/ppermute | solution.py:246
  39.0 0.0 collective-permute-done.9
  39.0 0.7 %collective-permute-done.7 = bf16[64,640]{1,0:T(8,128)(2,1)S(1)} collective-permute-done((bf16[64,640]{1,0:T(8,128)(2,1)S(1)}, bf16[64,640]{1,0:T(8,128)(2,1)S(1)}, u32[]{:S(2)}, u32[]{:S(2)}) %collective-permute-start.7) | collective-permute-done | bytes 81952 | tf_op jit(solution)/shard_map/ppermute | solution.py:246
  39.8 3.5 %collective-permute-start.14 = (bf16[64,640]{1,0:T(8,128)(2,1)S(1)}, bf16[64,640]{1,0:T(8,128)(2,1)S(1)}, u32[]{:S(2)}, u32[]{:S(2)}) collective-permute-start(bf16[64,640]{1,0:T(8,128)(2,1)S(1)} %add_convert_fusion.6), channel_id=1, source_target_pairs={{0,12},{4,8},{8,4},{12,0},{1,13},{5,9},{9,5},{13,1},{2,14},{6,10},... | collective-permute-start | bytes 245768 | tf_op jit(solution)/shard_map/ppermute | solution.py:246
  43.3 0.0 collective-permute-done.8
  43.3 1.4 %collective-permute-start.18 = (bf16[64,640]{1,0:T(8,128)(2,1)S(1)}, bf16[64,640]{1,0:T(8,128)(2,1)S(1)}, u32[]{:S(2)}, u32[]{:S(2)}) collective-permute-start(bf16[64,640]{1,0:T(8,128)(2,1)S(1)} %add_convert_fusion.5), channel_id=1, source_target_pairs={{0,12},{4,8},{8,4},{12,0},{1,13},{5,9},{9,5},{13,1},{2,14},{6,10},... | collective-permute-start | bytes 245768 | tf_op jit(solution)/shard_map/ppermute | solution.py:246
  44.8 0.0 collective-permute-start.10
  44.8 0.0 collective-permute-done.11
  44.9 1.5 %collective-permute-start.13 = (bf16[128,640]{1,0:T(8,128)(2,1)S(1)}, bf16[128,640]{1,0:T(8,128)(2,1)S(1)}, u32[]{:S(2)}, u32[]{:S(2)}) collective-permute-start(bf16[128,640]{1,0:T(8,128)(2,1)S(1)} %get-tuple-element.81), channel_id=1, source_target_pairs={{0,2},{2,0},{1,3},{3,1},{4,6},{6,4},{5,7},{7,5},{8,10},{10,8},{9,1... | collective-permute-start | bytes 491528 | tf_op jit(solution)/shard_map/ppermute | solution.py:246
  46.4 1.2 %collective-permute-done.16 = bf16[128,640]{1,0:T(8,128)(2,1)S(1)} collective-permute-done((bf16[128,640]{1,0:T(8,128)(2,1)S(1)}, bf16[128,640]{1,0:T(8,128)(2,1)S(1)}, u32[]{:S(2)}, u32[]{:S(2)}) %collective-permute-start.16) | collective-permute-done | bytes 163872 | tf_op jit(solution)/shard_map/ppermute | solution.py:246
  47.7 0.9 %collective-permute-done.14 = bf16[64,640]{1,0:T(8,128)(2,1)S(1)} collective-permute-done((bf16[64,640]{1,0:T(8,128)(2,1)S(1)}, bf16[64,640]{1,0:T(8,128)(2,1)S(1)}, u32[]{:S(2)}, u32[]{:S(2)}) %collective-permute-start.14) | collective-permute-done | bytes 81952 | tf_op jit(solution)/shard_map/ppermute | solution.py:246
  48.6 1.1 %collective-permute-done.18 = bf16[64,640]{1,0:T(8,128)(2,1)S(1)} collective-permute-done((bf16[64,640]{1,0:T(8,128)(2,1)S(1)}, bf16[64,640]{1,0:T(8,128)(2,1)S(1)}, u32[]{:S(2)}, u32[]{:S(2)}) %collective-permute-start.18) | collective-permute-done | bytes 81952 | tf_op jit(solution)/shard_map/ppermute | solution.py:246
  49.7 1.5 %collective-permute-start.19 = (bf16[64,640]{1,0:T(8,128)(2,1)S(1)}, bf16[64,640]{1,0:T(8,128)(2,1)S(1)}, u32[]{:S(2)}, u32[]{:S(2)}) collective-permute-start(bf16[64,640]{1,0:T(8,128)(2,1)S(1)} %get-tuple-element.83), channel_id=1, source_target_pairs={{0,2},{2,0},{1,3},{3,1},{4,6},{6,4},{5,7},{7,5},{8,10},{10,8},{9,1... | collective-permute-start | bytes 245768 | tf_op jit(solution)/shard_map/ppermute | solution.py:246
  51.3 0.6 %collective-permute-start.17 = (bf16[64,640]{1,0:T(8,128)(2,1)S(1)}, bf16[64,640]{1,0:T(8,128)(2,1)S(1)}, u32[]{:S(2)}, u32[]{:S(2)}) collective-permute-start(bf16[64,640]{1,0:T(8,128)(2,1)S(1)} %get-tuple-element.87), channel_id=1, source_target_pairs={{0,2},{2,0},{1,3},{3,1},{4,6},{6,4},{5,7},{7,5},{8,10},{10,8},{9,1... | collective-permute-start | bytes 245768 | tf_op jit(solution)/shard_map/ppermute | solution.py:246
  51.9 0.0 collective-permute-done.10
  52.0 0.1 convert_reduce_fusion
  52.2 0.2 fusion
  52.4 0.9 %shard_map.104 = (f32[32,640]{1,0:T(8,128)S(1)}, f32[32,640]{1,0:T(8,128)S(1)}) custom-call(s32[4]{0:T(128)S(1)} %copy-done, s32[1]{0:T(128)} %bitcast.core_ref, s32[1]{0:T(128)} %bitcast.6.place_ref, bf16[32,128]{1,0:T(8,128)(2,1)S(1)} %get-tuple-element.65.card_ref.refs_0_, bf16[32,128]{1,0:T(8,128)(2,1)S(1)} %get-tuple-element.68.refs_1_, ...), custom_call_target="tpu_custom_call" | custom-call | flops 8589934592 | bytes 33554432 | tf_op jit(solution)/shard_map/pallas_call | solution.py:34
  53.2 0.1 collective-permute-start.20
  53.3 0.7 %multiply_bitcast_fusion = f32[1280,2,16]{0,2,1:T(8,128)} fusion(f32[2,16,1280]{2,1,0:T(8,128)S(1)} %bitcast.34, f32[2]{0:T(128)S(1)} %broadcast_multiply_fusion.1), kind=kLoop, calls=%fused_computation.3 | loop fusion | flops 40960 | bytes 327688 | tf_op jit(solution)/shard_map/transpose | solution.py:361
  54.1 0.5 collective-permute-done.20
  54.6 0.7 %broadcast_multiply_fusion = f32[2,16,640]{2,1,0:T(8,128)} fusion(f32[2,16,640]{2,1,0:T(8,128)S(1)} %bitcast.35, f32[2]{0:T(128)S(1)} %broadcast_multiply_fusion.1), kind=kLoop, calls=%fused_computation.16 | loop fusion | flops 20480 | bytes 163848 | tf_op jit(solution)/shard_map/mul | solution.py:399
  55.3 0.0 collective-permute-done.19.refs_14_
  55.3 0.5 collective-permute-done.17.refs_12_
  55.8 0.0 collective-permute-done.13.refs_10_
  55.8 1.1 %shard_map.103 = bf16[128,2560]{1,0:T(8,128)(2,1)} custom-call(f32[1,4]{1,0:T(1,128)S(1)} %fusion.3.refs_0_, f32[128,128]{1,0:T(8,128)S(1)} %get-tuple-element.72.refs_1_, s32[1]{0:T(128)} %bitcast.14.refs_2_, s32[1]{0:T(128)} %bitcast.15.refs_3_, s32[1]{0:T(128)} %bitcast.16.refs_4_.refs_6_, s32[1]{0:T(128)} %bitcast.17.refs_5_.refs_7_, ...), custom_call_target="tpu_custom_call" | custom-call | flops 8589934592 | bytes 33554432 | tf_op jit(solution)/shard_map/pallas_call | solution.py:34
  (36 shorter events, 0.4 us)
Async XLA Ops:
  0.6 5.8 %collective-permute-start = (bf16[640,1280]{1,0:T(8,128)(2,1)}, bf16[640,1280]{1,0:T(8,128)(2,1)S(1)}, u32[]{:S(2)}, u32[]{:S(2)}) collective-permute-start(bf16[640,1280]{1,0:T(8,128)(2,1)} %refs_2_.9), channel_id=1, source_target_pairs={{0,1},{1,0},{2,3},{3,2},{4,5},{5,4},{6,7},{7,6},{8,9},{9,8},{10,11... | collective-permute-start | bytes 4915208 | tf_op jit(solution)/shard_map/ppermute | solution.py:246
  1.1 19.3 %collective-permute-start.2 = (bf16[128,1280]{1,0:T(8,128)(2,1)}, bf16[128,1280]{1,0:T(8,128)(2,1)S(1)}, u32[]{:S(2)}, u32[]{:S(2)}) collective-permute-start(bf16[128,1280]{1,0:T(8,128)(2,1)} %refs_4_.1), channel_id=1, source_target_pairs={{0,8},{4,12},{8,0},{12,4},{1,9},{5,13},{9,1},{13,5},{2,10},{6,14},... | collective-permute-start | bytes 983048 | tf_op jit(solution)/shard_map/ppermute | solution.py:246
  4.8 24.1 %collective-permute-start.4 = (bf16[128,1280]{1,0:T(8,128)(2,1)}, bf16[128,1280]{1,0:T(8,128)(2,1)S(1)}, u32[]{:S(2)}, u32[]{:S(2)}) collective-permute-start(bf16[128,1280]{1,0:T(8,128)(2,1)} %refs_4_.1), channel_id=1, source_target_pairs={{0,4},{4,0},{8,12},{12,8},{1,5},{5,1},{9,13},{13,9},{2,6},{6,2},{1... | collective-permute-start | bytes 983048 | tf_op jit(solution)/shard_map/ppermute | solution.py:246
  6.4 1.1 %copy-start.2 = (bf16[128,2560]{1,0:T(8,128)(2,1)S(1)}, bf16[128,2560]{1,0:T(8,128)(2,1)}, u32[]{:S(2)}) copy-start(bf16[128,2560]{1,0:T(8,128)(2,1)} %x_ref.3) | copy-start | bytes 1966084
  7.5 1.0 %copy-start.4 = (bf16[2560,4,16]{0,2,1:T(8,128)(2,1)S(1)}, bf16[2560,4,16]{0,2,1:T(8,128)(2,1)}, u32[]{:S(2)}) copy-start(bf16[2560,4,16]{0,2,1:T(8,128)(2,1)} %param.12) | copy-start | bytes 983044
  8.5 1.0 %copy-start.6 = (bf16[128,1280]{1,0:T(8,128)(2,1)S(1)}, bf16[128,1280]{1,0:T(8,128)(2,1)}, u32[]{:S(2)}) copy-start(bf16[128,1280]{1,0:T(8,128)(2,1)} %refs_4_.1) | copy-start | bytes 983044
  9.4 0.9 %copy-start.8 = (bf16[4,16,1280]{2,1,0:T(8,128)(2,1)S(1)}, bf16[4,16,1280]{2,1,0:T(8,128)(2,1)}, u32[]{:S(2)}) copy-start(bf16[4,16,1280]{2,1,0:T(8,128)(2,1)} %param.13) | copy-start | bytes 491524
  10.3 0.7 %copy-start.9 = (s32[256]{0:T(256)S(1)}, s32[256]{0:T(256)}, u32[]{:S(2)}) copy-start(s32[256]{0:T(256)} %param.9) | copy-start | bytes 3076
  11.0 2.0 %copy-start.1 = (bf16[640,1280]{1,0:T(8,128)(2,1)S(1)}, bf16[640,1280]{1,0:T(8,128)(2,1)}, u32[]{:S(2)}) copy-start(bf16[640,1280]{1,0:T(8,128)(2,1)} %refs_2_.9) | copy-start | bytes 4915204
  11.5 3.8 %collective-permute-start.1 = (f32[32,128]{1,0:T(8,128)S(1)}, f32[32,128]{1,0:T(8,128)S(1)}, u32[]{:S(2)}, u32[]{:S(2)}) collective-permute-start(f32[32,128]{1,0:T(8,128)S(1)} %shard_map.94.rest_0_), channel_id=1, source_target_pairs={{0,2},{2,0},{1,3},{3,1},{4,6},{6,4},{5,7},{7,5},{8,10},{10,8},{9,1... | collective-permute-start | bytes 49160 | tf_op jit(solution)/shard_map/ppermute | solution.py:246
  13.1 2.2 %copy-start = (s32[4]{0:T(128)S(1)}, s32[4]{0:T(128)}, u32[]{:S(2)}) copy-start(s32[4]{0:T(128)} %slot_ref.3) | copy-start | bytes 52
  13.1 2.2 %copy-start.3 = (bf16[128,2560]{1,0:T(8,128)(2,1)S(1)}, bf16[128,2560]{1,0:T(8,128)(2,1)}, u32[]{:S(2)}) copy-start(bf16[128,2560]{1,0:T(8,128)(2,1)} %x_ref.3) | copy-start | bytes 1966084
  14.2 7.0 %copy-start.5 = (bf16[2560,4,16]{0,2,1:T(8,128)(2,1)S(1)}, bf16[2560,4,16]{0,2,1:T(8,128)(2,1)}, u32[]{:S(2)}) copy-start(bf16[2560,4,16]{0,2,1:T(8,128)(2,1)} %param.12) | copy-start | bytes 983044
  14.2 7.4 %collective-permute-start.12 = (bf16[128,640]{1,0:T(8,128)(2,1)S(1)}, bf16[128,640]{1,0:T(8,128)(2,1)S(1)}, u32[]{:S(2)}, u32[]{:S(2)}) collective-permute-start(bf16[128,640]{1,0:T(8,128)(2,1)S(1)} %get-tuple-element.46), channel_id=1, source_target_pairs={{0,2},{2,0},{1,3},{3,1},{4,6},{6,4},{5,7},{7,5},{8,10},{10,8},{9,1... | collective-permute-start | bytes 491528 | tf_op jit(solution)/shard_map/ppermute | solution.py:246
  20.5 14.1 %collective-permute-start.3 = (bf16[128,1280]{1,0:T(8,128)(2,1)S(1)}, bf16[128,1280]{1,0:T(8,128)(2,1)S(1)}, u32[]{:S(2)}, u32[]{:S(2)}) collective-permute-start(bf16[128,1280]{1,0:T(8,128)(2,1)S(1)} %collective-permute-done.2.refs_1_.refs_6_), channel_id=1, source_target_pairs={{0,4},{4,0},{8,12},{12,8},{1,5},{5,1},{9,13},{13,9},{2,6},{6,2},{1... | collective-permute-start | bytes 983048 | tf_op jit(solution)/shard_map/ppermute | solution.py:246
  21.2 1.6 %collective-permute-start.5 = (bf16[128,1280]{1,0:T(8,128)(2,1)S(1)}, bf16[128,1280]{1,0:T(8,128)(2,1)S(1)}, u32[]{:S(2)}, u32[]{:S(2)}) collective-permute-start(bf16[128,1280]{1,0:T(8,128)(2,1)S(1)} %get-tuple-element.50), channel_id=1, source_target_pairs={{0,1},{1,0},{2,3},{3,2},{4,5},{5,4},{6,7},{7,6},{8,9},{9,8},{10,11... | collective-permute-start | bytes 983048 | tf_op jit(solution)/shard_map/ppermute | solution.py:246
  22.9 16.1 %collective-permute-start.9 = (bf16[32,2688]{1,0:T(8,128)(2,1)S(1)}, bf16[32,2688]{1,0:T(8,128)(2,1)S(1)}, u32[]{:S(2)}, u32[]{:S(2)}) collective-permute-start(bf16[32,2688]{1,0:T(8,128)(2,1)S(1)} %get-tuple-element.51), channel_id=1, source_target_pairs={{0,8},{4,12},{8,0},{12,4},{1,9},{5,13},{9,1},{13,5},{2,10},{6,14},... | collective-permute-start | bytes 516104 | tf_op jit(solution)/shard_map/ppermute | solution.py:246
  27.3 7.1 %collective-permute-start.6 = (bf16[128,640]{1,0:T(8,128)(2,1)S(1)}, bf16[128,640]{1,0:T(8,128)(2,1)S(1)}, u32[]{:S(2)}, u32[]{:S(2)}) collective-permute-start(bf16[128,640]{1,0:T(8,128)(2,1)S(1)} %get-tuple-element.54), channel_id=1, source_target_pairs={{0,2},{2,0},{1,3},{3,1},{4,6},{6,4},{5,7},{7,5},{8,10},{10,8},{9,1... | collective-permute-start | bytes 491528 | tf_op jit(solution)/shard_map/ppermute | solution.py:246
  30.0 8.0 %collective-permute-start.15 = (bf16[128,640]{1,0:T(8,128)(2,1)S(1)}, bf16[128,640]{1,0:T(8,128)(2,1)S(1)}, u32[]{:S(2)}, u32[]{:S(2)}) collective-permute-start(bf16[128,640]{1,0:T(8,128)(2,1)S(1)} %get-tuple-element.57), channel_id=1, source_target_pairs={{0,2},{2,0},{1,3},{3,1},{4,6},{6,4},{5,7},{7,5},{8,10},{10,8},{9,1... | collective-permute-start | bytes 491528 | tf_op jit(solution)/shard_map/ppermute | solution.py:246
  34.5 10.3 %collective-permute-start.11 = (bf16[128,640]{1,0:T(8,128)(2,1)S(1)}, bf16[128,640]{1,0:T(8,128)(2,1)S(1)}, u32[]{:S(2)}, u32[]{:S(2)}) collective-permute-start(bf16[128,640]{1,0:T(8,128)(2,1)S(1)} %add_convert_fusion.2), channel_id=1, source_target_pairs={{0,8},{4,12},{8,0},{12,4},{1,9},{5,13},{9,1},{13,5},{2,10},{6,14},... | collective-permute-start | bytes 491528 | tf_op jit(solution)/shard_map/ppermute | solution.py:246
  35.3 4.5 %collective-permute-start.7 = (bf16[64,640]{1,0:T(8,128)(2,1)S(1)}, bf16[64,640]{1,0:T(8,128)(2,1)S(1)}, u32[]{:S(2)}, u32[]{:S(2)}) collective-permute-start(bf16[64,640]{1,0:T(8,128)(2,1)S(1)} %get-tuple-element.59), channel_id=1, source_target_pairs={{0,2},{2,0},{1,3},{3,1},{4,6},{6,4},{5,7},{7,5},{8,10},{10,8},{9,1... | collective-permute-start | bytes 245768 | tf_op jit(solution)/shard_map/ppermute | solution.py:246
  36.8 6.5 %collective-permute-start.8 = (bf16[64,640]{1,0:T(8,128)(2,1)S(1)}, bf16[64,640]{1,0:T(8,128)(2,1)S(1)}, u32[]{:S(2)}, u32[]{:S(2)}) collective-permute-start(bf16[64,640]{1,0:T(8,128)(2,1)S(1)} %get-tuple-element.60), channel_id=1, source_target_pairs={{0,2},{2,0},{1,3},{3,1},{4,6},{6,4},{5,7},{7,5},{8,10},{10,8},{9,1... | collective-permute-start | bytes 245768 | tf_op jit(solution)/shard_map/ppermute | solution.py:246
  38.1 14.3 %copy-start.7 = (bf16[128,1280]{1,0:T(8,128)(2,1)S(1)}, bf16[128,1280]{1,0:T(8,128)(2,1)}, u32[]{:S(2)}) copy-start(bf16[128,1280]{1,0:T(8,128)(2,1)} %refs_4_.1) | copy-start | bytes 983044
  38.1 9.6 %collective-permute-start.16 = (bf16[128,640]{1,0:T(8,128)(2,1)S(1)}, bf16[128,640]{1,0:T(8,128)(2,1)S(1)}, u32[]{:S(2)}, u32[]{:S(2)}) collective-permute-start(bf16[128,640]{1,0:T(8,128)(2,1)S(1)} %add_convert_fusion), channel_id=1, source_target_pairs={{0,4},{4,0},{8,12},{12,8},{1,5},{5,1},{9,13},{13,9},{2,6},{6,2},{1... | collective-permute-start | bytes 491528 | tf_op jit(solution)/shard_map/ppermute | solution.py:246
  39.8 8.8 %collective-permute-start.14 = (bf16[64,640]{1,0:T(8,128)(2,1)S(1)}, bf16[64,640]{1,0:T(8,128)(2,1)S(1)}, u32[]{:S(2)}, u32[]{:S(2)}) collective-permute-start(bf16[64,640]{1,0:T(8,128)(2,1)S(1)} %add_convert_fusion.6), channel_id=1, source_target_pairs={{0,12},{4,8},{8,4},{12,0},{1,13},{5,9},{9,5},{13,1},{2,14},{6,10},... | collective-permute-start | bytes 245768 | tf_op jit(solution)/shard_map/ppermute | solution.py:246
  43.3 6.4 %collective-permute-start.18 = (bf16[64,640]{1,0:T(8,128)(2,1)S(1)}, bf16[64,640]{1,0:T(8,128)(2,1)S(1)}, u32[]{:S(2)}, u32[]{:S(2)}) collective-permute-start(bf16[64,640]{1,0:T(8,128)(2,1)S(1)} %add_convert_fusion.5), channel_id=1, source_target_pairs={{0,12},{4,8},{8,4},{12,0},{1,13},{5,9},{9,5},{13,1},{2,14},{6,10},... | collective-permute-start | bytes 245768 | tf_op jit(solution)/shard_map/ppermute | solution.py:246
  44.8 7.1 %collective-permute-start.10 = (bf16[32,1536]{1,0:T(8,128)(2,1)S(1)}, bf16[32,1536]{1,0:T(8,128)(2,1)S(1)}, u32[]{:S(2)}, u32[]{:S(2)}) collective-permute-start(bf16[32,1536]{1,0:T(8,128)(2,1)S(1)} %pad_maximum_fusion), channel_id=1, source_target_pairs={{0,4},{4,0},{8,12},{12,8},{1,5},{5,1},{9,13},{13,9},{2,6},{6,2},{1... | collective-permute-start | bytes 294920 | tf_op jit(solution)/shard_map/ppermute | solution.py:246
  44.9 10.9 %collective-permute-start.13 = (bf16[128,640]{1,0:T(8,128)(2,1)S(1)}, bf16[128,640]{1,0:T(8,128)(2,1)S(1)}, u32[]{:S(2)}, u32[]{:S(2)}) collective-permute-start(bf16[128,640]{1,0:T(8,128)(2,1)S(1)} %get-tuple-element.81), channel_id=1, source_target_pairs={{0,2},{2,0},{1,3},{3,1},{4,6},{6,4},{5,7},{7,5},{8,10},{10,8},{9,1... | collective-permute-start | bytes 491528 | tf_op jit(solution)/shard_map/ppermute | solution.py:246
  49.7 5.6 %collective-permute-start.19 = (bf16[64,640]{1,0:T(8,128)(2,1)S(1)}, bf16[64,640]{1,0:T(8,128)(2,1)S(1)}, u32[]{:S(2)}, u32[]{:S(2)}) collective-permute-start(bf16[64,640]{1,0:T(8,128)(2,1)S(1)} %get-tuple-element.83), channel_id=1, source_target_pairs={{0,2},{2,0},{1,3},{3,1},{4,6},{6,4},{5,7},{7,5},{8,10},{10,8},{9,1... | collective-permute-start | bytes 245768 | tf_op jit(solution)/shard_map/ppermute | solution.py:246
  51.3 4.5 %collective-permute-start.17 = (bf16[64,640]{1,0:T(8,128)(2,1)S(1)}, bf16[64,640]{1,0:T(8,128)(2,1)S(1)}, u32[]{:S(2)}, u32[]{:S(2)}) collective-permute-start(bf16[64,640]{1,0:T(8,128)(2,1)S(1)} %get-tuple-element.87), channel_id=1, source_target_pairs={{0,2},{2,0},{1,3},{3,1},{4,6},{6,4},{5,7},{7,5},{8,10},{10,8},{9,1... | collective-permute-start | bytes 245768 | tf_op jit(solution)/shard_map/ppermute | solution.py:246
  53.2 1.3 %collective-permute-start.20 = (f32[32,640]{1,0:T(8,128)S(1)}, f32[32,640]{1,0:T(8,128)S(1)}, u32[]{:S(2)}, u32[]{:S(2)}) collective-permute-start(f32[32,640]{1,0:T(8,128)S(1)} %get-tuple-element.80), channel_id=1, source_target_pairs={{0,1},{1,0},{2,3},{3,2},{4,5},{5,4},{6,7},{7,6},{8,9},{9,8},{10,11... | collective-permute-start | bytes 245768 | tf_op jit(solution)/shard_map/ppermute | solution.py:246
